TPU v7x, 32 devices: a whole 2x2x4 slice. The times are simulated.
32 devices in a mesh: row: 4 (over y, x), col: 8 (over z, core).
Axes of the slice: x: 2, y: 2, z: 4, core: 2. Of those that a mesh axis runs over, the one named last changes fastest.
Arguments:
- tokens: bfloat16 [128, 12288], P('row', 'col'), may hold values from -6 to 6
- grad_out: bfloat16 [128, 12288], P('row', 'col'), may hold values from -1.796875 to 1.796875
- pre_act: bfloat16 [128, 24576], P('col', 'row'), may hold values from -6 to 6
- w_in: bfloat16 [24576, 12288], P('row', 'col'), may hold values from -0.0546875 to 0.0546875
- w_out: bfloat16 [24576, 12288], P('row', 'col'), may hold values from -0.0390625 to 0.0390625
Outputs:
- grad_tokens: bfloat16 [128, 12288], P('row', 'col')
- grad_w_in: bfloat16 [24576, 12288], P('row', 'col')
- grad_w_out: bfloat16 [24576, 12288], P('row', 'col')
All inputs are finite; a program needn't handle non-finite values.
Results may differ from a plain program's by a relative error of at most 0.005.
Values may be sent and summed in bfloat16 or wider, within the bound.
No kernel may reach another device: no remote copies, remote signals or barrier semaphores. Data moves between devices by JAX's collectives and lax.ppermute only.
A program may use at most 128 MiB of HBM per device.

v0:
```python
import jax
import jax.numpy as jnp
from jax import lax
from jax.sharding import PartitionSpec as P

tanh_scale = 0.7978845608028654
cubic_term = 0.044715


def gelu_parts(pre_act):
    pre_value = pre_act.astype(jnp.float32)
    tanh_arg = tanh_scale * (pre_value + cubic_term * pre_value * pre_value * pre_value)
    tangent = jnp.tanh(tanh_arg)
    hidden_value = 0.5 * pre_value * (1.0 + tangent)
    gelu_slope = 0.5 * (1.0 + tangent) + 0.5 * pre_value * (
        1.0 - tangent * tangent
    ) * tanh_scale * (1.0 + 3.0 * cubic_term * pre_value * pre_value)
    return (hidden_value, gelu_slope)


def per_device(tokens, grad_out, pre_act, w_in, w_out):
    contract_rows = (((0,), (0,)), ((), ()))
    contract_cols = (((1,), (1,)), ((), ()))
    out_cols = lax.all_gather(grad_out, "row", axis=0, tiled=True)
    row_block = out_cols
    grad_hidden = lax.psum_scatter(
        lax.dot_general(row_block, w_out, contract_cols, preferred_element_type=jnp.float32),
        "col",
        scatter_dimension=0,
        tiled=True,
    )
    hidden_value, gelu_slope = gelu_parts(pre_act)
    hidden_local = hidden_value.astype(jnp.bfloat16)
    grad_pre_local = (grad_hidden * gelu_slope).astype(jnp.bfloat16)
    hidden_all, grad_pre_all = (
        lax.all_gather(hidden_local, "col", axis=0, tiled=True),
        lax.all_gather(grad_pre_local, "col", axis=0, tiled=True),
    )
    grad_w_out = lax.dot_general(
        hidden_all, out_cols, contract_rows, preferred_element_type=jnp.float32
    ).astype(jnp.bfloat16)
    tok_cols = lax.all_gather(tokens, "row", axis=0, tiled=True)
    grad_w_in = lax.dot_general(
        grad_pre_all, tok_cols, contract_rows, preferred_element_type=jnp.float32
    ).astype(jnp.bfloat16)
    row_block = grad_pre_all
    grad_tokens = lax.psum_scatter(
        jnp.dot(row_block, w_in, preferred_element_type=jnp.float32),
        "row",
        scatter_dimension=0,
        tiled=True,
    ).astype(jnp.bfloat16)
    return (grad_tokens, grad_w_in, grad_w_out)


def solution(mesh):
    in_specs = (P("row", "col"), P("row", "col"), P("col", "row"), P("row", "col"), P("row", "col"))
    out_specs = (P("row", "col"), P("row", "col"), P("row", "col"))
    return jax.shard_map(
        per_device, mesh=mesh, in_specs=in_specs, out_specs=out_specs, check_vma=False
    )
```

profile of v0, /device:TPU:0, one launch (start us, length us, event | category | flops | bytes accessed | tf_op | source)
XLA Modules:
  0.0 163.2 jit_solution(7481109505277494441)
XLA Ops:
  7.2 0.0 reduce-scatter.3.cloned.1.call-start
  7.2 11.3 %all_gather.12 = bf16[128,1536]{1,0:T(8,128)(2,1)S(1)} all-gather(bf16[32,1536]{1,0:T(8,128)(2,1)} %param.6), channel_id=1, replica_groups=mesh['row'=4,'col'=8] {'row'}, dimensions={0}, use_global_device_ids=true | all-gather | bytes 491520 | tf_op jit(solution)/shard_map/all_gather | solution.py:24
  18.5 0.0 copy-start.1
  18.5 0.0 copy-start.2
  18.5 14.2 %fusion.11 = f32[128,6144]{1,0:T(8,128)} fusion(bf16[128,1536]{1,0:T(8,128)(2,1)S(1)} %all_gather.12, bf16[6144,1536]{1,0:T(8,128)(2,1)} %param.9), kind=kOutput, calls=%fused_computation.20 | convolution fusion | flops 2415919104 | bytes 22413312 | tf_op jit(solution)/shard_map/dot_general | solution.py:27
  32.7 0.0 reduce-scatter.3.cloned.1.call-update
  32.7 0.0 all-gather.3.cloned.1.call-start
  32.8 40.6 %reduce-scatter.3.cloned.1.call-done = f32[16,6144]{1,0:T(8,128)} async-done(((f32[128,6144]{1,0:T(8,128)}), f32[16,6144]{1,0:T(8,128)}) %reduce-scatter.3.cloned.1.call-update) | async-done | bytes 393232 | tf_op jit(solution)/shard_map/reduce_scatter | solution.py:26
  73.4 0.0 copy-done.1
  73.4 2.0 %fusion.7 = (bf16[16,6144]{1,0:T(8,128)(2,1)}, bf16[16,6144]{1,0:T(8,128)(2,1)}) fusion(bf16[16,6144]{1,0:T(8,128)(2,1)S(1)} %copy-done.1, f32[16,6144]{1,0:T(8,128)} %reduce-scatter.3.cloned.1.call-done), kind=kLoop, calls=%fused_computation.16 | loop fusion | flops 2162688 | bytes 983040 | tf_op jit(solution)/shard_map/convert_element_type | solution.py:33
  75.4 0.0 all-gather.3.cloned.1.call-update
  75.5 0.0 all-gather.5.cloned.1.call-start
  75.5 0.7 all-gather.5.cloned.1.call-update
  76.2 0.0 reduce-scatter.5.cloned.1.call-start
  76.2 0.0 copy-done.2
  76.3 9.6 %all_gather.14 = bf16[128,1536]{1,0:T(8,128)(2,1)S(1)} all-gather(bf16[32,1536]{1,0:T(8,128)(2,1)S(1)} %copy-done.2), channel_id=1, replica_groups=mesh['row'=4,'col'=8] {'row'}, dimensions={0}, use_global_device_ids=true | all-gather | bytes 491520 | tf_op jit(solution)/shard_map/all_gather | solution.py:42
  85.8 14.0 %all-gather.3.cloned.1.call-done = bf16[128,6144]{1,0:T(8,128)(2,1)} async-done(((bf16[16,6144]{1,0:T(8,128)(2,1)}), bf16[128,6144]{1,0:T(8,128)(2,1)}) %all-gather.3.cloned.1.call-update) | async-done | bytes 1572880 | tf_op jit(solution)/shard_map/all_gather | solution.py:37
  99.8 0.0 copy-start
  99.8 10.5 %fusion.12 = f32[128,1536]{1,0:T(8,128)} fusion(bf16[128,6144]{1,0:T(8,128)(2,1)} %all-gather.3.cloned.1.call-done, bf16[6144,1536]{1,0:T(8,128)(2,1)} %param.8), kind=kOutput, calls=%fused_computation.21 | convolution fusion | flops 2415919104 | bytes 21233664 | tf_op jit(solution)/shard_map/dot_general | solution.py:48
  110.3 0.0 reduce-scatter.5.cloned.1.call-update
  110.3 0.0 copy-done
  110.3 9.5 %convolution_convert_fusion.1 = bf16[6144,1536]{1,0:T(8,128)(2,1)} fusion(bf16[128,6144]{1,0:T(8,128)(2,1)S(1)} %copy-done, bf16[128,1536]{1,0:T(8,128)(2,1)S(1)} %all_gather.14), kind=kOutput, calls=%fused_computation.1 | convolution fusion | flops 2425356288 | bytes 20840448 | tf_op jit(solution)/shard_map/dot_general | solution.py:43
  119.8 6.8 %all-gather.5.cloned.1.call-done = bf16[128,6144]{1,0:T(8,128)(2,1)} async-done(((bf16[16,6144]{1,0:T(8,128)(2,1)}), bf16[128,6144]{1,0:T(8,128)(2,1)}) %all-gather.5.cloned.1.call-update) | async-done | bytes 1572880 | tf_op jit(solution)/shard_map/all_gather | solution.py:36
  126.7 10.9 %convolution_convert_fusion = bf16[6144,1536]{1,0:T(8,128)(2,1)} fusion(bf16[128,6144]{1,0:T(8,128)(2,1)} %all-gather.5.cloned.1.call-done, bf16[128,1536]{1,0:T(8,128)(2,1)S(1)} %all_gather.12), kind=kOutput, calls=%fused_computation | convolution fusion | flops 2425356288 | bytes 20840448 | tf_op jit(solution)/shard_map/dot_general | solution.py:39
  137.6 17.5 %reduce-scatter.5.cloned.1.call-done = f32[32,1536]{1,0:T(8,128)} async-done(((f32[128,1536]{1,0:T(8,128)}), f32[32,1536]{1,0:T(8,128)}) %reduce-scatter.5.cloned.1.call-update) | async-done | bytes 196624 | tf_op jit(solution)/shard_map/reduce_scatter | solution.py:47
  155.1 1.6 convert_element_type.20
Async XLA Ops:
  7.2 66.3 %reduce-scatter.3.cloned.1.call-start = ((), (), s32[]{:S(2)}) async-start(), calls=%async_computation.2 | async-start | bytes 3538944 | tf_op jit(solution)/shard_map/reduce_scatter | solution.py:26
  18.5 54.9 %copy-start.1 = (bf16[16,6144]{1,0:T(8,128)(2,1)S(1)}, bf16[16,6144]{1,0:T(8,128)(2,1)}, u32[]{:S(2)}) copy-start(bf16[16,6144]{1,0:T(8,128)(2,1)} %param.7) | copy-start | bytes 589828
  18.5 57.7 %copy-start.2 = (bf16[32,1536]{1,0:T(8,128)(2,1)S(1)}, bf16[32,1536]{1,0:T(8,128)(2,1)}, u32[]{:S(2)}) copy-start(bf16[32,1536]{1,0:T(8,128)(2,1)} %param.5) | copy-start | bytes 294916
  32.7 67.1 %all-gather.3.cloned.1.call-start = ((), (), s32[]{:S(2)}) async-start(), calls=%async_computation.3 | async-start | bytes 1769472 | tf_op jit(solution)/shard_map/all_gather | solution.py:37
  75.5 51.2 %all-gather.5.cloned.1.call-start = ((), (), s32[]{:S(2)}) async-start(), calls=%async_computation.5 | async-start | bytes 1769472 | tf_op jit(solution)/shard_map/all_gather | solution.py:36
  76.2 78.9 %reduce-scatter.5.cloned.1.call-start = ((), (), s32[]{:S(2)}) async-start(), calls=%async_computation.4 | async-start | bytes 983040 | tf_op jit(solution)/shard_map/reduce_scatter | solution.py:47
  99.8 10.5 %copy-start = (bf16[128,6144]{1,0:T(8,128)(2,1)S(1)}, bf16[128,6144]{1,0:T(8,128)(2,1)}, u32[]{:S(2)}) copy-start(bf16[128,6144]{1,0:T(8,128)(2,1)} %all-gather.3.cloned.1.call-done) | copy-start | bytes 4718596
Sparse Core Ops, SparseCore 0:
  32.8 40.5 reduce-scatter.2
  75.6 24.1 all-gather.2
  102.1 24.5 all-gather.4
  129.4 25.6 reduce-scatter.4
where the time goes:
time: 163 us
  waiting for transfers between devices  79.7 us (49%)
  matrix products  45.1 us (28%)
  blocking collectives  20.9 us (13%)
  between operations  13.8 us (8%)
  other arithmetic  3.6 us (2%)
    reduce_scatter x1, waiting for transfers between devices, per_device(): lax.psum_scatter(lax.dot_general(row_block, w_out, contract_cols, preferr...  40.6 us
    reduce_scatter x1, waiting for transfers between devices, per_device(): lax.psum_scatter(jnp.dot(row_block, w_in, preferred_element_type=jnp.floa...  17.5 us
    dot_general x1, matrix products, per_device(): lax.dot_general(row_block, w_out, contract_cols, preferred_element_type=j...  14.2 us
    all_gather x1, waiting for transfers between devices, per_device(): lax.all_gather(grad_pre_local, 'col', axis=0, tiled=True)  14 us
    all_gather x1, blocking collectives, per_device(): out_cols = lax.all_gather(grad_out, 'row', axis=0, tiled=True)  11.3 us
    dot_general x1, matrix products, per_device(): lax.dot_general(hidden_all, out_cols, contract_rows, preferred_element_ty...  10.9 us
    dot_general x1, matrix products, per_device(): jnp.dot(row_block, w_in, preferred_element_type=jnp.float32)  10.5 us
    all_gather x1, blocking collectives, per_device(): tok_cols = lax.all_gather(tokens, 'row', axis=0, tiled=True)  9.58 us
  transfers between devices with their start and end apart: 4, of which 4 were waited for; matrix products, arithmetic and copies ran while one was open for 19% of the time, Pallas kernels for 0%

commit v1 on v0

v1 whole, which is shorter than its diff:
```python
import functools

import jax
import jax.numpy as jnp
from jax import lax
from jax.experimental import pallas as pl
from jax.experimental.pallas import tpu as pltpu
from jax.sharding import PartitionSpec as P

tanh_scale = 0.7978845608028654
cubic_term = 0.044715
VMEM_LIMIT = 16 * 1024 * 1024
CHUNKS = 2
AHEAD = 4
FLOPS = 8_000_000_000


def gelu_parts(pre_act):
    pre_value = pre_act.astype(jnp.float32)
    tanh_arg = tanh_scale * (pre_value + cubic_term * pre_value * pre_value * pre_value)
    tangent = jnp.tanh(tanh_arg)
    hidden_value = 0.5 * pre_value * (1.0 + tangent)
    gelu_slope = 0.5 * (1.0 + tangent) + 0.5 * pre_value * (
        1.0 - tangent * tangent
    ) * tanh_scale * (1.0 + 3.0 * cubic_term * pre_value * pre_value)
    return (hidden_value, gelu_slope)


def per_device_any(tokens, grad_out, pre_act, w_in, w_out):
    contract_rows = (((0,), (0,)), ((), ()))
    contract_cols = (((1,), (1,)), ((), ()))
    out_cols = lax.all_gather(grad_out, "row", axis=0, tiled=True)
    grad_hidden = lax.psum_scatter(
        lax.dot_general(out_cols, w_out, contract_cols, preferred_element_type=jnp.float32),
        "col",
        scatter_dimension=0,
        tiled=True,
    )
    hidden_value, gelu_slope = gelu_parts(pre_act)
    grad_pre = (grad_hidden * gelu_slope).astype(jnp.bfloat16)
    hidden_all = lax.all_gather(hidden_value.astype(jnp.bfloat16), "col", axis=0, tiled=True)
    grad_pre_all = lax.all_gather(grad_pre, "col", axis=0, tiled=True)
    grad_w_out = lax.dot_general(
        hidden_all, out_cols, contract_rows, preferred_element_type=jnp.float32
    ).astype(jnp.bfloat16)
    tok_cols = lax.all_gather(tokens, "row", axis=0, tiled=True)
    grad_w_in = lax.dot_general(
        grad_pre_all, tok_cols, contract_rows, preferred_element_type=jnp.float32
    ).astype(jnp.bfloat16)
    grad_tokens = lax.psum_scatter(
        jnp.dot(grad_pre_all, w_in, preferred_element_type=jnp.float32),
        "row",
        scatter_dimension=0,
        tiled=True,
    ).astype(jnp.bfloat16)
    return (grad_tokens, grad_w_in, grad_w_out)


RELATIVE = (0, 2, 1, 3)
ANY = pl.BlockSpec(memory_space=pl.ANY)
VMEM = pl.BlockSpec(memory_space=pltpu.VMEM)
SMEM = pl.BlockSpec(memory_space=pltpu.SMEM)


COST = pl.CostEstimate(flops=FLOPS, bytes_accessed=0, transcendentals=0)
SHORT = pl.CostEstimate(flops=FLOPS // 4, bytes_accessed=0, transcendentals=0)
LIGHT = pl.CostEstimate(flops=FLOPS // 100, bytes_accessed=0, transcendentals=0)


def params(**kw):
    return pltpu.CompilerParams(vmem_limit_bytes=VMEM_LIMIT, **kw)


def swap_rows(array, d):
    return lax.ppermute(array, "row", [(r, r ^ d) for r in range(4)])


def swap_chips(array, d):
    return lax.ppermute(array, "col", [(i, i ^ (2 * d)) for i in range(8)])


def swap_cores(array):
    return lax.ppermute(array, "col", [(i, i ^ 1) for i in range(8)])


def cuts(width, step=256):
    return [slice(n, n + step) for n in range(0, width, step)]


def join_rows(pieces, place, after=()):
    rows, width = pieces[0].shape

    def body(place_ref, p0, p1, p2, p3, *rest):
        place_rows((p0, p1, p2, p3), place_ref, rest[len(after)])

    return pl.pallas_call(
        body,
        out_shape=jax.ShapeDtypeStruct((4 * rows, width), pieces[0].dtype),
        in_specs=[SMEM] + [VMEM] * 4 + [ANY] * len(after),
        out_specs=VMEM,
        compiler_params=params(),
        cost_estimate=LIGHT,
        name="join_rows",
    )(place, *pieces, *after)


def place_rows(pieces, place_ref, out):
    block = pieces[0].shape[0] // 2
    core = place_ref[4]
    for d, piece in enumerate(pieces):
        at = place_ref[d]
        own = pl.multiple_of(core * block, block)
        other = pl.multiple_of((1 - core) * block, block)
        low = pl.multiple_of(at * block, block)
        high = pl.multiple_of((at + 4) * block, block)
        out[pl.ds(low, block), :] = piece[pl.ds(own, block), :]
        out[pl.ds(high, block), :] = piece[pl.ds(other, block), :]


def hidden_grad(x, w_out, first, units, after=(), place=None):
    join = place is not None
    width = w_out.shape[1]
    tokens = 4 * x[0].shape[0] if join else x[0].shape[1]
    half = tokens // 2
    cut = cuts(units)
    pieces = len(x)

    def body(*refs):
        refs = list(refs)
        place_ref = refs.pop(0) if join else None
        x_refs, w_ref = refs[:pieces], refs[pieces]
        own, other, *rest = refs[pieces + 1 + len(after) :]
        held, sems = rest[-2:]
        copies = [
            pltpu.make_async_copy(
                w_ref.at[pl.ds(first + c.start, c.stop - c.start)], held.at[c], sems.at[n]
            )
            for n, c in enumerate(cut)
        ]
        for copy in copies[:AHEAD]:
            copy.start()
        if join:
            joined, flipped = rest[:2]
            place_rows(x_refs, place_ref, joined)
            flipped[...] = joined[...].T
        else:
            flipped = x_refs[0]
        for n, c in enumerate(cut):
            copies[n].wait()
            if n + AHEAD < len(cut):
                copies[n + AHEAD].start()
            value = jnp.dot(held[c, :], flipped[...], preferred_element_type=jnp.float32).T
            own[:, c] = value[:half]
            other[:, c] = value[half:].astype(jnp.bfloat16)

    shapes = [
        jax.ShapeDtypeStruct((half, units), jnp.float32),
        jax.ShapeDtypeStruct((half, units), jnp.bfloat16),
    ]
    if join:
        shapes += [
            jax.ShapeDtypeStruct((tokens, width), jnp.bfloat16),
            jax.ShapeDtypeStruct((width, tokens), jnp.bfloat16),
        ]
    return pl.pallas_call(
        body,
        in_specs=[SMEM] * join + [VMEM] * pieces + [ANY] * (1 + len(after)),
        out_specs=[VMEM] * len(shapes),
        out_shape=shapes,
        scratch_shapes=[
            pltpu.VMEM((units, width), jnp.bfloat16),
            pltpu.SemaphoreType.DMA((len(cut),)),
        ],
        compiler_params=params(),
        cost_estimate=LIGHT if join else COST,
        name="hidden_grad",
    )(*([place] if join else []), *x, w_out, *after)


def add(own, got):
    return own[...] + got[...].astype(jnp.float32)


def halve(value, held, send):
    keep = held.shape[0]
    held[...] = value[:keep]
    send[...] = value[keep:].astype(jnp.bfloat16)


def slope_times(value, pre_ref, first):
    units = value.shape[1]
    slope = gelu_parts(pre_ref[:, first * units : (first + 1) * units])[1]
    return (value * slope).astype(jnp.bfloat16)


def small(body, operands, shapes, after=(), cost=COST, name="small"):
    inputs = len(operands)

    def call(*refs):
        body(*refs[:inputs], *refs[inputs + len(after) :])

    return pl.pallas_call(
        call,
        out_shape=[jax.ShapeDtypeStruct(shape, kind) for shape, kind in shapes],
        in_specs=[VMEM] * inputs + [ANY] * len(after),
        out_specs=[VMEM] * len(shapes),
        compiler_params=params(),
        cost_estimate=cost,
        name=name,
    )(*operands, *after)


def sum_cores(own, got, after=()):
    rows, units = own.shape
    half = (rows // 2, units)

    def body(own, got, held, send):
        halve(add(own, got), held, send)

    return small(
        body, [own, got], [(half, jnp.float32), (half, jnp.bfloat16)], after, name="sum_cores"
    )


def sum_near(held0, near0, own1, core1, after=()):
    rows, units = own1.shape
    half, quarter = (rows // 2, units), (rows // 4, units)

    def body(held0, near0, own1, core1, mine0, send0, held1, send1):
        halve(add(held0, near0), mine0, send0)
        halve(add(own1, core1), held1, send1)

    return small(
        body,
        [held0, near0, own1, core1],
        [
            (quarter, jnp.float32),
            (quarter, jnp.bfloat16),
            (half, jnp.float32),
            (half, jnp.bfloat16),
        ],
        after,
        name="sum_near",
    )


def sum_far(mine0, far0, held1, near1, pre_act, after=()):
    quarter = mine0.shape

    def body(mine0, far0, held1, near1, pre_ref, grad0, mine1, send1):
        grad0[...] = slope_times(add(mine0, far0), pre_ref, 0)
        halve(add(held1, near1), mine1, send1)

    return small(
        body,
        [mine0, far0, held1, near1, pre_act],
        [(quarter, jnp.bfloat16), (quarter, jnp.float32), (quarter, jnp.bfloat16)],
        after,
        name="sum_far",
    )


def pair_far(grad0, far0, mine1, far1, pre_act, pre_most, pre_last, after=()):
    rows, units = grad0.shape
    most, wide = pre_most.shape

    def body(grad0, far0, mine1, far1, pre_ref, pre_most, pre_last, pair0, grad1, pre_own):
        pair0[:rows] = grad0[...]
        pair0[rows:] = far0[...]
        grad1[...] = slope_times(add(mine1, far1), pre_ref, 1)
        pre_own[:most] = pre_most[...]
        pre_own[most:] = pre_last[...]

    return small(
        body,
        [grad0, far0, mine1, far1, pre_act, pre_most, pre_last],
        [
            ((2 * rows, units), jnp.bfloat16),
            ((rows, units), jnp.bfloat16),
            ((most + rows, wide), jnp.bfloat16),
        ],
        after,
        name="pair_far",
    )


def pair_near(near0, grad1, far1, after=()):
    rows, units = grad1.shape

    def body(near0, grad1, far1, blocks0, pair1):
        blocks0[...] = near0[...]
        pair1[:rows] = grad1[...]
        pair1[rows:] = far1[...]

    return small(
        body,
        [near0, grad1, far1],
        [(near0.shape, jnp.bfloat16), ((2 * rows, units), jnp.bfloat16)],
        after,
        LIGHT,
        "pair_near",
    )


def out_weight_grad(pre, x, first, rows, held, after=()):
    tokens, width = x.shape
    units = pre[0].shape[1]
    pieces = len(pre)
    extra = len(after) + (held is not None)
    parts = cuts(rows)

    def body(*refs):
        pre_refs, x_ref = refs[:pieces], refs[pieces]
        out, token, stage, sems = refs[pieces + 1 + extra :]
        copies = []
        for n, part in enumerate(parts):
            some = slice(first + part.start, first + part.stop)
            value = jnp.concatenate([ref[:, some] for ref in pre_refs], axis=0)
            value = value.astype(jnp.float32)
            tangent = jnp.tanh(tanh_scale * (value + cubic_term * value * value * value))
            hidden = (0.5 * value * (1.0 + tangent)).astype(jnp.bfloat16).T
            for cut in cuts(width):
                stage[part, cut] = jnp.dot(
                    hidden, x_ref[:, cut], preferred_element_type=jnp.float32
                ).astype(jnp.bfloat16)
            copies.append(pltpu.make_async_copy(stage.at[part], out.at[some], sems.at[n]))
            copies[-1].start()
        token[...] = jnp.zeros_like(token)
        for copy in copies:
            copy.wait()

    operands = [*pre, x] + ([] if held is None else [held]) + list(after)
    return pl.pallas_call(
        body,
        in_specs=[VMEM] * (pieces + 1) + [ANY] * extra,
        out_specs=[ANY, VMEM],
        out_shape=[
            jax.ShapeDtypeStruct((units, width), jnp.bfloat16),
            jax.ShapeDtypeStruct((8, 128), jnp.float32),
        ],
        scratch_shapes=[
            pltpu.VMEM((rows, width), jnp.bfloat16),
            pltpu.SemaphoreType.DMA((len(parts),)),
        ],
        input_output_aliases={} if held is None else {pieces + 1: 0},
        compiler_params=params(),
        cost_estimate=COST,
        name="out_weight_grad",
    )(*operands)


def in_grads(grad_pre, w_in, tok, first, count, rows, held, total, place, after=()):
    tokens, width = tok.shape
    block = tokens // 8
    pieces = len(grad_pre)
    start, last = total is None, place is not None

    def body(*refs):
        refs = list(refs)
        place_ref = refs.pop(0) if last else None
        w_ref, tok_ref = refs[pieces : pieces + 2]
        if last:
            out, parts, sums = refs[-6], refs[-5:-1], refs[-1]
        else:
            out, sums = refs[-2:]
        value = jnp.concatenate([ref[...] for ref in refs[:pieces]], axis=0)

        @pl.when(pl.program_id(0) == 0)
        def _():
            sums[...] = jnp.zeros_like(sums) if start else refs[pieces + 3][...]

        here = pl.multiple_of((first + pl.program_id(0)) * rows, rows)
        sums[...] += jnp.dot(
            value, w_ref[pl.ds(here, rows), :], preferred_element_type=jnp.float32
        )
        for some in cuts(rows):
            flipped = value[:, some].T
            for cut in cuts(width):
                out[some, cut] = jnp.dot(
                    flipped, tok_ref[:, cut], preferred_element_type=jnp.float32
                ).astype(jnp.bfloat16)

        if last:

            @pl.when(pl.program_id(0) == count - 1)
            def _():
                core = place_ref[4]
                for d, part in enumerate(parts):
                    low = pl.multiple_of((place_ref[d] + 4 * core) * block, block)
                    high = pl.multiple_of((place_ref[d] + 4 * (1 - core)) * block, block)
                    part[:block] = sums[pl.ds(low, block), :].astype(part.dtype)
                    part[block:] = sums[pl.ds(high, block), :].astype(part.dtype)

    whole = pl.BlockSpec((tokens, width), lambda i: (0, 0))
    in_specs = [pl.BlockSpec((p.shape[0], rows), lambda i: (0, i)) for p in grad_pre]
    in_specs += [
        VMEM,
        whole,
    ]
    operands = [*grad_pre, w_in, tok]
    if not start:
        in_specs += [ANY, whole]
        operands += [held, total]
    in_specs += [ANY] * len(after)
    operands += after
    out_specs = [pl.BlockSpec((rows, width), lambda i: (first + i, 0))]
    out_shape = [jax.ShapeDtypeStruct(w_in.shape, jnp.bfloat16)]
    scratch = []
    if last:
        in_specs = [SMEM] + in_specs
        operands = [place] + operands
        out_specs += [pl.BlockSpec((2 * block, width), lambda i: (0, 0))] * 4
        out_shape += [
            jax.ShapeDtypeStruct((2 * block, width), kind)
            for kind in (jnp.float32, jnp.bfloat16, jnp.bfloat16, jnp.bfloat16)
        ]
        scratch = [pltpu.VMEM((tokens, width), jnp.float32)]
    else:
        out_specs.append(whole)
        out_shape.append(jax.ShapeDtypeStruct((tokens, width), jnp.float32))
    return pl.pallas_call(
        body,
        grid=(count,),
        in_specs=in_specs,
        out_specs=out_specs,
        out_shape=out_shape,
        scratch_shapes=scratch,
        input_output_aliases={} if start else {pieces + 2 + last: 0},
        compiler_params=params(),
        cost_estimate=COST,
        name="in_grads",
    )(*operands)


def mark(after=(), cost=SHORT):
    def body(*refs):
        refs[-1][...] = jnp.zeros_like(refs[-1])

    return pl.pallas_call(
        body,
        out_shape=jax.ShapeDtypeStruct((8, 128), jnp.float32),
        in_specs=[ANY] * len(after),
        out_specs=VMEM,
        compiler_params=params(),
        cost_estimate=cost,
        name="mark",
    )(*after)


def tie(value, after, cost=LIGHT):
    def body(*refs):
        pass

    return pl.pallas_call(
        body,
        out_shape=jax.ShapeDtypeStruct(value.shape, value.dtype),
        in_specs=[ANY] * (1 + len(after)),
        out_specs=ANY,
        input_output_aliases={0: 0},
        compiler_params=params(),
        cost_estimate=cost,
        name="tie",
    )(value, *after)


def stack(pieces, after=()):
    rows, units = pieces[0].shape
    count = len(pieces)

    def body(*refs):
        for n in range(count):
            refs[-1][n * rows : (n + 1) * rows] = refs[n][...]

    return pl.pallas_call(
        body,
        out_shape=jax.ShapeDtypeStruct((count * rows, units), pieces[0].dtype),
        in_specs=[VMEM] * count + [ANY] * len(after),
        out_specs=VMEM,
        compiler_params=params(),
        cost_estimate=COST,
        name="stack",
    )(*pieces, *after)


def per_device_line(tokens, grad_out, pre_act, w_in, w_out):
    row = lax.axis_index("row")
    col = lax.axis_index("col")
    chip, core = col // 2, col % 2
    apart = [chip ^ row ^ d for d in range(4)]
    spots = [2 * (v & 1) + v // 2 for v in apart]
    place = jnp.stack(spots + [core]).astype(jnp.int32)

    units = w_out.shape[0]
    rows = 512
    per_chunk = units // CHUNKS
    count = per_chunk // rows

    started = mark()
    for _ in range(7):
        started = mark((started,))
    w_out = pltpu.with_memory_space_constraint(w_out, pltpu.HBM)
    pre_far, pre_near = swap_chips(pre_act, 2), swap_chips(pre_act, 1)
    own0, send0, x, flipped = hidden_grad(
        [grad_out] + [swap_rows(grad_out, d) for d in (1, 2, 3)],
        w_out,
        0,
        per_chunk,
        (started,),
        place,
    )
    pre_most = stack([pre_act, pre_far, pre_near], (send0,))
    step = mark((pre_most,), COST)
    held0, out0 = sum_cores(own0, swap_cores(send0), (step,))
    own1, send1 = hidden_grad([flipped], w_out, per_chunk, per_chunk, (out0,))
    mine = stack([tokens], (send1,))
    mine0, out0, held1, out1 = sum_near(
        held0, swap_chips(out0, 1), own1, swap_cores(send1), (mine,)
    )
    grad0, mine1, out1 = sum_far(
        mine0, swap_chips(out0, 2), held1, swap_chips(out1, 1), pre_act
    )
    tok = join_rows([mine] + [swap_rows(mine, d) for d in (1, 2, 3)], place, (grad0,))
    pair0, grad1, pre_own = pair_far(
        grad0,
        swap_chips(grad0, 2),
        mine1,
        swap_chips(out1, 2),
        pre_act,
        pre_most,
        swap_chips(pre_far, 1),
        (tok,),
    )
    pre = [pre_own, swap_cores(pre_own)]
    grad_w_out, token = out_weight_grad(pre, x, 0, units // 2, None, (pair0,))
    near0, pair1 = pair_near(swap_chips(pair0, 1), grad1, swap_chips(grad1, 2), (token,))
    whole = [pair0, near0, swap_cores(pair0), swap_cores(near0)]
    grad_w_in, total = in_grads(
        whole, w_in, tok, 0, count // 2, 2 * rows, None, None, None, (pair1,)
    )
    near1 = tie(swap_chips(pair1, 1), (total,))
    whole = [pair1, near1, swap_cores(pair1), swap_cores(near1)]
    grad_w_in, part, *parts = in_grads(
        whole, w_in, tok, count // 2, count // 2, 2 * rows, grad_w_in, total, place
    )
    grad_w_out, _ = out_weight_grad(pre, x, units // 2, units // 2, grad_w_out, (part,))
    for d in (1, 2, 3):
        part = part + swap_rows(parts[d - 1], d).astype(jnp.float32)
    return (part.astype(jnp.bfloat16), grad_w_in, grad_w_out)


def solution(mesh):
    line = mesh.shape["row"] == 4 and mesh.shape["col"] == 8
    in_specs = (P("row", "col"), P("row", "col"), P("col", "row"), P("row", "col"), P("row", "col"))
    out_specs = (P("row", "col"), P("row", "col"), P("row", "col"))
    return jax.shard_map(
        per_device_line if line else per_device_any,
        mesh=mesh,
        in_specs=in_specs,
        out_specs=out_specs,
        check_vma=False,
    )
```

time: 163 us -> 86.5 us (0.53)
  waiting for transfers between devices: 79.7 us -> 16.5 us
  matrix products: 45.1 us -> 0 us
  Pallas kernels: 0 us -> 37.8 us
  starting transfers between devices: 0.16 us -> 30.3 us
  blocking collectives: 20.9 us -> 0 us
  between operations: 13.8 us -> 0.97 us
  other arithmetic: 3.6 us -> 0.69 us
    reduce_scatter x2 -> x0, waiting for transfers between devices: 58.2 us -> none  [the longest x1 40.6 us: per_device(): lax.psum_scatter(lax.dot_general(row_block, w_out, contract_cols, preferr...]
    dot_general x4 -> x0, matrix products: 45.1 us -> none  [the longest x1 14.2 us: per_device(): lax.dot_general(row_block, w_out, contract_cols, preferred_element_type=j...]
    pallas_call x0 -> x24, Pallas kernels: none -> 37.8 us  [the longest x2 13.5 us: hidden_grad(): pl.pallas_call(body, in_specs=[SMEM] * join + [VMEM] * pieces + [ANY] * (...]
    ppermute x0 -> x27, starting transfers between devices: none -> 30.3 us  [the longest x11 17.2 us: swap_chips(): return lax.ppermute(array, 'col', [(i, i ^ 2 * d) for i in range(8)])]
    all_gather x2 -> x0, blocking collectives: 20.9 us -> none  [the longest x1 11.3 us: per_device(): out_cols = lax.all_gather(grad_out, 'row', axis=0, tiled=True)]
    all_gather x2 -> x0, waiting for transfers between devices: 20.8 us -> none  [the longest x1 14 us: per_device(): lax.all_gather(grad_pre_local, 'col', axis=0, tiled=True)]
    ppermute x0 -> x27, waiting for transfers between devices: none -> 16.5 us  [the longest x11 10.9 us: swap_chips(): return lax.ppermute(array, 'col', [(i, i ^ 2 * d) for i in range(8)])]
    convert_element_type x2 -> x1, other arithmetic: 3.6 us -> 0.69 us  [per_device_line(): return (part.astype(jnp.bfloat16), grad_w_in, grad_w_out)]
  transfers between devices with their start and end apart: 4 -> 27, of which waited for: 4 -> 12; matrix products, arithmetic and copies ran while one was open for 19% -> 0% of each run, Pallas kernels for 0% -> 35%
where the time goes in v1:
time: 86.5 us; the launch traced here: 86.4 us
  Pallas kernels  37.8 us (44%)
  starting transfers between devices  30.3 us (35%)
  waiting for transfers between devices  16.5 us (19%)
  between operations  0.97 us (1%)
    ppermute x11, starting transfers between devices, swap_chips(): return lax.ppermute(array, 'col', [(i, i ^ 2 * d) for i in range(8)])  17.2 us
    pallas_call x2, Pallas kernels, hidden_grad(): pl.pallas_call(body, in_specs=[SMEM] * join + [VMEM] * pieces + [ANY] * (...  13.5 us
    pallas_call x2, Pallas kernels, in_grads(): pl.pallas_call(body, grid=(count,), in_specs=in_specs, out_specs=out_spec...  13.2 us
    ppermute x9, starting transfers between devices, swap_rows(): return lax.ppermute(array, 'row', [(r, r ^ d) for r in range(4)])  11.8 us
    ppermute x11, waiting for transfers between devices, swap_chips(): return lax.ppermute(array, 'col', [(i, i ^ 2 * d) for i in range(8)])  10.9 us
    pallas_call x2, Pallas kernels, out_weight_grad(): pl.pallas_call(body, in_specs=[VMEM] * (pieces + 1) + [ANY] * extra, out_...  9.87 us
    ppermute x7, waiting for transfers between devices, swap_cores(): return lax.ppermute(array, 'col', [(i, i ^ 1) for i in range(8)])  4.68 us
  transfers between devices with their start and end apart: 27, of which 12 were waited for; matrix products, arithmetic and copies ran while one was open for 0% of the time, Pallas kernels for 35%

profile of v1, /device:TPU:0, one launch (start us, length us, event | category | flops | bytes accessed | tf_op | source)
XLA Modules:
  0.0 86.4 jit_solution(3688107786730139997)
XLA Ops:
  0.6 3.0 %collective-permute-start.1 = (bf16[32,1536]{1,0:T(8,128)(2,1)}, bf16[32,1536]{1,0:T(8,128)(2,1)S(1)}, u32[]{:S(2)}, u32[]{:S(2)}) collective-permute-start(bf16[32,1536]{1,0:T(8,128)(2,1)} %refs_1_.2), channel_id=1, source_target_pairs={{0,16},{8,24},{16,0},{24,8},{1,17},{9,25},{17,1},{25,9},{2,18},{10... | collective-permute-start | bytes 294920 | tf_op jit(solution)/shard_map/ppermute | solution.py:75
  3.7 1.5 %collective-permute-start = (bf16[32,1536]{1,0:T(8,128)(2,1)}, bf16[32,1536]{1,0:T(8,128)(2,1)S(1)}, u32[]{:S(2)}, u32[]{:S(2)}) collective-permute-start(bf16[32,1536]{1,0:T(8,128)(2,1)} %refs_1_.2), channel_id=1, source_target_pairs={{0,8},{8,0},{16,24},{24,16},{1,9},{9,1},{17,25},{25,17},{2,10},{10... | collective-permute-start | bytes 294920 | tf_op jit(solution)/shard_map/ppermute | solution.py:75
  5.2 2.0 %collective-permute-start.5 = (bf16[16,6144]{1,0:T(8,128)(2,1)}, bf16[16,6144]{1,0:T(8,128)(2,1)S(1)}, u32[]{:S(2)}, u32[]{:S(2)}) collective-permute-start(bf16[16,6144]{1,0:T(8,128)(2,1)} %refs_4_.4), channel_id=1, source_target_pairs={{0,2},{1,3},{2,0},{3,1},{4,6},{5,7},{6,4},{7,5},{8,10},{9,11},{10,... | collective-permute-start | bytes 589832 | tf_op jit(solution)/shard_map/ppermute | solution.py:79
  7.2 2.6 %collective-permute-start.4 = (bf16[16,6144]{1,0:T(8,128)(2,1)}, bf16[16,6144]{1,0:T(8,128)(2,1)S(1)}, u32[]{:S(2)}, u32[]{:S(2)}) collective-permute-start(bf16[16,6144]{1,0:T(8,128)(2,1)} %refs_4_.4), channel_id=1, source_target_pairs={{0,4},{1,5},{2,6},{3,7},{4,0},{5,1},{6,2},{7,3},{8,12},{9,13},{10,... | collective-permute-start | bytes 589832 | tf_op jit(solution)/shard_map/ppermute | solution.py:79
  10.0 0.9 collective-permute-done.2.refs_4_
  10.9 7.0 %hidden_grad.2 = (f32[64,3072]{1,0:T(8,128)S(1)}, bf16[64,3072]{1,0:T(8,128)(2,1)S(1)}, bf16[128,1536]{1,0:T(8,128)(2,1)S(1)}, bf16[1536,128]{1,0:T(8,128)(2,1)S(1)}) custom-call(s32[5]{0:T(128)S(1)} %stack.25.refs_0_.place_ref, bf16[32,1536]{1,0:T(8,128)(2,1)S(1)} %copy-done, bf16[32,1536]{1,0:T(8,128)(2,1)S(1)} %collective-permute-done.refs_2_, ...), custom_call_target="tpu_custom_call" | custom-call | flops 80000000 | tf_op jit(solution)/shard_map/hidden_grad/pallas_call | solution.py:165
  18.2 1.5 %collective-permute-done.3.refs_1_ = bf16[64,3072]{1,0:T(8,128)(2,1)S(1)} collective-permute-done((bf16[64,3072]{1,0:T(8,128)(2,1)S(1)}, bf16[64,3072]{1,0:T(8,128)(2,1)S(1)}, u32[]{:S(2)}, u32[]{:S(2)}) %collective-permute-start.3) | collective-permute-done | bytes 393248 | tf_op jit(solution)/shard_map/ppermute | solution.py:83
  19.8 1.6 %collective-permute-start.6 = (bf16[32,3072]{1,0:T(8,128)(2,1)S(1)}, bf16[32,3072]{1,0:T(8,128)(2,1)S(1)}, u32[]{:S(2)}, u32[]{:S(2)}) collective-permute-start(bf16[32,3072]{1,0:T(8,128)(2,1)S(1)} %get-tuple-element.36.refs_2_), channel_id=1, source_target_pairs={{0,2},{1,3},{2,0},{3,1},{4,6},{5,7},{6,4},{7,5},{8,10},{9,11},{10,... | collective-permute-start | bytes 589832 | tf_op jit(solution)/shard_map/ppermute | solution.py:79
  21.4 6.4 %hidden_grad.3 = (f32[64,3072]{1,0:T(8,128)S(1)}, bf16[64,3072]{1,0:T(8,128)(2,1)S(1)}) custom-call(bf16[1536,128]{1,0:T(8,128)(2,1)S(1)} %get-tuple-element.37.refs_0_, bf16[6144,1536]{1,0:T(8,128)(2,1)} %refs_1_.3, bf16[32,3072]{1,0:T(8,128)(2,1)S(1)} %get-tuple-element.36.refs_2_), custom_call_target="tpu_custom_call" | custom-call | flops 8000000000 | tf_op jit(solution)/shard_map/hidden_grad/pallas_call | solution.py:165
  28.0 1.7 %collective-permute-done.7.refs_3_ = bf16[64,3072]{1,0:T(8,128)(2,1)S(1)} collective-permute-done((bf16[64,3072]{1,0:T(8,128)(2,1)S(1)}, bf16[64,3072]{1,0:T(8,128)(2,1)S(1)}, u32[]{:S(2)}, u32[]{:S(2)}) %collective-permute-start.7) | collective-permute-done | bytes 393248 | tf_op jit(solution)/shard_map/ppermute | solution.py:83
  30.3 2.6 %collective-permute-start.8 = (bf16[16,3072]{1,0:T(8,128)(2,1)S(1)}, bf16[16,3072]{1,0:T(8,128)(2,1)S(1)}, u32[]{:S(2)}, u32[]{:S(2)}) collective-permute-start(bf16[16,3072]{1,0:T(8,128)(2,1)S(1)} %get-tuple-element.41), channel_id=1, source_target_pairs={{0,4},{1,5},{2,6},{3,7},{4,0},{5,1},{6,2},{7,3},{8,12},{9,13},{10,... | collective-permute-start | bytes 294920 | tf_op jit(solution)/shard_map/ppermute | solution.py:79
  32.9 1.6 %collective-permute-start.12 = (bf16[16,6144]{1,0:T(8,128)(2,1)S(1)}, bf16[16,6144]{1,0:T(8,128)(2,1)S(1)}, u32[]{:S(2)}, u32[]{:S(2)}) collective-permute-start(bf16[16,6144]{1,0:T(8,128)(2,1)S(1)} %collective-permute-done.4.refs_1_), channel_id=1, source_target_pairs={{0,2},{1,3},{2,0},{3,1},{4,6},{5,7},{6,4},{7,5},{8,10},{9,11},{10,... | collective-permute-start | bytes 589832 | tf_op jit(solution)/shard_map/ppermute | solution.py:79
  34.5 1.7 %collective-permute-start.15 = (bf16[32,1536]{1,0:T(8,128)(2,1)S(1)}, bf16[32,1536]{1,0:T(8,128)(2,1)S(1)}, u32[]{:S(2)}, u32[]{:S(2)}) collective-permute-start(bf16[32,1536]{1,0:T(8,128)(2,1)S(1)} %stack.27.refs_4_.p0), channel_id=1, source_target_pairs={{0,24},{8,16},{16,8},{24,0},{1,25},{9,17},{17,9},{25,1},{2,26},{10... | collective-permute-start | bytes 294920 | tf_op jit(solution)/shard_map/ppermute | solution.py:75
  36.9 0.8 collective-permute-done.8.refs_1_
  37.7 1.3 %collective-permute-start.13 = (bf16[32,1536]{1,0:T(8,128)(2,1)S(1)}, bf16[32,1536]{1,0:T(8,128)(2,1)S(1)}, u32[]{:S(2)}, u32[]{:S(2)}) collective-permute-start(bf16[32,1536]{1,0:T(8,128)(2,1)S(1)} %stack.27.refs_4_.p0), channel_id=1, source_target_pairs={{0,8},{8,0},{16,24},{24,16},{1,9},{9,1},{17,25},{25,17},{2,10},{10... | collective-permute-start | bytes 294920 | tf_op jit(solution)/shard_map/ppermute | solution.py:75
  39.0 0.7 collective-permute-done.9.refs_3_
  39.9 2.7 %collective-permute-start.11 = (bf16[16,3072]{1,0:T(8,128)(2,1)S(1)}, bf16[16,3072]{1,0:T(8,128)(2,1)S(1)}, u32[]{:S(2)}, u32[]{:S(2)}) collective-permute-start(bf16[16,3072]{1,0:T(8,128)(2,1)S(1)} %get-tuple-element.46), channel_id=1, source_target_pairs={{0,4},{1,5},{2,6},{3,7},{4,0},{5,1},{6,2},{7,3},{8,12},{9,13},{10,... | collective-permute-start | bytes 294920 | tf_op jit(solution)/shard_map/ppermute | solution.py:79
  43.5 1.5 %collective-permute-done.12.refs_6_ = bf16[16,6144]{1,0:T(8,128)(2,1)S(1)} collective-permute-done((bf16[16,6144]{1,0:T(8,128)(2,1)S(1)}, bf16[16,6144]{1,0:T(8,128)(2,1)S(1)}, u32[]{:S(2)}, u32[]{:S(2)}) %collective-permute-start.12) | collective-permute-done | bytes 196640 | tf_op jit(solution)/shard_map/ppermute | solution.py:79
  44.9 5.4 %collective-permute-done.11.refs_3_ = bf16[16,3072]{1,0:T(8,128)(2,1)S(1)} collective-permute-done((bf16[16,3072]{1,0:T(8,128)(2,1)S(1)}, bf16[16,3072]{1,0:T(8,128)(2,1)S(1)}, u32[]{:S(2)}, u32[]{:S(2)}) %collective-permute-start.11) | collective-permute-done | bytes 98336 | tf_op jit(solution)/shard_map/ppermute | solution.py:79
  50.4 1.1 %collective-permute-done.10.refs_1_ = bf16[16,3072]{1,0:T(8,128)(2,1)S(1)} collective-permute-done((bf16[16,3072]{1,0:T(8,128)(2,1)S(1)}, bf16[16,3072]{1,0:T(8,128)(2,1)S(1)}, u32[]{:S(2)}, u32[]{:S(2)}) %collective-permute-start.10) | collective-permute-done | bytes 98336 | tf_op jit(solution)/shard_map/ppermute | solution.py:79
  52.2 2.5 %collective-permute-start.17 = (bf16[16,3072]{1,0:T(8,128)(2,1)S(1)}, bf16[16,3072]{1,0:T(8,128)(2,1)S(1)}, u32[]{:S(2)}, u32[]{:S(2)}) collective-permute-start(bf16[16,3072]{1,0:T(8,128)(2,1)S(1)} %get-tuple-element.48.refs_1_), channel_id=1, source_target_pairs={{0,4},{1,5},{2,6},{3,7},{4,0},{5,1},{6,2},{7,3},{8,12},{9,13},{10,... | collective-permute-start | bytes 294920 | tf_op jit(solution)/shard_map/ppermute | solution.py:79
  54.7 5.2 %out_weight_grad.2 = (bf16[6144,1536]{1,0:T(8,128)(2,1)}, f32[8,128]{1,0:T(8,128)S(1)}) custom-call(bf16[64,6144]{1,0:T(8,128)(2,1)S(1)} %get-tuple-element.49.refs_0_, bf16[64,6144]{1,0:T(8,128)(2,1)S(1)} %collective-permute-done.18.refs_1_, bf16[128,1536]{1,0:T(8,128)(2,1)S(1)} %get-tuple-element.50.refs_2_, ...), custom_call_target="tpu_custom_call" | custom-call | flops 8000000000 | tf_op jit(solution)/shard_map/out_weight_grad/pallas_call | solution.py:333
  59.9 1.3 %collective-permute-done.16.refs_0_ = bf16[32,3072]{1,0:T(8,128)(2,1)S(1)} collective-permute-done((bf16[32,3072]{1,0:T(8,128)(2,1)S(1)}, bf16[32,3072]{1,0:T(8,128)(2,1)S(1)}, u32[]{:S(2)}, u32[]{:S(2)}) %collective-permute-start.16) | collective-permute-done | bytes 196640 | tf_op jit(solution)/shard_map/ppermute | solution.py:79
  61.8 0.8 collective-permute-start.19
  62.8 6.3 %in_grads.2 = (bf16[6144,1536]{1,0:T(8,128)(2,1)}, f32[128,1536]{1,0:T(8,128)S(1)}) custom-call(bf16[32,3072]{1,0:T(8,128)(2,1)S(1)} %get-tuple-element.47.refs_3_.refs_0_, bf16[32,3072]{1,0:T(8,128)(2,1)S(1)} %get-tuple-element.53.refs_1_, bf16[32,3072]{1,0:T(8,128)(2,1)S(1)} %collective-permute-done.20.refs_2_, ...), custom_call_target="tpu_custom_call" | custom-call | flops 8000000000 | tf_op jit(solution)/shard_map/in_grads/pallas_call | solution.py:421
  69.2 1.3 %collective-permute-done.23.refs_4_ = bf16[32,3072]{1,0:T(8,128)(2,1)S(1)} collective-permute-done((bf16[32,3072]{1,0:T(8,128)(2,1)S(1)}, bf16[32,3072]{1,0:T(8,128)(2,1)S(1)}, u32[]{:S(2)}, u32[]{:S(2)}) %collective-permute-start.23) | collective-permute-done | bytes 196640 | tf_op jit(solution)/shard_map/ppermute | solution.py:83
  70.6 6.9 %in_grads.3 = (bf16[6144,1536]{1,0:T(8,128)(2,1)}, f32[32,1536]{1,0:T(8,128)S(1)}, bf16[32,1536]{1,0:T(8,128)(2,1)S(1)}, bf16[32,1536]{1,0:T(8,128)(2,1)S(1)}, bf16[32,1536]{1,0:T(8,128)(2,1)S(1)}) custom-call(s32[5]{0:T(128)S(1)} %stack.25.refs_0_.place_ref, ...), custom_call_target="tpu_custom_call", output_to_operand_aliasing={{0}: (7, {})} | custom-call | flops 8000000000 | tf_op jit(solution)/shard_map/in_grads/pallas_call | solution.py:421
  77.4 0.9 %collective-permute-start.24 = (bf16[32,1536]{1,0:T(8,128)(2,1)S(1)}, bf16[32,1536]{1,0:T(8,128)(2,1)S(1)}, u32[]{:S(2)}, u32[]{:S(2)}) collective-permute-start(bf16[32,1536]{1,0:T(8,128)(2,1)S(1)} %get-tuple-element.57), channel_id=1, source_target_pairs={{0,8},{8,0},{16,24},{24,16},{1,9},{9,1},{17,25},{25,17},{2,10},{10... | collective-permute-start | bytes 294920 | tf_op jit(solution)/shard_map/ppermute | solution.py:75
  78.3 1.2 %collective-permute-start.25 = (bf16[32,1536]{1,0:T(8,128)(2,1)S(1)}, bf16[32,1536]{1,0:T(8,128)(2,1)S(1)}, u32[]{:S(2)}, u32[]{:S(2)}) collective-permute-start(bf16[32,1536]{1,0:T(8,128)(2,1)S(1)} %get-tuple-element.58), channel_id=1, source_target_pairs={{0,16},{8,24},{16,0},{24,8},{1,17},{9,25},{17,1},{25,9},{2,18},{10... | collective-permute-start | bytes 294920 | tf_op jit(solution)/shard_map/ppermute | solution.py:75
  79.5 1.4 %collective-permute-start.26 = (bf16[32,1536]{1,0:T(8,128)(2,1)S(1)}, bf16[32,1536]{1,0:T(8,128)(2,1)S(1)}, u32[]{:S(2)}, u32[]{:S(2)}) collective-permute-start(bf16[32,1536]{1,0:T(8,128)(2,1)S(1)} %get-tuple-element.59), channel_id=1, source_target_pairs={{0,24},{8,16},{16,8},{24,0},{1,25},{9,17},{17,9},{25,1},{2,26},{10... | collective-permute-start | bytes 294920 | tf_op jit(solution)/shard_map/ppermute | solution.py:75
  80.9 4.7 %out_weight_grad.3 = (bf16[6144,1536]{1,0:T(8,128)(2,1)}, f32[8,128]{1,0:T(8,128)}) custom-call(bf16[64,6144]{1,0:T(8,128)(2,1)S(1)} %get-tuple-element.49.refs_0_, bf16[64,6144]{1,0:T(8,128)(2,1)S(1)} %collective-permute-done.18.refs_1_, bf16[128,1536]{1,0:T(8,128)(2,1)S(1)} %get-tuple-element.50.refs_2_, ...), custom_call_target="tpu_custom_call", output_to_operand_aliasing={{0}: (3, {})} | custom-call | flops 8000000000 | tf_op jit(solution)/shard_map/out_weight_grad/pallas_call | solution.py:333
  85.7 0.7 add_convert_fusion
  (65 shorter events, 4.6 us)
Async XLA Ops:
  0.6 9.4 %collective-permute-start.1 = (bf16[32,1536]{1,0:T(8,128)(2,1)}, bf16[32,1536]{1,0:T(8,128)(2,1)S(1)}, u32[]{:S(2)}, u32[]{:S(2)}) collective-permute-start(bf16[32,1536]{1,0:T(8,128)(2,1)} %refs_1_.2), channel_id=1, source_target_pairs={{0,16},{8,24},{16,0},{24,8},{1,17},{9,25},{17,1},{25,9},{2,18},{10... | collective-permute-start | bytes 294920 | tf_op jit(solution)/shard_map/ppermute | solution.py:75
  3.7 6.4 %collective-permute-start = (bf16[32,1536]{1,0:T(8,128)(2,1)}, bf16[32,1536]{1,0:T(8,128)(2,1)S(1)}, u32[]{:S(2)}, u32[]{:S(2)}) collective-permute-start(bf16[32,1536]{1,0:T(8,128)(2,1)} %refs_1_.2), channel_id=1, source_target_pairs={{0,8},{8,0},{16,24},{24,16},{1,9},{9,1},{17,25},{25,17},{2,10},{10... | collective-permute-start | bytes 294920 | tf_op jit(solution)/shard_map/ppermute | solution.py:75
  5.2 5.7 %collective-permute-start.2 = (bf16[32,1536]{1,0:T(8,128)(2,1)}, bf16[32,1536]{1,0:T(8,128)(2,1)S(1)}, u32[]{:S(2)}, u32[]{:S(2)}) collective-permute-start(bf16[32,1536]{1,0:T(8,128)(2,1)} %refs_1_.2), channel_id=1, source_target_pairs={{0,24},{8,16},{16,8},{24,0},{1,25},{9,17},{17,9},{25,1},{2,26},{10... | collective-permute-start | bytes 294920 | tf_op jit(solution)/shard_map/ppermute | solution.py:75
  5.2 12.8 %collective-permute-start.5 = (bf16[16,6144]{1,0:T(8,128)(2,1)}, bf16[16,6144]{1,0:T(8,128)(2,1)S(1)}, u32[]{:S(2)}, u32[]{:S(2)}) collective-permute-start(bf16[16,6144]{1,0:T(8,128)(2,1)} %refs_4_.4), channel_id=1, source_target_pairs={{0,2},{1,3},{2,0},{3,1},{4,6},{5,7},{6,4},{7,5},{8,10},{9,11},{10,... | collective-permute-start | bytes 589832 | tf_op jit(solution)/shard_map/ppermute | solution.py:79
  7.2 10.9 %collective-permute-start.4 = (bf16[16,6144]{1,0:T(8,128)(2,1)}, bf16[16,6144]{1,0:T(8,128)(2,1)S(1)}, u32[]{:S(2)}, u32[]{:S(2)}) collective-permute-start(bf16[16,6144]{1,0:T(8,128)(2,1)} %refs_4_.4), channel_id=1, source_target_pairs={{0,4},{1,5},{2,6},{3,7},{4,0},{5,1},{6,2},{7,3},{8,12},{9,13},{10,... | collective-permute-start | bytes 589832 | tf_op jit(solution)/shard_map/ppermute | solution.py:79
  9.8 8.3 %copy-start.1 = (bf16[16,6144]{1,0:T(8,128)(2,1)S(1)}, bf16[16,6144]{1,0:T(8,128)(2,1)}, u32[]{:S(2)}) copy-start(bf16[16,6144]{1,0:T(8,128)(2,1)} %refs_4_.4) | copy-start | bytes 589828
  17.9 1.8 %collective-permute-start.3 = (bf16[64,3072]{1,0:T(8,128)(2,1)S(1)}, bf16[64,3072]{1,0:T(8,128)(2,1)S(1)}, u32[]{:S(2)}, u32[]{:S(2)}) collective-permute-start(bf16[64,3072]{1,0:T(8,128)(2,1)S(1)} %get-tuple-element.34.refs_3_), channel_id=1, source_target_pairs={{0,1},{1,0},{2,3},{3,2},{4,5},{5,4},{6,7},{7,6},{8,9},{9,8},{10,11... | collective-permute-start | bytes 1179656 | tf_op jit(solution)/shard_map/ppermute | solution.py:83
  19.8 8.2 %copy-start.2 = (bf16[32,1536]{1,0:T(8,128)(2,1)S(1)}, bf16[32,1536]{1,0:T(8,128)(2,1)}, u32[]{:S(2)}) copy-start(bf16[32,1536]{1,0:T(8,128)(2,1)} %refs_0_.3) | copy-start | bytes 294916
  19.8 8.2 %collective-permute-start.6 = (bf16[32,3072]{1,0:T(8,128)(2,1)S(1)}, bf16[32,3072]{1,0:T(8,128)(2,1)S(1)}, u32[]{:S(2)}, u32[]{:S(2)}) collective-permute-start(bf16[32,3072]{1,0:T(8,128)(2,1)S(1)} %get-tuple-element.36.refs_2_), channel_id=1, source_target_pairs={{0,2},{1,3},{2,0},{3,1},{4,6},{5,7},{6,4},{7,5},{8,10},{9,11},{10,... | collective-permute-start | bytes 589832 | tf_op jit(solution)/shard_map/ppermute | solution.py:79
  27.9 1.8 %collective-permute-start.7 = (bf16[64,3072]{1,0:T(8,128)(2,1)S(1)}, bf16[64,3072]{1,0:T(8,128)(2,1)S(1)}, u32[]{:S(2)}, u32[]{:S(2)}) collective-permute-start(bf16[64,3072]{1,0:T(8,128)(2,1)S(1)} %get-tuple-element.39.refs_1_), channel_id=1, source_target_pairs={{0,1},{1,0},{2,3},{3,2},{4,5},{5,4},{6,7},{7,6},{8,9},{9,8},{10,11... | collective-permute-start | bytes 1179656 | tf_op jit(solution)/shard_map/ppermute | solution.py:83
  29.8 9.9 %collective-permute-start.9 = (bf16[32,3072]{1,0:T(8,128)(2,1)S(1)}, bf16[32,3072]{1,0:T(8,128)(2,1)S(1)}, u32[]{:S(2)}, u32[]{:S(2)}) collective-permute-start(bf16[32,3072]{1,0:T(8,128)(2,1)S(1)} %get-tuple-element.43), channel_id=1, source_target_pairs={{0,2},{1,3},{2,0},{3,1},{4,6},{5,7},{6,4},{7,5},{8,10},{9,11},{10,... | collective-permute-start | bytes 589832 | tf_op jit(solution)/shard_map/ppermute | solution.py:79
  30.3 7.4 %collective-permute-start.8 = (bf16[16,3072]{1,0:T(8,128)(2,1)S(1)}, bf16[16,3072]{1,0:T(8,128)(2,1)S(1)}, u32[]{:S(2)}, u32[]{:S(2)}) collective-permute-start(bf16[16,3072]{1,0:T(8,128)(2,1)S(1)} %get-tuple-element.41), channel_id=1, source_target_pairs={{0,4},{1,5},{2,6},{3,7},{4,0},{5,1},{6,2},{7,3},{8,12},{9,13},{10,... | collective-permute-start | bytes 294920 | tf_op jit(solution)/shard_map/ppermute | solution.py:79
  32.9 12.1 %collective-permute-start.12 = (bf16[16,6144]{1,0:T(8,128)(2,1)S(1)}, bf16[16,6144]{1,0:T(8,128)(2,1)S(1)}, u32[]{:S(2)}, u32[]{:S(2)}) collective-permute-start(bf16[16,6144]{1,0:T(8,128)(2,1)S(1)} %collective-permute-done.4.refs_1_), channel_id=1, source_target_pairs={{0,2},{1,3},{2,0},{3,1},{4,6},{5,7},{6,4},{7,5},{8,10},{9,11},{10,... | collective-permute-start | bytes 589832 | tf_op jit(solution)/shard_map/ppermute | solution.py:79
  34.5 8.1 %collective-permute-start.15 = (bf16[32,1536]{1,0:T(8,128)(2,1)S(1)}, bf16[32,1536]{1,0:T(8,128)(2,1)S(1)}, u32[]{:S(2)}, u32[]{:S(2)}) collective-permute-start(bf16[32,1536]{1,0:T(8,128)(2,1)S(1)} %stack.27.refs_4_.p0), channel_id=1, source_target_pairs={{0,24},{8,16},{16,8},{24,0},{1,25},{9,17},{17,9},{25,1},{2,26},{10... | collective-permute-start | bytes 294920 | tf_op jit(solution)/shard_map/ppermute | solution.py:75
  36.2 6.7 %collective-permute-start.14 = (bf16[32,1536]{1,0:T(8,128)(2,1)S(1)}, bf16[32,1536]{1,0:T(8,128)(2,1)S(1)}, u32[]{:S(2)}, u32[]{:S(2)}) collective-permute-start(bf16[32,1536]{1,0:T(8,128)(2,1)S(1)} %stack.27.refs_4_.p0), channel_id=1, source_target_pairs={{0,16},{8,24},{16,0},{24,8},{1,17},{9,25},{17,1},{25,9},{2,18},{10... | collective-permute-start | bytes 294920 | tf_op jit(solution)/shard_map/ppermute | solution.py:75
  37.7 5.2 %collective-permute-start.13 = (bf16[32,1536]{1,0:T(8,128)(2,1)S(1)}, bf16[32,1536]{1,0:T(8,128)(2,1)S(1)}, u32[]{:S(2)}, u32[]{:S(2)}) collective-permute-start(bf16[32,1536]{1,0:T(8,128)(2,1)S(1)} %stack.27.refs_4_.p0), channel_id=1, source_target_pairs={{0,8},{8,0},{16,24},{24,16},{1,9},{9,1},{17,25},{25,17},{2,10},{10... | collective-permute-start | bytes 294920 | tf_op jit(solution)/shard_map/ppermute | solution.py:75
  39.9 10.5 %collective-permute-start.11 = (bf16[16,3072]{1,0:T(8,128)(2,1)S(1)}, bf16[16,3072]{1,0:T(8,128)(2,1)S(1)}, u32[]{:S(2)}, u32[]{:S(2)}) collective-permute-start(bf16[16,3072]{1,0:T(8,128)(2,1)S(1)} %get-tuple-element.46), channel_id=1, source_target_pairs={{0,4},{1,5},{2,6},{3,7},{4,0},{5,1},{6,2},{7,3},{8,12},{9,13},{10,... | collective-permute-start | bytes 294920 | tf_op jit(solution)/shard_map/ppermute | solution.py:79
  42.6 8.8 %collective-permute-start.10 = (bf16[16,3072]{1,0:T(8,128)(2,1)S(1)}, bf16[16,3072]{1,0:T(8,128)(2,1)S(1)}, u32[]{:S(2)}, u32[]{:S(2)}) collective-permute-start(bf16[16,3072]{1,0:T(8,128)(2,1)S(1)} %get-tuple-element.44.rest_0_.refs_0_), channel_id=1, source_target_pairs={{0,4},{1,5},{2,6},{3,7},{4,0},{5,1},{6,2},{7,3},{8,12},{9,13},{10,... | collective-permute-start | bytes 294920 | tf_op jit(solution)/shard_map/ppermute | solution.py:79
  51.4 11.3 %slice-start = ((s8[18874368]{0:T(1024)(128)(4,1)}), s8[4194304]{0:T(1024)(128)(4,1)S(1)}, s32[]{:S(2)}) async-start(s8[18874368]{0:T(1024)(128)(4,1)} %bitcast.5), calls=%async_computation | async-start | bytes 8388608
  51.4 11.3 %slice-start.1 = ((s8[18874368]{0:T(1024)(128)(4,1)}), s8[4194304]{0:T(1024)(128)(4,1)S(1)}, s32[]{:S(2)}) async-start(s8[18874368]{0:T(1024)(128)(4,1)} %bitcast.5), calls=%async_computation.1 | async-start | bytes 8388608
  51.4 11.3 %slice-start.2 = ((s8[18874368]{0:T(1024)(128)(4,1)}), s8[4194304]{0:T(1024)(128)(4,1)S(1)}, s32[]{:S(2)}) async-start(s8[18874368]{0:T(1024)(128)(4,1)} %bitcast.5), calls=%async_computation.2 | async-start | bytes 8388608
  51.6 3.1 %collective-permute-start.18 = (bf16[64,6144]{1,0:T(8,128)(2,1)S(1)}, bf16[64,6144]{1,0:T(8,128)(2,1)S(1)}, u32[]{:S(2)}, u32[]{:S(2)}) collective-permute-start(bf16[64,6144]{1,0:T(8,128)(2,1)S(1)} %get-tuple-element.49.refs_0_), channel_id=1, source_target_pairs={{0,1},{1,0},{2,3},{3,2},{4,5},{5,4},{6,7},{7,6},{8,9},{9,8},{10,11... | collective-permute-start | bytes 2359304 | tf_op jit(solution)/shard_map/ppermute | solution.py:83
  51.7 10.9 %collective-permute-start.20 = (bf16[32,3072]{1,0:T(8,128)(2,1)S(1)}, bf16[32,3072]{1,0:T(8,128)(2,1)S(1)}, u32[]{:S(2)}, u32[]{:S(2)}) collective-permute-start(bf16[32,3072]{1,0:T(8,128)(2,1)S(1)} %get-tuple-element.47.refs_3_.refs_0_), channel_id=1, source_target_pairs={{0,1},{1,0},{2,3},{3,2},{4,5},{5,4},{6,7},{7,6},{8,9},{9,8},{10,11... | collective-permute-start | bytes 589832 | tf_op jit(solution)/shard_map/ppermute | solution.py:83
  52.2 9.0 %collective-permute-start.16 = (bf16[32,3072]{1,0:T(8,128)(2,1)S(1)}, bf16[32,3072]{1,0:T(8,128)(2,1)S(1)}, u32[]{:S(2)}, u32[]{:S(2)}) collective-permute-start(bf16[32,3072]{1,0:T(8,128)(2,1)S(1)} %get-tuple-element.47.refs_3_.refs_0_), channel_id=1, source_target_pairs={{0,2},{1,3},{2,0},{3,1},{4,6},{5,7},{6,4},{7,5},{8,10},{9,11},{10,... | collective-permute-start | bytes 589832 | tf_op jit(solution)/shard_map/ppermute | solution.py:79
  52.2 7.7 %collective-permute-start.17 = (bf16[16,3072]{1,0:T(8,128)(2,1)S(1)}, bf16[16,3072]{1,0:T(8,128)(2,1)S(1)}, u32[]{:S(2)}, u32[]{:S(2)}) collective-permute-start(bf16[16,3072]{1,0:T(8,128)(2,1)S(1)} %get-tuple-element.48.refs_1_), channel_id=1, source_target_pairs={{0,4},{1,5},{2,6},{3,7},{4,0},{5,1},{6,2},{7,3},{8,12},{9,13},{10,... | collective-permute-start | bytes 294920 | tf_op jit(solution)/shard_map/ppermute | solution.py:79
  61.2 1.5 %collective-permute-start.21 = (bf16[32,3072]{1,0:T(8,128)(2,1)S(1)}, bf16[32,3072]{1,0:T(8,128)(2,1)S(1)}, u32[]{:S(2)}, u32[]{:S(2)}) collective-permute-start(bf16[32,3072]{1,0:T(8,128)(2,1)S(1)} %get-tuple-element.53.refs_1_), channel_id=1, source_target_pairs={{0,1},{1,0},{2,3},{3,2},{4,5},{5,4},{6,7},{7,6},{8,9},{9,8},{10,11... | collective-permute-start | bytes 589832 | tf_op jit(solution)/shard_map/ppermute | solution.py:83
  61.3 8.0 %collective-permute-start.22 = (bf16[32,3072]{1,0:T(8,128)(2,1)S(1)}, bf16[32,3072]{1,0:T(8,128)(2,1)S(1)}, u32[]{:S(2)}, u32[]{:S(2)}) collective-permute-start(bf16[32,3072]{1,0:T(8,128)(2,1)S(1)} %get-tuple-element.52.refs_6_.refs_1_), channel_id=1, source_target_pairs={{0,1},{1,0},{2,3},{3,2},{4,5},{5,4},{6,7},{7,6},{8,9},{9,8},{10,11... | collective-permute-start | bytes 589832 | tf_op jit(solution)/shard_map/ppermute | solution.py:83
  61.8 7.3 %collective-permute-start.19 = (bf16[32,3072]{1,0:T(8,128)(2,1)S(1)}, bf16[32,3072]{1,0:T(8,128)(2,1)S(1)}, u32[]{:S(2)}, u32[]{:S(2)}) collective-permute-start(bf16[32,3072]{1,0:T(8,128)(2,1)S(1)} %get-tuple-element.52.refs_6_.refs_1_), channel_id=1, source_target_pairs={{0,2},{1,3},{2,0},{3,1},{4,6},{5,7},{6,4},{7,5},{8,10},{9,11},{10,... | collective-permute-start | bytes 589832 | tf_op jit(solution)/shard_map/ppermute | solution.py:79
  69.1 1.4 %collective-permute-start.23 = (bf16[32,3072]{1,0:T(8,128)(2,1)S(1)}, bf16[32,3072]{1,0:T(8,128)(2,1)S(1)}, u32[]{:S(2)}, u32[]{:S(2)}) collective-permute-start(bf16[32,3072]{1,0:T(8,128)(2,1)S(1)} %tie.1.refs_2_), channel_id=1, source_target_pairs={{0,1},{1,0},{2,3},{3,2},{4,5},{5,4},{6,7},{7,6},{8,9},{9,8},{10,11... | collective-permute-start | bytes 589832 | tf_op jit(solution)/shard_map/ppermute | solution.py:83
  77.4 8.2 %collective-permute-start.24 = (bf16[32,1536]{1,0:T(8,128)(2,1)S(1)}, bf16[32,1536]{1,0:T(8,128)(2,1)S(1)}, u32[]{:S(2)}, u32[]{:S(2)}) collective-permute-start(bf16[32,1536]{1,0:T(8,128)(2,1)S(1)} %get-tuple-element.57), channel_id=1, source_target_pairs={{0,8},{8,0},{16,24},{24,16},{1,9},{9,1},{17,25},{25,17},{2,10},{10... | collective-permute-start | bytes 294920 | tf_op jit(solution)/shard_map/ppermute | solution.py:75
  78.3 7.3 %collective-permute-start.25 = (bf16[32,1536]{1,0:T(8,128)(2,1)S(1)}, bf16[32,1536]{1,0:T(8,128)(2,1)S(1)}, u32[]{:S(2)}, u32[]{:S(2)}) collective-permute-start(bf16[32,1536]{1,0:T(8,128)(2,1)S(1)} %get-tuple-element.58), channel_id=1, source_target_pairs={{0,16},{8,24},{16,0},{24,8},{1,17},{9,25},{17,1},{25,9},{2,18},{10... | collective-permute-start | bytes 294920 | tf_op jit(solution)/shard_map/ppermute | solution.py:75
  79.5 6.2 %collective-permute-start.26 = (bf16[32,1536]{1,0:T(8,128)(2,1)S(1)}, bf16[32,1536]{1,0:T(8,128)(2,1)S(1)}, u32[]{:S(2)}, u32[]{:S(2)}) collective-permute-start(bf16[32,1536]{1,0:T(8,128)(2,1)S(1)} %get-tuple-element.59), channel_id=1, source_target_pairs={{0,24},{8,16},{16,8},{24,0},{1,25},{9,17},{17,9},{25,1},{2,26},{10... | collective-permute-start | bytes 294920 | tf_op jit(solution)/shard_map/ppermute | solution.py:75
  (3 other events, 17.2 us)

commit v2 on v1

--- a/solution.py
+++ b/solution.py
@@ -11,7 +11,6 @@
 cubic_term = 0.044715
 VMEM_LIMIT = 16 * 1024 * 1024
 CHUNKS = 2
-AHEAD = 4
 FLOPS = 8_000_000_000
 
 
@@ -122,7 +121,9 @@
     width = w_out.shape[1]
     tokens = 4 * x[0].shape[0] if join else x[0].shape[1]
     half = tokens // 2
-    cut = cuts(units)
+    bounds = [units * n // 12 for n in (0, 3, 6, 8, 10, 11, 12)]
+    cut = [slice(a, b) for a, b in zip(bounds[:-1], bounds[1:])]
+    groups = [cut[n : n + 2] for n in (0, 2, 4)]
     pieces = len(x)
 
     def body(*refs):
@@ -137,7 +138,7 @@
             )
             for n, c in enumerate(cut)
         ]
-        for copy in copies[:AHEAD]:
+        for copy in copies[:2]:
             copy.start()
         if join:
             joined, flipped = rest[:2]
@@ -145,13 +146,16 @@
             flipped[...] = joined[...].T
         else:
             flipped = x_refs[0]
-        for n, c in enumerate(cut):
-            copies[n].wait()
-            if n + AHEAD < len(cut):
-                copies[n + AHEAD].start()
-            value = jnp.dot(held[c, :], flipped[...], preferred_element_type=jnp.float32).T
-            own[:, c] = value[:half]
-            other[:, c] = value[half:].astype(jnp.bfloat16)
+        for n, group in enumerate(groups):
+            for copy in copies[2 * n : 2 * n + 2]:
+                copy.wait()
+            for copy in copies[2 * n + 2 : 2 * n + 4]:
+                copy.start()
+            for c in cuts(group[1].stop - group[0].start, 512):
+                c = slice(group[0].start + c.start, group[0].start + c.stop)
+                value = jnp.dot(held[c, :], flipped[...], preferred_element_type=jnp.float32).T
+                own[:, c] = value[:half]
+                other[:, c] = value[half:].astype(jnp.bfloat16)
 
     shapes = [
         jax.ShapeDtypeStruct((half, units), jnp.float32),
@@ -260,25 +264,18 @@
     )
 
 
-def pair_far(grad0, far0, mine1, far1, pre_act, pre_most, pre_last, after=()):
+def pair_far(grad0, far0, mine1, far1, pre_act, after=()):
     rows, units = grad0.shape
-    most, wide = pre_most.shape
-
-    def body(grad0, far0, mine1, far1, pre_ref, pre_most, pre_last, pair0, grad1, pre_own):
+
+    def body(grad0, far0, mine1, far1, pre_ref, pair0, grad1):
         pair0[:rows] = grad0[...]
         pair0[rows:] = far0[...]
         grad1[...] = slope_times(add(mine1, far1), pre_ref, 1)
-        pre_own[:most] = pre_most[...]
-        pre_own[most:] = pre_last[...]
 
     return small(
         body,
-        [grad0, far0, mine1, far1, pre_act, pre_most, pre_last],
-        [
-            ((2 * rows, units), jnp.bfloat16),
-            ((rows, units), jnp.bfloat16),
-            ((most + rows, wide), jnp.bfloat16),
-        ],
+        [grad0, far0, mine1, far1, pre_act],
+        [((2 * rows, units), jnp.bfloat16), ((rows, units), jnp.bfloat16)],
         after,
         name="pair_far",
     )
@@ -302,37 +299,42 @@
     )
 
 
-def out_weight_grad(pre, x, first, rows, held, after=()):
+def weight_grad(pieces, x, first, start, rows, units, held, activate, after=()):
     tokens, width = x.shape
-    units = pre[0].shape[1]
-    pieces = len(pre)
+    count = len(pieces)
     extra = len(after) + (held is not None)
-    parts = cuts(rows)
+    parts = cuts(rows, 512)
 
     def body(*refs):
-        pre_refs, x_ref = refs[:pieces], refs[pieces]
-        out, token, stage, sems = refs[pieces + 1 + extra :]
+        a_refs, x_ref = refs[:count], refs[count]
+        out, token, stage, sems = refs[count + 1 + extra :]
         copies = []
         for n, part in enumerate(parts):
-            some = slice(first + part.start, first + part.stop)
-            value = jnp.concatenate([ref[:, some] for ref in pre_refs], axis=0)
-            value = value.astype(jnp.float32)
-            tangent = jnp.tanh(tanh_scale * (value + cubic_term * value * value * value))
-            hidden = (0.5 * value * (1.0 + tangent)).astype(jnp.bfloat16).T
-            for cut in cuts(width):
-                stage[part, cut] = jnp.dot(
-                    hidden, x_ref[:, cut], preferred_element_type=jnp.float32
-                ).astype(jnp.bfloat16)
-            copies.append(pltpu.make_async_copy(stage.at[part], out.at[some], sems.at[n]))
+            for here in cuts(part.stop - part.start):
+                low = start + part.start + here.start
+                high = start + part.start + here.stop
+                a = jnp.concatenate([ref[:, low:high] for ref in a_refs], axis=0)
+                if activate:
+                    value = a.astype(jnp.float32)
+                    cube = cubic_term * value * value * value
+                    tangent = jnp.tanh(tanh_scale * (value + cube))
+                    a = (0.5 * value * (1.0 + tangent)).astype(jnp.bfloat16)
+                a = a.T
+                for cut in cuts(width):
+                    stage[low - start : high - start, cut] = jnp.dot(
+                        a, x_ref[:, cut], preferred_element_type=jnp.float32
+                    ).astype(jnp.bfloat16)
+            there = pl.ds(first + start + part.start, part.stop - part.start)
+            copies.append(pltpu.make_async_copy(stage.at[part], out.at[there], sems.at[n]))
             copies[-1].start()
         token[...] = jnp.zeros_like(token)
         for copy in copies:
             copy.wait()
 
-    operands = [*pre, x] + ([] if held is None else [held]) + list(after)
-    return pl.pallas_call(
-        body,
-        in_specs=[VMEM] * (pieces + 1) + [ANY] * extra,
+    operands = [*pieces, x] + ([] if held is None else [held]) + list(after)
+    return pl.pallas_call(
+        body,
+        in_specs=[VMEM] * (count + 1) + [ANY] * extra,
         out_specs=[ANY, VMEM],
         out_shape=[
             jax.ShapeDtypeStruct((units, width), jnp.bfloat16),
@@ -342,94 +344,61 @@
             pltpu.VMEM((rows, width), jnp.bfloat16),
             pltpu.SemaphoreType.DMA((len(parts),)),
         ],
-        input_output_aliases={} if held is None else {pieces + 1: 0},
+        input_output_aliases={} if held is None else {count + 1: 0},
         compiler_params=params(),
         cost_estimate=COST,
-        name="out_weight_grad",
+        name="out_weight_grad" if activate else "in_weight_grad",
     )(*operands)
 
 
-def in_grads(grad_pre, w_in, tok, first, count, rows, held, total, place, after=()):
-    tokens, width = tok.shape
+def token_grad(pieces, w_in, first, total, place, after=()):
+    count = len(pieces)
+    tokens, units = count * pieces[0].shape[0], pieces[0].shape[1]
+    width = w_in.shape[1]
     block = tokens // 8
-    pieces = len(grad_pre)
-    start, last = total is None, place is not None
+    last, more = place is not None, total is not None
 
     def body(*refs):
         refs = list(refs)
         place_ref = refs.pop(0) if last else None
-        w_ref, tok_ref = refs[pieces : pieces + 2]
+        w_ref = refs[count]
+        outs = refs[count + 1 + more + len(after) :]
+        sums = outs[-1]
+        value = jnp.concatenate([ref[...] for ref in refs[:count]], axis=0)
+        for n, some in enumerate(cuts(units, 1024)):
+            part = jnp.dot(
+                value[:, some],
+                w_ref[first + some.start : first + some.stop, :],
+                preferred_element_type=jnp.float32,
+            )
+            if n > 0:
+                sums[...] += part
+            else:
+                sums[...] = part + refs[count + 1][...] if more else part
         if last:
-            out, parts, sums = refs[-6], refs[-5:-1], refs[-1]
-        else:
-            out, sums = refs[-2:]
-        value = jnp.concatenate([ref[...] for ref in refs[:pieces]], axis=0)
-
-        @pl.when(pl.program_id(0) == 0)
-        def _():
-            sums[...] = jnp.zeros_like(sums) if start else refs[pieces + 3][...]
-
-        here = pl.multiple_of((first + pl.program_id(0)) * rows, rows)
-        sums[...] += jnp.dot(
-            value, w_ref[pl.ds(here, rows), :], preferred_element_type=jnp.float32
-        )
-        for some in cuts(rows):
-            flipped = value[:, some].T
-            for cut in cuts(width):
-                out[some, cut] = jnp.dot(
-                    flipped, tok_ref[:, cut], preferred_element_type=jnp.float32
-                ).astype(jnp.bfloat16)
-
-        if last:
-
-            @pl.when(pl.program_id(0) == count - 1)
-            def _():
-                core = place_ref[4]
-                for d, part in enumerate(parts):
-                    low = pl.multiple_of((place_ref[d] + 4 * core) * block, block)
-                    high = pl.multiple_of((place_ref[d] + 4 * (1 - core)) * block, block)
-                    part[:block] = sums[pl.ds(low, block), :].astype(part.dtype)
-                    part[block:] = sums[pl.ds(high, block), :].astype(part.dtype)
-
-    whole = pl.BlockSpec((tokens, width), lambda i: (0, 0))
-    in_specs = [pl.BlockSpec((p.shape[0], rows), lambda i: (0, i)) for p in grad_pre]
-    in_specs += [
-        VMEM,
-        whole,
-    ]
-    operands = [*grad_pre, w_in, tok]
-    if not start:
-        in_specs += [ANY, whole]
-        operands += [held, total]
-    in_specs += [ANY] * len(after)
-    operands += after
-    out_specs = [pl.BlockSpec((rows, width), lambda i: (first + i, 0))]
-    out_shape = [jax.ShapeDtypeStruct(w_in.shape, jnp.bfloat16)]
-    scratch = []
+            core = place_ref[4]
+            for d, part in enumerate(outs[:4]):
+                low = pl.multiple_of((place_ref[d] + 4 * core) * block, block)
+                high = pl.multiple_of((place_ref[d] + 4 * (1 - core)) * block, block)
+                part[:block] = sums[pl.ds(low, block), :].astype(part.dtype)
+                part[block:] = sums[pl.ds(high, block), :].astype(part.dtype)
+
+    shapes = [jax.ShapeDtypeStruct((tokens, width), jnp.float32)]
     if last:
-        in_specs = [SMEM] + in_specs
-        operands = [place] + operands
-        out_specs += [pl.BlockSpec((2 * block, width), lambda i: (0, 0))] * 4
-        out_shape += [
+        shapes = [
             jax.ShapeDtypeStruct((2 * block, width), kind)
             for kind in (jnp.float32, jnp.bfloat16, jnp.bfloat16, jnp.bfloat16)
         ]
-        scratch = [pltpu.VMEM((tokens, width), jnp.float32)]
-    else:
-        out_specs.append(whole)
-        out_shape.append(jax.ShapeDtypeStruct((tokens, width), jnp.float32))
-    return pl.pallas_call(
-        body,
-        grid=(count,),
-        in_specs=in_specs,
-        out_specs=out_specs,
-        out_shape=out_shape,
-        scratch_shapes=scratch,
-        input_output_aliases={} if start else {pieces + 2 + last: 0},
+    return pl.pallas_call(
+        body,
+        in_specs=[SMEM] * last + [VMEM] * (count + 1 + more) + [ANY] * len(after),
+        out_specs=[VMEM] * len(shapes),
+        out_shape=shapes,
+        scratch_shapes=[pltpu.VMEM((tokens, width), jnp.float32)] if last else [],
         compiler_params=params(),
         cost_estimate=COST,
-        name="in_grads",
-    )(*operands)
+        name="token_grad",
+    )(*([place] if last else []), *pieces, w_in, *([total] if more else []), *after)
 
 
 def mark(after=(), cost=SHORT):
@@ -491,9 +460,7 @@
     place = jnp.stack(spots + [core]).astype(jnp.int32)
 
     units = w_out.shape[0]
-    rows = 512
     per_chunk = units // CHUNKS
-    count = per_chunk // rows
 
     started = mark()
     for _ in range(7):
@@ -516,33 +483,28 @@
     mine0, out0, held1, out1 = sum_near(
         held0, swap_chips(out0, 1), own1, swap_cores(send1), (mine,)
     )
+    pre_own = stack([pre_act, pre_far, pre_near, swap_chips(pre_far, 1)], (out1,))
+    pre = [pre_own, swap_cores(pre_own)]
     grad0, mine1, out1 = sum_far(
-        mine0, swap_chips(out0, 2), held1, swap_chips(out1, 1), pre_act
+        mine0, swap_chips(out0, 2), held1, swap_chips(out1, 1), pre_act, (pre_own,)
     )
     tok = join_rows([mine] + [swap_rows(mine, d) for d in (1, 2, 3)], place, (grad0,))
-    pair0, grad1, pre_own = pair_far(
-        grad0,
-        swap_chips(grad0, 2),
-        mine1,
-        swap_chips(out1, 2),
-        pre_act,
-        pre_most,
-        swap_chips(pre_far, 1),
-        (tok,),
-    )
-    pre = [pre_own, swap_cores(pre_own)]
-    grad_w_out, token = out_weight_grad(pre, x, 0, units // 2, None, (pair0,))
+    half = units // 2
+    grad_w_out, token = weight_grad(pre, x, 0, 0, half, units, None, True, (tok,))
+    pair0, grad1 = pair_far(
+        grad0, swap_chips(grad0, 2), mine1, swap_chips(out1, 2), pre_act, (token,)
+    )
+    grad_w_out, token = weight_grad(pre, x, 0, half, half, units, grad_w_out, True, (pair0,))
     near0, pair1 = pair_near(swap_chips(pair0, 1), grad1, swap_chips(grad1, 2), (token,))
     whole = [pair0, near0, swap_cores(pair0), swap_cores(near0)]
-    grad_w_in, total = in_grads(
-        whole, w_in, tok, 0, count // 2, 2 * rows, None, None, None, (pair1,)
-    )
-    near1 = tie(swap_chips(pair1, 1), (total,))
+    grad_w_in, token = weight_grad(whole, tok, 0, 0, per_chunk, units, None, False, (pair1,))
+    near1 = tie(swap_chips(pair1, 1), (token,))
+    (total,) = token_grad(whole, w_in, 0, None, None, (near1,))
     whole = [pair1, near1, swap_cores(pair1), swap_cores(near1)]
-    grad_w_in, part, *parts = in_grads(
-        whole, w_in, tok, count // 2, count // 2, 2 * rows, grad_w_in, total, place
-    )
-    grad_w_out, _ = out_weight_grad(pre, x, units // 2, units // 2, grad_w_out, (part,))
+    part, *parts = token_grad(whole, w_in, per_chunk, total, place)
+    grad_w_in, _ = weight_grad(
+        whole, tok, per_chunk, 0, per_chunk, units, grad_w_in, False, (part,)
+    )
     for d in (1, 2, 3):
         part = part + swap_rows(parts[d - 1], d).astype(jnp.float32)
     return (part.astype(jnp.bfloat16), grad_w_in, grad_w_out)

time: 86.5 us -> 82.4 us (0.953)
  starting transfers between devices: 30.3 us -> 27.8 us
  waiting for transfers between devices: 16.5 us -> 15.1 us
    ppermute x7, waiting for transfers between devices: 4.68 us -> 1.3 us  [swap_cores(): return lax.ppermute(array, 'col', [(i, i ^ 1) for i in range(8)])]
    ppermute x11, waiting for transfers between devices: 10.9 us -> 12.9 us  [swap_chips(): return lax.ppermute(array, 'col', [(i, i ^ 2 * d) for i in range(8)])]
    ppermute x11, starting transfers between devices: 17.2 us -> 16 us  [swap_chips(): return lax.ppermute(array, 'col', [(i, i ^ 2 * d) for i in range(8)])]
    pallas_call x4 -> x6, Pallas kernels: 23.1 us -> 22.2 us  [the longest x4 18.8 us: weight_grad(): pl.pallas_call(body, in_specs=[VMEM] * (count + 1) + [ANY] * extra, out_s...]
  transfers between devices with their start and end apart: 27 -> 27, of which waited for: 12 -> 11; matrix products, arithmetic and copies ran while one was open for 0% -> 0% of each run, Pallas kernels for 35% -> 43%
where the time goes in v2:
time: 82.4 us; the launch traced here: 82.2 us
  Pallas kernels  37.4 us (45%)
  starting transfers between devices  27.8 us (34%)
  waiting for transfers between devices  15.1 us (18%)
  between operations  1.08 us (1%)
    pallas_call x4, Pallas kernels, weight_grad(): pl.pallas_call(body, in_specs=[VMEM] * (count + 1) + [ANY] * extra, out_s...  18.8 us
    ppermute x11, starting transfers between devices, swap_chips(): return lax.ppermute(array, 'col', [(i, i ^ 2 * d) for i in range(8)])  16 us
    pallas_call x2, Pallas kernels, hidden_grad(): pl.pallas_call(body, in_specs=[SMEM] * join + [VMEM] * pieces + [ANY] * (...  14 us
    ppermute x11, waiting for transfers between devices, swap_chips(): return lax.ppermute(array, 'col', [(i, i ^ 2 * d) for i in range(8)])  12.9 us
    ppermute x9, starting transfers between devices, swap_rows(): return lax.ppermute(array, 'row', [(r, r ^ d) for r in range(4)])  11.2 us
    pallas_call x2, Pallas kernels, token_grad(): pl.pallas_call(body, in_specs=[SMEM] * last + [VMEM] * (count + 1 + more)...  3.37 us
  transfers between devices with their start and end apart: 27, of which 11 were waited for; matrix products, arithmetic and copies ran while one was open for 0% of the time, Pallas kernels for 43%

profile of v2, /device:TPU:0, one launch (start us, length us, event | category | flops | bytes accessed | tf_op | source)
XLA Modules:
  0.0 82.2 jit_solution(3899870370401145852)
XLA Ops:
  0.6 3.0 %collective-permute-start = (bf16[32,1536]{1,0:T(8,128)(2,1)}, bf16[32,1536]{1,0:T(8,128)(2,1)S(1)}, u32[]{:S(2)}, u32[]{:S(2)}) collective-permute-start(bf16[32,1536]{1,0:T(8,128)(2,1)} %refs_1_.2), channel_id=1, source_target_pairs={{0,8},{8,0},{16,24},{24,16},{1,9},{9,1},{17,25},{25,17},{2,10},{10... | collective-permute-start | bytes 294920 | tf_op jit(solution)/shard_map/ppermute | solution.py:74
  3.6 1.5 %collective-permute-start.1 = (bf16[32,1536]{1,0:T(8,128)(2,1)}, bf16[32,1536]{1,0:T(8,128)(2,1)S(1)}, u32[]{:S(2)}, u32[]{:S(2)}) collective-permute-start(bf16[32,1536]{1,0:T(8,128)(2,1)} %refs_1_.2), channel_id=1, source_target_pairs={{0,16},{8,24},{16,0},{24,8},{1,17},{9,25},{17,1},{25,9},{2,18},{10... | collective-permute-start | bytes 294920 | tf_op jit(solution)/shard_map/ppermute | solution.py:74
  5.2 3.0 %collective-permute-start.4 = (bf16[16,6144]{1,0:T(8,128)(2,1)}, bf16[16,6144]{1,0:T(8,128)(2,1)S(1)}, u32[]{:S(2)}, u32[]{:S(2)}) collective-permute-start(bf16[16,6144]{1,0:T(8,128)(2,1)} %refs_4_.4), channel_id=1, source_target_pairs={{0,4},{1,5},{2,6},{3,7},{4,0},{5,1},{6,2},{7,3},{8,12},{9,13},{10,... | collective-permute-start | bytes 589832 | tf_op jit(solution)/shard_map/ppermute | solution.py:78
  8.2 1.6 %collective-permute-start.5 = (bf16[16,6144]{1,0:T(8,128)(2,1)}, bf16[16,6144]{1,0:T(8,128)(2,1)S(1)}, u32[]{:S(2)}, u32[]{:S(2)}) collective-permute-start(bf16[16,6144]{1,0:T(8,128)(2,1)} %refs_4_.4), channel_id=1, source_target_pairs={{0,2},{1,3},{2,0},{3,1},{4,6},{5,7},{6,4},{7,5},{8,10},{9,11},{10,... | collective-permute-start | bytes 589832 | tf_op jit(solution)/shard_map/ppermute | solution.py:78
  10.0 0.9 %collective-permute-done.2.refs_4_ = bf16[32,1536]{1,0:T(8,128)(2,1)S(1)} collective-permute-done((bf16[32,1536]{1,0:T(8,128)(2,1)}, bf16[32,1536]{1,0:T(8,128)(2,1)S(1)}, u32[]{:S(2)}, u32[]{:S(2)}) %collective-permute-start.2) | collective-permute-done | bytes 98336 | tf_op jit(solution)/shard_map/ppermute | solution.py:74
  10.9 7.3 %hidden_grad.2 = (f32[64,3072]{1,0:T(8,128)S(1)}, bf16[64,3072]{1,0:T(8,128)(2,1)S(1)}, bf16[128,1536]{1,0:T(8,128)(2,1)S(1)}, bf16[1536,128]{1,0:T(8,128)(2,1)S(1)}) custom-call(s32[5]{0:T(128)S(1)} %stack.26.refs_0_.place_ref, bf16[32,1536]{1,0:T(8,128)(2,1)S(1)} %copy-done, bf16[32,1536]{1,0:T(8,128)(2,1)S(1)} %collective-permute-done.refs_2_, ...), custom_call_target="tpu_custom_call" | custom-call | flops 80000000 | tf_op jit(solution)/shard_map/hidden_grad/pallas_call | solution.py:169
  18.2 1.6 %collective-permute-start.10 = (bf16[16,6144]{1,0:T(8,128)(2,1)S(1)}, bf16[16,6144]{1,0:T(8,128)(2,1)S(1)}, u32[]{:S(2)}, u32[]{:S(2)}) collective-permute-start(bf16[16,6144]{1,0:T(8,128)(2,1)S(1)} %collective-permute-done.4.refs_1_), channel_id=1, source_target_pairs={{0,2},{1,3},{2,0},{3,1},{4,6},{5,7},{6,4},{7,5},{8,10},{9,11},{10,... | collective-permute-start | bytes 589832 | tf_op jit(solution)/shard_map/ppermute | solution.py:78
  20.1 1.6 %collective-permute-start.6 = (bf16[32,3072]{1,0:T(8,128)(2,1)S(1)}, bf16[32,3072]{1,0:T(8,128)(2,1)S(1)}, u32[]{:S(2)}, u32[]{:S(2)}) collective-permute-start(bf16[32,3072]{1,0:T(8,128)(2,1)S(1)} %get-tuple-element.36.refs_2_), channel_id=1, source_target_pairs={{0,2},{1,3},{2,0},{3,1},{4,6},{5,7},{6,4},{7,5},{8,10},{9,11},{10,... | collective-permute-start | bytes 589832 | tf_op jit(solution)/shard_map/ppermute | solution.py:78
  21.7 6.7 %hidden_grad.3 = (f32[64,3072]{1,0:T(8,128)S(1)}, bf16[64,3072]{1,0:T(8,128)(2,1)S(1)}) custom-call(bf16[1536,128]{1,0:T(8,128)(2,1)S(1)} %get-tuple-element.37.refs_0_, bf16[6144,1536]{1,0:T(8,128)(2,1)} %refs_1_.3, bf16[32,3072]{1,0:T(8,128)(2,1)S(1)} %get-tuple-element.36.refs_2_), custom_call_target="tpu_custom_call" | custom-call | flops 8000000000 | tf_op jit(solution)/shard_map/hidden_grad/pallas_call | solution.py:169
  28.5 1.3 %collective-permute-done.6.refs_1_ = bf16[32,3072]{1,0:T(8,128)(2,1)S(1)} collective-permute-done((bf16[32,3072]{1,0:T(8,128)(2,1)S(1)}, bf16[32,3072]{1,0:T(8,128)(2,1)S(1)}, u32[]{:S(2)}, u32[]{:S(2)}) %collective-permute-start.6) | collective-permute-done | bytes 196640 | tf_op jit(solution)/shard_map/ppermute | solution.py:78
  30.3 2.7 %collective-permute-start.8 = (bf16[16,3072]{1,0:T(8,128)(2,1)S(1)}, bf16[16,3072]{1,0:T(8,128)(2,1)S(1)}, u32[]{:S(2)}, u32[]{:S(2)}) collective-permute-start(bf16[16,3072]{1,0:T(8,128)(2,1)S(1)} %get-tuple-element.41), channel_id=1, source_target_pairs={{0,4},{1,5},{2,6},{3,7},{4,0},{5,1},{6,2},{7,3},{8,12},{9,13},{10,... | collective-permute-start | bytes 294920 | tf_op jit(solution)/shard_map/ppermute | solution.py:78
  33.0 1.2 %collective-permute-start.9 = (bf16[32,3072]{1,0:T(8,128)(2,1)S(1)}, bf16[32,3072]{1,0:T(8,128)(2,1)S(1)}, u32[]{:S(2)}, u32[]{:S(2)}) collective-permute-start(bf16[32,3072]{1,0:T(8,128)(2,1)S(1)} %get-tuple-element.43.refs_4_), channel_id=1, source_target_pairs={{0,2},{1,3},{2,0},{3,1},{4,6},{5,7},{6,4},{7,5},{8,10},{9,11},{10,... | collective-permute-start | bytes 589832 | tf_op jit(solution)/shard_map/ppermute | solution.py:78
  34.3 0.7 collective-permute-start.14
  35.0 1.0 %collective-permute-start.15 = (bf16[32,1536]{1,0:T(8,128)(2,1)S(1)}, bf16[32,1536]{1,0:T(8,128)(2,1)S(1)}, u32[]{:S(2)}, u32[]{:S(2)}) collective-permute-start(bf16[32,1536]{1,0:T(8,128)(2,1)S(1)} %stack.28.refs_4_.p0), channel_id=1, source_target_pairs={{0,16},{8,24},{16,0},{24,8},{1,17},{9,25},{17,1},{25,9},{2,18},{10... | collective-permute-start | bytes 294920 | tf_op jit(solution)/shard_map/ppermute | solution.py:74
  35.9 2.3 %collective-permute-done.8.refs_1_ = bf16[16,3072]{1,0:T(8,128)(2,1)S(1)} collective-permute-done((bf16[16,3072]{1,0:T(8,128)(2,1)S(1)}, bf16[16,3072]{1,0:T(8,128)(2,1)S(1)}, u32[]{:S(2)}, u32[]{:S(2)}) %collective-permute-start.8) | collective-permute-done | bytes 98336 | tf_op jit(solution)/shard_map/ppermute | solution.py:78
  38.3 1.4 %collective-permute-start.16 = (bf16[32,1536]{1,0:T(8,128)(2,1)S(1)}, bf16[32,1536]{1,0:T(8,128)(2,1)S(1)}, u32[]{:S(2)}, u32[]{:S(2)}) collective-permute-start(bf16[32,1536]{1,0:T(8,128)(2,1)S(1)} %stack.28.refs_4_.p0), channel_id=1, source_target_pairs={{0,24},{8,16},{16,8},{24,0},{1,25},{9,17},{17,9},{25,1},{2,26},{10... | collective-permute-start | bytes 294920 | tf_op jit(solution)/shard_map/ppermute | solution.py:74
  39.7 1.7 %collective-permute-done.9.refs_3_ = bf16[32,3072]{1,0:T(8,128)(2,1)S(1)} collective-permute-done((bf16[32,3072]{1,0:T(8,128)(2,1)S(1)}, bf16[32,3072]{1,0:T(8,128)(2,1)S(1)}, u32[]{:S(2)}, u32[]{:S(2)}) %collective-permute-start.9) | collective-permute-done | bytes 196640 | tf_op jit(solution)/shard_map/ppermute | solution.py:78
  41.7 2.9 %collective-permute-start.12 = (bf16[16,3072]{1,0:T(8,128)(2,1)S(1)}, bf16[16,3072]{1,0:T(8,128)(2,1)S(1)}, u32[]{:S(2)}, u32[]{:S(2)}) collective-permute-start(bf16[16,3072]{1,0:T(8,128)(2,1)S(1)} %get-tuple-element.46), channel_id=1, source_target_pairs={{0,4},{1,5},{2,6},{3,7},{4,0},{5,1},{6,2},{7,3},{8,12},{9,13},{10,... | collective-permute-start | bytes 294920 | tf_op jit(solution)/shard_map/ppermute | solution.py:78
  45.2 4.3 %out_weight_grad.2 = (bf16[6144,1536]{1,0:T(8,128)(2,1)}, f32[8,128]{1,0:T(8,128)S(1)}) custom-call(bf16[64,6144]{1,0:T(8,128)(2,1)S(1)} %stack.29.refs_5_.refs_0_, bf16[64,6144]{1,0:T(8,128)(2,1)S(1)} %collective-permute-done.13.refs_1_, bf16[128,1536]{1,0:T(8,128)(2,1)S(1)} %get-tuple-element.47.refs_2_, bf16[128,1536]{1,0:T(8,128)(2,1)S(1)} %join_rows.1.refs_3_.refs_4_), custom_call_target="tpu_custom_call" | custom-call | flops 8000000000 | tf_op jit(solution)/shard_map/out_weight_grad/pallas_call | solution.py:335
  49.5 1.5 %collective-permute-done.11.refs_1_ = bf16[16,3072]{1,0:T(8,128)(2,1)S(1)} collective-permute-done((bf16[16,3072]{1,0:T(8,128)(2,1)S(1)}, bf16[16,3072]{1,0:T(8,128)(2,1)S(1)}, u32[]{:S(2)}, u32[]{:S(2)}) %collective-permute-start.11) | collective-permute-done | bytes 98336 | tf_op jit(solution)/shard_map/ppermute | solution.py:78
  51.0 2.0 %collective-permute-done.12.refs_3_ = bf16[16,3072]{1,0:T(8,128)(2,1)S(1)} collective-permute-done((bf16[16,3072]{1,0:T(8,128)(2,1)S(1)}, bf16[16,3072]{1,0:T(8,128)(2,1)S(1)}, u32[]{:S(2)}, u32[]{:S(2)}) %collective-permute-start.12) | collective-permute-done | bytes 98336 | tf_op jit(solution)/shard_map/ppermute | solution.py:78
  53.3 1.0 %collective-permute-start.18 = (bf16[16,3072]{1,0:T(8,128)(2,1)S(1)}, bf16[16,3072]{1,0:T(8,128)(2,1)S(1)}, u32[]{:S(2)}, u32[]{:S(2)}) collective-permute-start(bf16[16,3072]{1,0:T(8,128)(2,1)S(1)} %get-tuple-element.50.refs_1_), channel_id=1, source_target_pairs={{0,4},{1,5},{2,6},{3,7},{4,0},{5,1},{6,2},{7,3},{8,12},{9,13},{10,... | collective-permute-start | bytes 294920 | tf_op jit(solution)/shard_map/ppermute | solution.py:78
  54.3 5.3 %out_weight_grad.3 = (bf16[6144,1536]{1,0:T(8,128)(2,1)}, f32[8,128]{1,0:T(8,128)S(1)}) custom-call(bf16[64,6144]{1,0:T(8,128)(2,1)S(1)} %stack.29.refs_5_.refs_0_, bf16[64,6144]{1,0:T(8,128)(2,1)S(1)} %collective-permute-done.13.refs_1_, bf16[128,1536]{1,0:T(8,128)(2,1)S(1)} %get-tuple-element.47.refs_2_, ...), custom_call_target="tpu_custom_call", output_to_operand_aliasing={{0}: (3, {})} | custom-call | flops 8000000000 | tf_op jit(solution)/shard_map/out_weight_grad/pallas_call | solution.py:335
  59.6 2.0 %collective-permute-done.18.refs_2_ = bf16[16,3072]{1,0:T(8,128)(2,1)S(1)} collective-permute-done((bf16[16,3072]{1,0:T(8,128)(2,1)S(1)}, bf16[16,3072]{1,0:T(8,128)(2,1)S(1)}, u32[]{:S(2)}, u32[]{:S(2)}) %collective-permute-start.18) | collective-permute-done | bytes 98336 | tf_op jit(solution)/shard_map/ppermute | solution.py:78
  62.8 0.9 %collective-permute-done.21.refs_3_ = bf16[32,3072]{1,0:T(8,128)(2,1)S(1)} collective-permute-done((bf16[32,3072]{1,0:T(8,128)(2,1)S(1)}, bf16[32,3072]{1,0:T(8,128)(2,1)S(1)}, u32[]{:S(2)}, u32[]{:S(2)}) %collective-permute-start.21) | collective-permute-done | bytes 196640 | tf_op jit(solution)/shard_map/ppermute | solution.py:82
  63.7 4.3 %in_weight_grad.2 = (bf16[6144,1536]{1,0:T(8,128)(2,1)}, f32[8,128]{1,0:T(8,128)S(1)}) custom-call(bf16[32,3072]{1,0:T(8,128)(2,1)S(1)} %get-tuple-element.49.refs_4_.refs_0_, bf16[32,3072]{1,0:T(8,128)(2,1)S(1)} %get-tuple-element.54.refs_1_, bf16[32,3072]{1,0:T(8,128)(2,1)S(1)} %collective-permute-done.20.refs_2_, ...), custom_call_target="tpu_custom_call" | custom-call | flops 8000000000 | tf_op jit(solution)/shard_map/in_weight_grad/pallas_call | solution.py:335
  68.0 1.6 %collective-permute-done.19.refs_0_ = bf16[32,3072]{1,0:T(8,128)(2,1)S(1)} collective-permute-done((bf16[32,3072]{1,0:T(8,128)(2,1)S(1)}, bf16[32,3072]{1,0:T(8,128)(2,1)S(1)}, u32[]{:S(2)}, u32[]{:S(2)}) %collective-permute-start.19) | collective-permute-done | bytes 196640 | tf_op jit(solution)/shard_map/ppermute | solution.py:78
  69.6 1.4 %token_grad.2.refs_6_ = f32[128,1536]{1,0:T(8,128)S(1)} custom-call(bf16[32,3072]{1,0:T(8,128)(2,1)S(1)} %get-tuple-element.49.refs_4_.refs_0_, bf16[32,3072]{1,0:T(8,128)(2,1)S(1)} %get-tuple-element.54.refs_1_, bf16[32,3072]{1,0:T(8,128)(2,1)S(1)} %collective-permute-done.20.refs_2_, bf16[32,3072]{1,0:T(8,128)(2,1)S(1)} %collective-permute-done.21.refs_3_, ...), custom_call_target="tpu_custom_call" | custom-call | flops 8000000000 | tf_op jit(solution)/shard_map/token_grad/pallas_call | solution.py:392
  71.0 2.0 %token_grad.3 = (f32[32,1536]{1,0:T(8,128)S(1)}, bf16[32,1536]{1,0:T(8,128)(2,1)S(1)}, bf16[32,1536]{1,0:T(8,128)(2,1)S(1)}, bf16[32,1536]{1,0:T(8,128)(2,1)S(1)}) custom-call(s32[5]{0:T(128)S(1)} %stack.26.refs_0_.place_ref, bf16[32,3072]{1,0:T(8,128)(2,1)S(1)} %get-tuple-element.53.refs_5_.refs_1_.refs_0_, ...), custom_call_target="tpu_custom_call" | custom-call | flops 8000000000 | tf_op jit(solution)/shard_map/token_grad/pallas_call | solution.py:392
  73.1 1.1 %collective-permute-start.25 = (bf16[32,1536]{1,0:T(8,128)(2,1)S(1)}, bf16[32,1536]{1,0:T(8,128)(2,1)S(1)}, u32[]{:S(2)}, u32[]{:S(2)}) collective-permute-start(bf16[32,1536]{1,0:T(8,128)(2,1)S(1)} %get-tuple-element.58), channel_id=1, source_target_pairs={{0,16},{8,24},{16,0},{24,8},{1,17},{9,25},{17,1},{25,9},{2,18},{10... | collective-permute-start | bytes 294920 | tf_op jit(solution)/shard_map/ppermute | solution.py:74
  74.3 2.3 %collective-permute-start.24 = (bf16[32,1536]{1,0:T(8,128)(2,1)S(1)}, bf16[32,1536]{1,0:T(8,128)(2,1)S(1)}, u32[]{:S(2)}, u32[]{:S(2)}) collective-permute-start(bf16[32,1536]{1,0:T(8,128)(2,1)S(1)} %get-tuple-element.57), channel_id=1, source_target_pairs={{0,8},{8,0},{16,24},{24,16},{1,9},{9,1},{17,25},{25,17},{2,10},{10... | collective-permute-start | bytes 294920 | tf_op jit(solution)/shard_map/ppermute | solution.py:74
  76.6 4.9 %in_weight_grad.3 = (bf16[6144,1536]{1,0:T(8,128)(2,1)}, f32[8,128]{1,0:T(8,128)}) custom-call(bf16[32,3072]{1,0:T(8,128)(2,1)S(1)} %get-tuple-element.53.refs_5_.refs_1_.refs_0_, bf16[32,3072]{1,0:T(8,128)(2,1)S(1)} %tie.1.refs_5_.refs_2_.refs_1_, bf16[32,3072]{1,0:T(8,128)(2,1)S(1)} %collective-permute-done.22.refs_3_.refs_2_, ...), custom_call_target="tpu_custom_call", output_to_operand_aliasing={{0}: (5, {})} | custom-call | flops 8000000000 | tf_op jit(solution)/shard_map/in_weight_grad/pallas_call | solution.py:335
  (68 shorter events, 4.2 us)
Async XLA Ops:
  0.6 9.4 %collective-permute-start = (bf16[32,1536]{1,0:T(8,128)(2,1)}, bf16[32,1536]{1,0:T(8,128)(2,1)S(1)}, u32[]{:S(2)}, u32[]{:S(2)}) collective-permute-start(bf16[32,1536]{1,0:T(8,128)(2,1)} %refs_1_.2), channel_id=1, source_target_pairs={{0,8},{8,0},{16,24},{24,16},{1,9},{9,1},{17,25},{25,17},{2,10},{10... | collective-permute-start | bytes 294920 | tf_op jit(solution)/shard_map/ppermute | solution.py:74
  3.6 6.4 %collective-permute-start.1 = (bf16[32,1536]{1,0:T(8,128)(2,1)}, bf16[32,1536]{1,0:T(8,128)(2,1)S(1)}, u32[]{:S(2)}, u32[]{:S(2)}) collective-permute-start(bf16[32,1536]{1,0:T(8,128)(2,1)} %refs_1_.2), channel_id=1, source_target_pairs={{0,16},{8,24},{16,0},{24,8},{1,17},{9,25},{17,1},{25,9},{2,18},{10... | collective-permute-start | bytes 294920 | tf_op jit(solution)/shard_map/ppermute | solution.py:74
  5.2 5.7 %collective-permute-start.2 = (bf16[32,1536]{1,0:T(8,128)(2,1)}, bf16[32,1536]{1,0:T(8,128)(2,1)S(1)}, u32[]{:S(2)}, u32[]{:S(2)}) collective-permute-start(bf16[32,1536]{1,0:T(8,128)(2,1)} %refs_1_.2), channel_id=1, source_target_pairs={{0,24},{8,16},{16,8},{24,0},{1,25},{9,17},{17,9},{25,1},{2,26},{10... | collective-permute-start | bytes 294920 | tf_op jit(solution)/shard_map/ppermute | solution.py:74
  5.2 13.1 %collective-permute-start.4 = (bf16[16,6144]{1,0:T(8,128)(2,1)}, bf16[16,6144]{1,0:T(8,128)(2,1)S(1)}, u32[]{:S(2)}, u32[]{:S(2)}) collective-permute-start(bf16[16,6144]{1,0:T(8,128)(2,1)} %refs_4_.4), channel_id=1, source_target_pairs={{0,4},{1,5},{2,6},{3,7},{4,0},{5,1},{6,2},{7,3},{8,12},{9,13},{10,... | collective-permute-start | bytes 589832 | tf_op jit(solution)/shard_map/ppermute | solution.py:78
  8.2 11.7 %collective-permute-start.5 = (bf16[16,6144]{1,0:T(8,128)(2,1)}, bf16[16,6144]{1,0:T(8,128)(2,1)S(1)}, u32[]{:S(2)}, u32[]{:S(2)}) collective-permute-start(bf16[16,6144]{1,0:T(8,128)(2,1)} %refs_4_.4), channel_id=1, source_target_pairs={{0,2},{1,3},{2,0},{3,1},{4,6},{5,7},{6,4},{7,5},{8,10},{9,11},{10,... | collective-permute-start | bytes 589832 | tf_op jit(solution)/shard_map/ppermute | solution.py:78
  9.8 10.1 %copy-start.1 = (bf16[16,6144]{1,0:T(8,128)(2,1)S(1)}, bf16[16,6144]{1,0:T(8,128)(2,1)}, u32[]{:S(2)}) copy-start(bf16[16,6144]{1,0:T(8,128)(2,1)} %refs_4_.4) | copy-start | bytes 589828
  18.2 1.8 %collective-permute-start.3 = (bf16[64,3072]{1,0:T(8,128)(2,1)S(1)}, bf16[64,3072]{1,0:T(8,128)(2,1)S(1)}, u32[]{:S(2)}, u32[]{:S(2)}) collective-permute-start(bf16[64,3072]{1,0:T(8,128)(2,1)S(1)} %get-tuple-element.34.refs_3_), channel_id=1, source_target_pairs={{0,1},{1,0},{2,3},{3,2},{4,5},{5,4},{6,7},{7,6},{8,9},{9,8},{10,11... | collective-permute-start | bytes 1179656 | tf_op jit(solution)/shard_map/ppermute | solution.py:82
  18.2 15.9 %collective-permute-start.10 = (bf16[16,6144]{1,0:T(8,128)(2,1)S(1)}, bf16[16,6144]{1,0:T(8,128)(2,1)S(1)}, u32[]{:S(2)}, u32[]{:S(2)}) collective-permute-start(bf16[16,6144]{1,0:T(8,128)(2,1)S(1)} %collective-permute-done.4.refs_1_), channel_id=1, source_target_pairs={{0,2},{1,3},{2,0},{3,1},{4,6},{5,7},{6,4},{7,5},{8,10},{9,11},{10,... | collective-permute-start | bytes 589832 | tf_op jit(solution)/shard_map/ppermute | solution.py:78
  20.1 8.4 %copy-start.2 = (bf16[32,1536]{1,0:T(8,128)(2,1)S(1)}, bf16[32,1536]{1,0:T(8,128)(2,1)}, u32[]{:S(2)}) copy-start(bf16[32,1536]{1,0:T(8,128)(2,1)} %refs_0_.4) | copy-start | bytes 294916
  20.1 9.7 %collective-permute-start.6 = (bf16[32,3072]{1,0:T(8,128)(2,1)S(1)}, bf16[32,3072]{1,0:T(8,128)(2,1)S(1)}, u32[]{:S(2)}, u32[]{:S(2)}) collective-permute-start(bf16[32,3072]{1,0:T(8,128)(2,1)S(1)} %get-tuple-element.36.refs_2_), channel_id=1, source_target_pairs={{0,2},{1,3},{2,0},{3,1},{4,6},{5,7},{6,4},{7,5},{8,10},{9,11},{10,... | collective-permute-start | bytes 589832 | tf_op jit(solution)/shard_map/ppermute | solution.py:78
  28.4 1.8 %collective-permute-start.7 = (bf16[64,3072]{1,0:T(8,128)(2,1)S(1)}, bf16[64,3072]{1,0:T(8,128)(2,1)S(1)}, u32[]{:S(2)}, u32[]{:S(2)}) collective-permute-start(bf16[64,3072]{1,0:T(8,128)(2,1)S(1)} %get-tuple-element.39.refs_1_), channel_id=1, source_target_pairs={{0,1},{1,0},{2,3},{3,2},{4,5},{5,4},{6,7},{7,6},{8,9},{9,8},{10,11... | collective-permute-start | bytes 1179656 | tf_op jit(solution)/shard_map/ppermute | solution.py:82
  30.3 8.0 %collective-permute-start.8 = (bf16[16,3072]{1,0:T(8,128)(2,1)S(1)}, bf16[16,3072]{1,0:T(8,128)(2,1)S(1)}, u32[]{:S(2)}, u32[]{:S(2)}) collective-permute-start(bf16[16,3072]{1,0:T(8,128)(2,1)S(1)} %get-tuple-element.41), channel_id=1, source_target_pairs={{0,4},{1,5},{2,6},{3,7},{4,0},{5,1},{6,2},{7,3},{8,12},{9,13},{10,... | collective-permute-start | bytes 294920 | tf_op jit(solution)/shard_map/ppermute | solution.py:78
  33.0 8.4 %collective-permute-start.9 = (bf16[32,3072]{1,0:T(8,128)(2,1)S(1)}, bf16[32,3072]{1,0:T(8,128)(2,1)S(1)}, u32[]{:S(2)}, u32[]{:S(2)}) collective-permute-start(bf16[32,3072]{1,0:T(8,128)(2,1)S(1)} %get-tuple-element.43.refs_4_), channel_id=1, source_target_pairs={{0,2},{1,3},{2,0},{3,1},{4,6},{5,7},{6,4},{7,5},{8,10},{9,11},{10,... | collective-permute-start | bytes 589832 | tf_op jit(solution)/shard_map/ppermute | solution.py:78
  34.2 11.0 %collective-permute-start.13 = (bf16[64,6144]{1,0:T(8,128)(2,1)S(1)}, bf16[64,6144]{1,0:T(8,128)(2,1)S(1)}, u32[]{:S(2)}, u32[]{:S(2)}) collective-permute-start(bf16[64,6144]{1,0:T(8,128)(2,1)S(1)} %stack.29.refs_5_.refs_0_), channel_id=1, source_target_pairs={{0,1},{1,0},{2,3},{3,2},{4,5},{5,4},{6,7},{7,6},{8,9},{9,8},{10,11... | collective-permute-start | bytes 2359304 | tf_op jit(solution)/shard_map/ppermute | solution.py:82
  34.3 7.4 %collective-permute-start.14 = (bf16[32,1536]{1,0:T(8,128)(2,1)S(1)}, bf16[32,1536]{1,0:T(8,128)(2,1)S(1)}, u32[]{:S(2)}, u32[]{:S(2)}) collective-permute-start(bf16[32,1536]{1,0:T(8,128)(2,1)S(1)} %stack.28.refs_4_.p0), channel_id=1, source_target_pairs={{0,8},{8,0},{16,24},{24,16},{1,9},{9,1},{17,25},{25,17},{2,10},{10... | collective-permute-start | bytes 294920 | tf_op jit(solution)/shard_map/ppermute | solution.py:74
  35.0 9.6 %collective-permute-start.15 = (bf16[32,1536]{1,0:T(8,128)(2,1)S(1)}, bf16[32,1536]{1,0:T(8,128)(2,1)S(1)}, u32[]{:S(2)}, u32[]{:S(2)}) collective-permute-start(bf16[32,1536]{1,0:T(8,128)(2,1)S(1)} %stack.28.refs_4_.p0), channel_id=1, source_target_pairs={{0,16},{8,24},{16,0},{24,8},{1,17},{9,25},{17,1},{25,9},{2,18},{10... | collective-permute-start | bytes 294920 | tf_op jit(solution)/shard_map/ppermute | solution.py:74
  38.3 6.3 %collective-permute-start.16 = (bf16[32,1536]{1,0:T(8,128)(2,1)S(1)}, bf16[32,1536]{1,0:T(8,128)(2,1)S(1)}, u32[]{:S(2)}, u32[]{:S(2)}) collective-permute-start(bf16[32,1536]{1,0:T(8,128)(2,1)S(1)} %stack.28.refs_4_.p0), channel_id=1, source_target_pairs={{0,24},{8,16},{16,8},{24,0},{1,25},{9,17},{17,9},{25,1},{2,26},{10... | collective-permute-start | bytes 294920 | tf_op jit(solution)/shard_map/ppermute | solution.py:74
  41.6 9.4 %collective-permute-start.11 = (bf16[16,3072]{1,0:T(8,128)(2,1)S(1)}, bf16[16,3072]{1,0:T(8,128)(2,1)S(1)}, u32[]{:S(2)}, u32[]{:S(2)}) collective-permute-start(bf16[16,3072]{1,0:T(8,128)(2,1)S(1)} %get-tuple-element.44.rest_0_.refs_0_), channel_id=1, source_target_pairs={{0,4},{1,5},{2,6},{3,7},{4,0},{5,1},{6,2},{7,3},{8,12},{9,13},{10,... | collective-permute-start | bytes 294920 | tf_op jit(solution)/shard_map/ppermute | solution.py:78
  41.7 11.3 %collective-permute-start.12 = (bf16[16,3072]{1,0:T(8,128)(2,1)S(1)}, bf16[16,3072]{1,0:T(8,128)(2,1)S(1)}, u32[]{:S(2)}, u32[]{:S(2)}) collective-permute-start(bf16[16,3072]{1,0:T(8,128)(2,1)S(1)} %get-tuple-element.46), channel_id=1, source_target_pairs={{0,4},{1,5},{2,6},{3,7},{4,0},{5,1},{6,2},{7,3},{8,12},{9,13},{10,... | collective-permute-start | bytes 294920 | tf_op jit(solution)/shard_map/ppermute | solution.py:78
  53.1 9.0 %collective-permute-start.17 = (bf16[32,3072]{1,0:T(8,128)(2,1)S(1)}, bf16[32,3072]{1,0:T(8,128)(2,1)S(1)}, u32[]{:S(2)}, u32[]{:S(2)}) collective-permute-start(bf16[32,3072]{1,0:T(8,128)(2,1)S(1)} %get-tuple-element.49.refs_4_.refs_0_), channel_id=1, source_target_pairs={{0,2},{1,3},{2,0},{3,1},{4,6},{5,7},{6,4},{7,5},{8,10},{9,11},{10,... | collective-permute-start | bytes 589832 | tf_op jit(solution)/shard_map/ppermute | solution.py:78
  53.2 9.6 %collective-permute-start.20 = (bf16[32,3072]{1,0:T(8,128)(2,1)S(1)}, bf16[32,3072]{1,0:T(8,128)(2,1)S(1)}, u32[]{:S(2)}, u32[]{:S(2)}) collective-permute-start(bf16[32,3072]{1,0:T(8,128)(2,1)S(1)} %get-tuple-element.49.refs_4_.refs_0_), channel_id=1, source_target_pairs={{0,1},{1,0},{2,3},{3,2},{4,5},{5,4},{6,7},{7,6},{8,9},{9,8},{10,11... | collective-permute-start | bytes 589832 | tf_op jit(solution)/shard_map/ppermute | solution.py:82
  53.3 8.4 %collective-permute-start.18 = (bf16[16,3072]{1,0:T(8,128)(2,1)S(1)}, bf16[16,3072]{1,0:T(8,128)(2,1)S(1)}, u32[]{:S(2)}, u32[]{:S(2)}) collective-permute-start(bf16[16,3072]{1,0:T(8,128)(2,1)S(1)} %get-tuple-element.50.refs_1_), channel_id=1, source_target_pairs={{0,4},{1,5},{2,6},{3,7},{4,0},{5,1},{6,2},{7,3},{8,12},{9,13},{10,... | collective-permute-start | bytes 294920 | tf_op jit(solution)/shard_map/ppermute | solution.py:78
  54.3 15.3 %slice-start = ((s8[18874368]{0:T(1024)(128)(4,1)}), s8[4194304]{0:T(1024)(128)(4,1)S(1)}, s32[]{:S(2)}) async-start(s8[18874368]{0:T(1024)(128)(4,1)} %bitcast.5), calls=%async_computation | async-start | bytes 8388608
  54.3 15.3 %slice-start.1 = ((s8[18874368]{0:T(1024)(128)(4,1)}), s8[4194304]{0:T(1024)(128)(4,1)S(1)}, s32[]{:S(2)}) async-start(s8[18874368]{0:T(1024)(128)(4,1)} %bitcast.5), calls=%async_computation.1 | async-start | bytes 8388608
  54.3 15.3 %slice-start.2 = ((s8[18874368]{0:T(1024)(128)(4,1)}), s8[4194304]{0:T(1024)(128)(4,1)S(1)}, s32[]{:S(2)}) async-start(s8[18874368]{0:T(1024)(128)(4,1)} %bitcast.5), calls=%async_computation.2 | async-start | bytes 8388608
  62.2 1.5 %collective-permute-start.21 = (bf16[32,3072]{1,0:T(8,128)(2,1)S(1)}, bf16[32,3072]{1,0:T(8,128)(2,1)S(1)}, u32[]{:S(2)}, u32[]{:S(2)}) collective-permute-start(bf16[32,3072]{1,0:T(8,128)(2,1)S(1)} %get-tuple-element.54.refs_1_), channel_id=1, source_target_pairs={{0,1},{1,0},{2,3},{3,2},{4,5},{5,4},{6,7},{7,6},{8,9},{9,8},{10,11... | collective-permute-start | bytes 589832 | tf_op jit(solution)/shard_map/ppermute | solution.py:82
  62.3 7.3 %collective-permute-start.19 = (bf16[32,3072]{1,0:T(8,128)(2,1)S(1)}, bf16[32,3072]{1,0:T(8,128)(2,1)S(1)}, u32[]{:S(2)}, u32[]{:S(2)}) collective-permute-start(bf16[32,3072]{1,0:T(8,128)(2,1)S(1)} %get-tuple-element.53.refs_5_.refs_1_.refs_0_), channel_id=1, source_target_pairs={{0,2},{1,3},{2,0},{3,1},{4,6},{5,7},{6,4},{7,5},{8,10},{9,11},{10,... | collective-permute-start | bytes 589832 | tf_op jit(solution)/shard_map/ppermute | solution.py:78
  62.5 8.5 %collective-permute-start.22 = (bf16[32,3072]{1,0:T(8,128)(2,1)S(1)}, bf16[32,3072]{1,0:T(8,128)(2,1)S(1)}, u32[]{:S(2)}, u32[]{:S(2)}) collective-permute-start(bf16[32,3072]{1,0:T(8,128)(2,1)S(1)} %get-tuple-element.53.refs_5_.refs_1_.refs_0_), channel_id=1, source_target_pairs={{0,1},{1,0},{2,3},{3,2},{4,5},{5,4},{6,7},{7,6},{8,9},{9,8},{10,11... | collective-permute-start | bytes 589832 | tf_op jit(solution)/shard_map/ppermute | solution.py:82
  69.6 1.5 %collective-permute-start.23 = (bf16[32,3072]{1,0:T(8,128)(2,1)S(1)}, bf16[32,3072]{1,0:T(8,128)(2,1)S(1)}, u32[]{:S(2)}, u32[]{:S(2)}) collective-permute-start(bf16[32,3072]{1,0:T(8,128)(2,1)S(1)} %tie.1.refs_5_.refs_2_.refs_1_), channel_id=1, source_target_pairs={{0,1},{1,0},{2,3},{3,2},{4,5},{5,4},{6,7},{7,6},{8,9},{9,8},{10,11... | collective-permute-start | bytes 589832 | tf_op jit(solution)/shard_map/ppermute | solution.py:82
  73.0 8.4 %collective-permute-start.26 = (bf16[32,1536]{1,0:T(8,128)(2,1)S(1)}, bf16[32,1536]{1,0:T(8,128)(2,1)S(1)}, u32[]{:S(2)}, u32[]{:S(2)}) collective-permute-start(bf16[32,1536]{1,0:T(8,128)(2,1)S(1)} %get-tuple-element.59), channel_id=1, source_target_pairs={{0,24},{8,16},{16,8},{24,0},{1,25},{9,17},{17,9},{25,1},{2,26},{10... | collective-permute-start | bytes 294920 | tf_op jit(solution)/shard_map/ppermute | solution.py:74
  73.1 8.4 %collective-permute-start.25 = (bf16[32,1536]{1,0:T(8,128)(2,1)S(1)}, bf16[32,1536]{1,0:T(8,128)(2,1)S(1)}, u32[]{:S(2)}, u32[]{:S(2)}) collective-permute-start(bf16[32,1536]{1,0:T(8,128)(2,1)S(1)} %get-tuple-element.58), channel_id=1, source_target_pairs={{0,16},{8,24},{16,0},{24,8},{1,17},{9,25},{17,1},{25,9},{2,18},{10... | collective-permute-start | bytes 294920 | tf_op jit(solution)/shard_map/ppermute | solution.py:74
  74.3 7.2 %collective-permute-start.24 = (bf16[32,1536]{1,0:T(8,128)(2,1)S(1)}, bf16[32,1536]{1,0:T(8,128)(2,1)S(1)}, u32[]{:S(2)}, u32[]{:S(2)}) collective-permute-start(bf16[32,1536]{1,0:T(8,128)(2,1)S(1)} %get-tuple-element.57), channel_id=1, source_target_pairs={{0,8},{8,0},{16,24},{24,16},{1,9},{9,1},{17,25},{25,17},{2,10},{10... | collective-permute-start | bytes 294920 | tf_op jit(solution)/shard_map/ppermute | solution.py:74
  (3 other events, 15.8 us)

commit v3 on v2

--- a/solution.py
+++ b/solution.py
@@ -11,6 +11,7 @@
 cubic_term = 0.044715
 VMEM_LIMIT = 16 * 1024 * 1024
 CHUNKS = 2
+AHEAD = 3
 FLOPS = 8_000_000_000
 
 
@@ -121,9 +122,9 @@
     width = w_out.shape[1]
     tokens = 4 * x[0].shape[0] if join else x[0].shape[1]
     half = tokens // 2
-    bounds = [units * n // 12 for n in (0, 3, 6, 8, 10, 11, 12)]
-    cut = [slice(a, b) for a, b in zip(bounds[:-1], bounds[1:])]
-    groups = [cut[n : n + 2] for n in (0, 2, 4)]
+    cut = cuts(units, 512)
+    groups = [cut[n : n + 2] for n in range(1, len(cut) - 1, 2)]
+    groups = [cut[:1]] + groups + [cut[-1:]]
     pieces = len(x)
 
     def body(*refs):
@@ -138,7 +139,7 @@
             )
             for n, c in enumerate(cut)
         ]
-        for copy in copies[:2]:
+        for copy in copies[:AHEAD]:
             copy.start()
         if join:
             joined, flipped = rest[:2]
@@ -146,13 +147,14 @@
             flipped[...] = joined[...].T
         else:
             flipped = x_refs[0]
-        for n, group in enumerate(groups):
-            for copy in copies[2 * n : 2 * n + 2]:
+        arrived = 0
+        for group in groups:
+            for copy in copies[arrived : arrived + len(group)]:
                 copy.wait()
-            for copy in copies[2 * n + 2 : 2 * n + 4]:
+            for copy in copies[arrived + AHEAD : arrived + AHEAD + len(group)]:
                 copy.start()
-            for c in cuts(group[1].stop - group[0].start, 512):
-                c = slice(group[0].start + c.start, group[0].start + c.stop)
+            arrived += len(group)
+            for c in group:
                 value = jnp.dot(held[c, :], flipped[...], preferred_element_type=jnp.float32).T
                 own[:, c] = value[:half]
                 other[:, c] = value[half:].astype(jnp.bfloat16)
@@ -214,7 +216,7 @@
     )(*operands, *after)
 
 
-def sum_cores(own, got, after=()):
+def add_halves(own, got, after=(), cost=COST):
     rows, units = own.shape
     half = (rows // 2, units)
 
@@ -222,7 +224,7 @@
         halve(add(own, got), held, send)
 
     return small(
-        body, [own, got], [(half, jnp.float32), (half, jnp.bfloat16)], after, name="sum_cores"
+        body, [own, got], [(half, jnp.float32), (half, jnp.bfloat16)], after, cost, "add_halves"
     )
 
 
@@ -248,58 +250,17 @@
     )
 
 
-def sum_far(mine0, far0, held1, near1, pre_act, after=()):
-    quarter = mine0.shape
-
-    def body(mine0, far0, held1, near1, pre_ref, grad0, mine1, send1):
-        grad0[...] = slope_times(add(mine0, far0), pre_ref, 0)
-        halve(add(held1, near1), mine1, send1)
-
-    return small(
-        body,
-        [mine0, far0, held1, near1, pre_act],
-        [(quarter, jnp.bfloat16), (quarter, jnp.float32), (quarter, jnp.bfloat16)],
-        after,
-        name="sum_far",
-    )
-
-
-def pair_far(grad0, far0, mine1, far1, pre_act, after=()):
-    rows, units = grad0.shape
-
-    def body(grad0, far0, mine1, far1, pre_ref, pair0, grad1):
-        pair0[:rows] = grad0[...]
-        pair0[rows:] = far0[...]
-        grad1[...] = slope_times(add(mine1, far1), pre_ref, 1)
-
-    return small(
-        body,
-        [grad0, far0, mine1, far1, pre_act],
-        [((2 * rows, units), jnp.bfloat16), ((rows, units), jnp.bfloat16)],
-        after,
-        name="pair_far",
-    )
-
-
-def pair_near(near0, grad1, far1, after=()):
-    rows, units = grad1.shape
-
-    def body(near0, grad1, far1, blocks0, pair1):
-        blocks0[...] = near0[...]
-        pair1[:rows] = grad1[...]
-        pair1[rows:] = far1[...]
-
-    return small(
-        body,
-        [near0, grad1, far1],
-        [(near0.shape, jnp.bfloat16), ((2 * rows, units), jnp.bfloat16)],
-        after,
-        LIGHT,
-        "pair_near",
-    )
-
-
-def weight_grad(pieces, x, first, start, rows, units, held, activate, after=()):
+def far_slope(mine, far, pre_act, chunk, after=(), cost=LIGHT):
+    def body(mine, far, pre_ref, grad):
+        grad[...] = slope_times(add(mine, far), pre_ref, chunk)
+
+    shapes = [(mine.shape, jnp.bfloat16)]
+    return small(body, [mine, far, pre_act], shapes, after, cost, "far_slope")[0]
+
+
+def weight_grad(
+    pieces, x, first, start, rows, units, held, activate, after=(), cost=COST
+):
     tokens, width = x.shape
     count = len(pieces)
     extra = len(after) + (held is not None)
@@ -346,7 +307,7 @@
         ],
         input_output_aliases={} if held is None else {count + 1: 0},
         compiler_params=params(),
-        cost_estimate=COST,
+        cost_estimate=cost,
         name="out_weight_grad" if activate else "in_weight_grad",
     )(*operands)
 
@@ -401,19 +362,19 @@
     )(*([place] if last else []), *pieces, w_in, *([total] if more else []), *after)
 
 
-def mark(after=(), cost=SHORT):
+def mark(after=(), cost=SHORT, held=()):
     def body(*refs):
         refs[-1][...] = jnp.zeros_like(refs[-1])
 
     return pl.pallas_call(
         body,
         out_shape=jax.ShapeDtypeStruct((8, 128), jnp.float32),
-        in_specs=[ANY] * len(after),
+        in_specs=[ANY] * len(after) + [VMEM] * len(held),
         out_specs=VMEM,
         compiler_params=params(),
         cost_estimate=cost,
         name="mark",
-    )(*after)
+    )(*after, *held)
 
 
 def tie(value, after, cost=LIGHT):
@@ -477,7 +438,7 @@
     )
     pre_most = stack([pre_act, pre_far, pre_near], (send0,))
     step = mark((pre_most,), COST)
-    held0, out0 = sum_cores(own0, swap_cores(send0), (step,))
+    held0, out0 = add_halves(own0, swap_cores(send0), (step,))
     own1, send1 = hidden_grad([flipped], w_out, per_chunk, per_chunk, (out0,))
     mine = stack([tokens], (send1,))
     mine0, out0, held1, out1 = sum_near(
@@ -485,23 +446,34 @@
     )
     pre_own = stack([pre_act, pre_far, pre_near, swap_chips(pre_far, 1)], (out1,))
     pre = [pre_own, swap_cores(pre_own)]
-    grad0, mine1, out1 = sum_far(
-        mine0, swap_chips(out0, 2), held1, swap_chips(out1, 1), pre_act, (pre_own,)
-    )
-    tok = join_rows([mine] + [swap_rows(mine, d) for d in (1, 2, 3)], place, (grad0,))
-    half = units // 2
-    grad_w_out, token = weight_grad(pre, x, 0, 0, half, units, None, True, (tok,))
-    pair0, grad1 = pair_far(
-        grad0, swap_chips(grad0, 2), mine1, swap_chips(out1, 2), pre_act, (token,)
-    )
-    grad_w_out, token = weight_grad(pre, x, 0, half, half, units, grad_w_out, True, (pair0,))
-    near0, pair1 = pair_near(swap_chips(pair0, 1), grad1, swap_chips(grad1, 2), (token,))
+    grad0 = far_slope(mine0, swap_chips(out0, 2), pre_act, 0, (pre_own,), COST)
+    mine1, out1 = add_halves(held1, swap_chips(out1, 1), (grad0,), LIGHT)
+    ends = [units * n // 12 for n in (0, 2, 7, 11, 12)]
+    parts = [b - a for a, b in zip(ends[:-1], ends[1:])]
+    grad_w_out, token = weight_grad(pre, x, 0, 0, parts[0], units, None, True, (out1,), LIGHT)
+    pair0 = stack([grad0, swap_chips(grad0, 2)], (token,))
+    grad_w_out, token = weight_grad(
+        pre, x, 0, ends[1], parts[1], units, grad_w_out, True, (pair0,)
+    )
+    tok = join_rows([mine] + [swap_rows(mine, d) for d in (1, 2, 3)], place, (token,))
+    grad1 = far_slope(mine1, swap_chips(out1, 2), pre_act, 1, (tok,))
+    near0 = tie(swap_chips(pair0, 1), (grad1,))
     whole = [pair0, near0, swap_cores(pair0), swap_cores(near0)]
-    grad_w_in, token = weight_grad(whole, tok, 0, 0, per_chunk, units, None, False, (pair1,))
-    near1 = tie(swap_chips(pair1, 1), (token,))
-    (total,) = token_grad(whole, w_in, 0, None, None, (near1,))
+    step = mark((near0,), LIGHT, (w_in,))
+    grad_w_in, token = weight_grad(
+        whole, tok, 0, 0, per_chunk, units, None, False, (step,), LIGHT
+    )
+    pair1 = stack([grad1, swap_chips(grad1, 2)], (token,))
+    grad_w_out, token = weight_grad(
+        pre, x, 0, ends[2], parts[2], units, grad_w_out, True, (pair1,), LIGHT
+    )
+    (total,) = token_grad(whole, w_in, 0, None, None, (token,))
+    near1 = tie(swap_chips(pair1, 1), (total,))
     whole = [pair1, near1, swap_cores(pair1), swap_cores(near1)]
-    part, *parts = token_grad(whole, w_in, per_chunk, total, place)
+    grad_w_out, token = weight_grad(
+        pre, x, 0, ends[3], parts[3], units, grad_w_out, True, (near1,)
+    )
+    part, *parts = token_grad(whole, w_in, per_chunk, total, place, (token,))
     grad_w_in, _ = weight_grad(
         whole, tok, per_chunk, 0, per_chunk, units, grad_w_in, False, (part,)
     )

time: 82.4 us -> 81.2 us (0.985)
  waiting for transfers between devices: 15.1 us -> 9.21 us
  starting transfers between devices: 27.8 us -> 31.2 us
  Pallas kernels: 37.4 us -> 38.6 us
    ppermute x11, waiting for transfers between devices: 12.9 us -> 8.31 us  [swap_chips(): return lax.ppermute(array, 'col', [(i, i ^ 2 * d) for i in range(8)])]
    ppermute x11, starting transfers between devices: 16 us -> 19.2 us  [swap_chips(): return lax.ppermute(array, 'col', [(i, i ^ 2 * d) for i in range(8)])]
    pallas_call x4 -> x6, Pallas kernels: 18.8 us -> 21.1 us  [weight_grad(): pl.pallas_call(body, in_specs=[VMEM] * (count + 1) + [ANY] * extra, out_s...]
    ppermute x7, waiting for transfers between devices: 1.3 us -> 0.02 us  [swap_cores(): return lax.ppermute(array, 'col', [(i, i ^ 1) for i in range(8)])]
    pallas_call x2, Pallas kernels: 14 us -> 12.8 us  [hidden_grad(): pl.pallas_call(body, in_specs=[SMEM] * join + [VMEM] * pieces + [ANY] * (...]
  transfers between devices with their start and end apart: 27 -> 27, of which waited for: 11 -> 6; matrix products, arithmetic and copies ran while one was open for 0% -> 0% of each run, Pallas kernels for 43% -> 45%
where the time goes in v3:
time: 81.2 us; the launch traced here: 81 us
  Pallas kernels  38.6 us (48%)
  starting transfers between devices  31.2 us (38%)
  waiting for transfers between devices  9.21 us (11%)
  between operations  1.15 us (1%)
    pallas_call x6, Pallas kernels, weight_grad(): pl.pallas_call(body, in_specs=[VMEM] * (count + 1) + [ANY] * extra, out_s...  21.1 us
    ppermute x11, starting transfers between devices, swap_chips(): return lax.ppermute(array, 'col', [(i, i ^ 2 * d) for i in range(8)])  19.2 us
    pallas_call x2, Pallas kernels, hidden_grad(): pl.pallas_call(body, in_specs=[SMEM] * join + [VMEM] * pieces + [ANY] * (...  12.8 us
    ppermute x9, starting transfers between devices, swap_rows(): return lax.ppermute(array, 'row', [(r, r ^ d) for r in range(4)])  11.1 us
    ppermute x11, waiting for transfers between devices, swap_chips(): return lax.ppermute(array, 'col', [(i, i ^ 2 * d) for i in range(8)])  8.31 us
    pallas_call x2, Pallas kernels, token_grad(): pl.pallas_call(body, in_specs=[SMEM] * last + [VMEM] * (count + 1 + more)...  3.36 us
  transfers between devices with their start and end apart: 27, of which 6 were waited for; matrix products, arithmetic and copies ran while one was open for 0% of the time, Pallas kernels for 45%

profile of v3, /device:TPU:0, one launch (start us, length us, event | category | flops | bytes accessed | tf_op | source)
XLA Modules:
  0.0 81.0 jit_solution(13769905050574877205)
XLA Ops:
  0.6 3.0 %collective-permute-start = (bf16[32,1536]{1,0:T(8,128)(2,1)}, bf16[32,1536]{1,0:T(8,128)(2,1)S(1)}, u32[]{:S(2)}, u32[]{:S(2)}) collective-permute-start(bf16[32,1536]{1,0:T(8,128)(2,1)} %refs_1_.3), channel_id=1, source_target_pairs={{0,8},{8,0},{16,24},{24,16},{1,9},{9,1},{17,25},{25,17},{2,10},{10... | collective-permute-start | bytes 294920 | tf_op jit(solution)/shard_map/ppermute | solution.py:75
  3.6 1.5 %collective-permute-start.1 = (bf16[32,1536]{1,0:T(8,128)(2,1)}, bf16[32,1536]{1,0:T(8,128)(2,1)S(1)}, u32[]{:S(2)}, u32[]{:S(2)}) collective-permute-start(bf16[32,1536]{1,0:T(8,128)(2,1)} %refs_1_.3), channel_id=1, source_target_pairs={{0,16},{8,24},{16,0},{24,8},{1,17},{9,25},{17,1},{25,9},{2,18},{10... | collective-permute-start | bytes 294920 | tf_op jit(solution)/shard_map/ppermute | solution.py:75
  5.2 3.0 %collective-permute-start.4 = (bf16[16,6144]{1,0:T(8,128)(2,1)}, bf16[16,6144]{1,0:T(8,128)(2,1)S(1)}, u32[]{:S(2)}, u32[]{:S(2)}) collective-permute-start(bf16[16,6144]{1,0:T(8,128)(2,1)} %refs_2_.3), channel_id=1, source_target_pairs={{0,4},{1,5},{2,6},{3,7},{4,0},{5,1},{6,2},{7,3},{8,12},{9,13},{10,... | collective-permute-start | bytes 589832 | tf_op jit(solution)/shard_map/ppermute | solution.py:79
  8.2 1.6 %collective-permute-start.5 = (bf16[16,6144]{1,0:T(8,128)(2,1)}, bf16[16,6144]{1,0:T(8,128)(2,1)S(1)}, u32[]{:S(2)}, u32[]{:S(2)}) collective-permute-start(bf16[16,6144]{1,0:T(8,128)(2,1)} %refs_2_.3), channel_id=1, source_target_pairs={{0,2},{1,3},{2,0},{3,1},{4,6},{5,7},{6,4},{7,5},{8,10},{9,11},{10,... | collective-permute-start | bytes 589832 | tf_op jit(solution)/shard_map/ppermute | solution.py:79
  10.0 0.9 %collective-permute-done.2.refs_4_ = bf16[32,1536]{1,0:T(8,128)(2,1)S(1)} collective-permute-done((bf16[32,1536]{1,0:T(8,128)(2,1)}, bf16[32,1536]{1,0:T(8,128)(2,1)S(1)}, u32[]{:S(2)}, u32[]{:S(2)}) %collective-permute-start.2) | collective-permute-done | bytes 98336 | tf_op jit(solution)/shard_map/ppermute | solution.py:75
  10.9 6.7 %hidden_grad.2 = (f32[64,3072]{1,0:T(8,128)S(1)}, bf16[64,3072]{1,0:T(8,128)(2,1)S(1)}, bf16[128,1536]{1,0:T(8,128)(2,1)S(1)}, bf16[1536,128]{1,0:T(8,128)(2,1)S(1)}) custom-call(s32[5]{0:T(128)S(1)} %stack.28.refs_0_.place_ref, bf16[32,1536]{1,0:T(8,128)(2,1)S(1)} %copy-done.1, bf16[32,1536]{1,0:T(8,128)(2,1)S(1)} %collective-permute-done.refs_2_, ...), custom_call_target="tpu_custom_call" | custom-call | flops 80000000 | tf_op jit(solution)/shard_map/hidden_grad/pallas_call | solution.py:171
  17.7 1.6 %collective-permute-start.10 = (bf16[16,6144]{1,0:T(8,128)(2,1)S(1)}, bf16[16,6144]{1,0:T(8,128)(2,1)S(1)}, u32[]{:S(2)}, u32[]{:S(2)}) collective-permute-start(bf16[16,6144]{1,0:T(8,128)(2,1)S(1)} %collective-permute-done.4.refs_1_), channel_id=1, source_target_pairs={{0,2},{1,3},{2,0},{3,1},{4,6},{5,7},{6,4},{7,5},{8,10},{9,11},{10,... | collective-permute-start | bytes 589832 | tf_op jit(solution)/shard_map/ppermute | solution.py:79
  19.5 1.6 %collective-permute-start.6 = (bf16[32,3072]{1,0:T(8,128)(2,1)S(1)}, bf16[32,3072]{1,0:T(8,128)(2,1)S(1)}, u32[]{:S(2)}, u32[]{:S(2)}) collective-permute-start(bf16[32,3072]{1,0:T(8,128)(2,1)S(1)} %get-tuple-element.35.refs_2_), channel_id=1, source_target_pairs={{0,2},{1,3},{2,0},{3,1},{4,6},{5,7},{6,4},{7,5},{8,10},{9,11},{10,... | collective-permute-start | bytes 589832 | tf_op jit(solution)/shard_map/ppermute | solution.py:79
  21.1 6.1 %hidden_grad.3 = (f32[64,3072]{1,0:T(8,128)S(1)}, bf16[64,3072]{1,0:T(8,128)(2,1)S(1)}) custom-call(bf16[1536,128]{1,0:T(8,128)(2,1)S(1)} %get-tuple-element.36.refs_0_, bf16[6144,1536]{1,0:T(8,128)(2,1)} %refs_1_.4, bf16[32,3072]{1,0:T(8,128)(2,1)S(1)} %get-tuple-element.35.refs_2_), custom_call_target="tpu_custom_call" | custom-call | flops 8000000000 | tf_op jit(solution)/shard_map/hidden_grad/pallas_call | solution.py:171
  27.4 1.8 %collective-permute-done.6.refs_1_ = bf16[32,3072]{1,0:T(8,128)(2,1)S(1)} collective-permute-done((bf16[32,3072]{1,0:T(8,128)(2,1)S(1)}, bf16[32,3072]{1,0:T(8,128)(2,1)S(1)}, u32[]{:S(2)}, u32[]{:S(2)}) %collective-permute-start.6) | collective-permute-done | bytes 196640 | tf_op jit(solution)/shard_map/ppermute | solution.py:79
  29.3 2.7 %collective-permute-start.9 = (bf16[16,3072]{1,0:T(8,128)(2,1)S(1)}, bf16[16,3072]{1,0:T(8,128)(2,1)S(1)}, u32[]{:S(2)}, u32[]{:S(2)}) collective-permute-start(bf16[16,3072]{1,0:T(8,128)(2,1)S(1)} %get-tuple-element.42), channel_id=1, source_target_pairs={{0,4},{1,5},{2,6},{3,7},{4,0},{5,1},{6,2},{7,3},{8,12},{9,13},{10,... | collective-permute-start | bytes 294920 | tf_op jit(solution)/shard_map/ppermute | solution.py:79
  32.0 1.6 %collective-permute-start.8 = (bf16[32,3072]{1,0:T(8,128)(2,1)S(1)}, bf16[32,3072]{1,0:T(8,128)(2,1)S(1)}, u32[]{:S(2)}, u32[]{:S(2)}) collective-permute-start(bf16[32,3072]{1,0:T(8,128)(2,1)S(1)} %get-tuple-element.40.refs_4_), channel_id=1, source_target_pairs={{0,2},{1,3},{2,0},{3,1},{4,6},{5,7},{6,4},{7,5},{8,10},{9,11},{10,... | collective-permute-start | bytes 589832 | tf_op jit(solution)/shard_map/ppermute | solution.py:79
  33.7 3.4 %collective-permute-done.9.refs_1_ = bf16[16,3072]{1,0:T(8,128)(2,1)S(1)} collective-permute-done((bf16[16,3072]{1,0:T(8,128)(2,1)S(1)}, bf16[16,3072]{1,0:T(8,128)(2,1)S(1)}, u32[]{:S(2)}, u32[]{:S(2)}) %collective-permute-start.9) | collective-permute-done | bytes 98336 | tf_op jit(solution)/shard_map/ppermute | solution.py:79
  37.2 1.5 %collective-permute-start.16 = (bf16[16,3072]{1,0:T(8,128)(2,1)S(1)}, bf16[16,3072]{1,0:T(8,128)(2,1)S(1)}, u32[]{:S(2)}, u32[]{:S(2)}) collective-permute-start(bf16[16,3072]{1,0:T(8,128)(2,1)S(1)} %far_slope.2.refs_2_.refs_0_), channel_id=1, source_target_pairs={{0,4},{1,5},{2,6},{3,7},{4,0},{5,1},{6,2},{7,3},{8,12},{9,13},{10,... | collective-permute-start | bytes 294920 | tf_op jit(solution)/shard_map/ppermute | solution.py:79
  38.8 0.6 collective-permute-start.12
  39.4 1.0 %collective-permute-start.13 = (bf16[32,1536]{1,0:T(8,128)(2,1)S(1)}, bf16[32,1536]{1,0:T(8,128)(2,1)S(1)}, u32[]{:S(2)}, u32[]{:S(2)}) collective-permute-start(bf16[32,1536]{1,0:T(8,128)(2,1)S(1)} %stack.30.refs_4_.p0), channel_id=1, source_target_pairs={{0,16},{8,24},{16,0},{24,8},{1,17},{9,25},{17,1},{25,9},{2,18},{10... | collective-permute-start | bytes 294920 | tf_op jit(solution)/shard_map/ppermute | solution.py:75
  40.9 1.4 %collective-permute-start.14 = (bf16[32,1536]{1,0:T(8,128)(2,1)S(1)}, bf16[32,1536]{1,0:T(8,128)(2,1)S(1)}, u32[]{:S(2)}, u32[]{:S(2)}) collective-permute-start(bf16[32,1536]{1,0:T(8,128)(2,1)S(1)} %stack.30.refs_4_.p0), channel_id=1, source_target_pairs={{0,24},{8,16},{16,8},{24,0},{1,25},{9,17},{17,9},{25,1},{2,26},{10... | collective-permute-start | bytes 294920 | tf_op jit(solution)/shard_map/ppermute | solution.py:75
  42.3 1.5 %collective-permute-start.11 = (bf16[16,3072]{1,0:T(8,128)(2,1)S(1)}, bf16[16,3072]{1,0:T(8,128)(2,1)S(1)}, u32[]{:S(2)}, u32[]{:S(2)}) collective-permute-start(bf16[16,3072]{1,0:T(8,128)(2,1)S(1)} %get-tuple-element.44.refs_3_), channel_id=1, source_target_pairs={{0,4},{1,5},{2,6},{3,7},{4,0},{5,1},{6,2},{7,3},{8,12},{9,13},{10,... | collective-permute-start | bytes 294920 | tf_op jit(solution)/shard_map/ppermute | solution.py:79
  43.8 2.3 %out_weight_grad.4 = (bf16[6144,1536]{1,0:T(8,128)(2,1)}, f32[8,128]{1,0:T(8,128)S(1)}) custom-call(bf16[64,6144]{1,0:T(8,128)(2,1)S(1)} %stack.31.refs_3_.refs_0_, bf16[64,6144]{1,0:T(8,128)(2,1)S(1)} %collective-permute-done.15.refs_1_, bf16[128,1536]{1,0:T(8,128)(2,1)S(1)} %get-tuple-element.45.refs_2_, bf16[16,3072]{1,0:T(8,128)(2,1)S(1)} %get-tuple-element.44.refs_3_), custom_call_target="tpu_custom_call" | custom-call | flops 80000000 | tf_op jit(solution)/shard_map/out_weight_grad/pallas_call | solution.py:296
  46.2 1.1 %collective-permute-start.18 = (bf16[32,3072]{1,0:T(8,128)(2,1)S(1)}, bf16[32,3072]{1,0:T(8,128)(2,1)S(1)}, u32[]{:S(2)}, u32[]{:S(2)}) collective-permute-start(bf16[32,3072]{1,0:T(8,128)(2,1)S(1)} %stack.32.refs_4_.refs_0_), channel_id=1, source_target_pairs={{0,2},{1,3},{2,0},{3,1},{4,6},{5,7},{6,4},{7,5},{8,10},{9,11},{10,... | collective-permute-start | bytes 589832 | tf_op jit(solution)/shard_map/ppermute | solution.py:79
  47.4 4.6 %out_weight_grad.5 = (bf16[6144,1536]{1,0:T(8,128)(2,1)}, f32[8,128]{1,0:T(8,128)S(1)}) custom-call(bf16[64,6144]{1,0:T(8,128)(2,1)S(1)} %stack.31.refs_3_.refs_0_, bf16[64,6144]{1,0:T(8,128)(2,1)S(1)} %collective-permute-done.15.refs_1_, bf16[128,1536]{1,0:T(8,128)(2,1)S(1)} %get-tuple-element.45.refs_2_, ...), custom_call_target="tpu_custom_call", output_to_operand_aliasing={{0}: (3, {})} | custom-call | flops 8000000000 | tf_op jit(solution)/shard_map/out_weight_grad/pallas_call | solution.py:296
  53.4 2.8 %collective-permute-start.17 = (bf16[16,3072]{1,0:T(8,128)(2,1)S(1)}, bf16[16,3072]{1,0:T(8,128)(2,1)S(1)}, u32[]{:S(2)}, u32[]{:S(2)}) collective-permute-start(bf16[16,3072]{1,0:T(8,128)(2,1)S(1)} %far_slope.3.refs_1_.refs_0_), channel_id=1, source_target_pairs={{0,4},{1,5},{2,6},{3,7},{4,0},{5,1},{6,2},{7,3},{8,12},{9,13},{10,... | collective-permute-start | bytes 294920 | tf_op jit(solution)/shard_map/ppermute | solution.py:79
  56.3 4.3 %in_weight_grad.2 = (bf16[6144,1536]{1,0:T(8,128)(2,1)}, f32[8,128]{1,0:T(8,128)S(1)}) custom-call(bf16[32,3072]{1,0:T(8,128)(2,1)S(1)} %stack.32.refs_4_.refs_0_, bf16[32,3072]{1,0:T(8,128)(2,1)S(1)} %tie.2.refs_0_.refs_1_, bf16[32,3072]{1,0:T(8,128)(2,1)S(1)} %collective-permute-done.19.refs_2_, bf16[32,3072]{1,0:T(8,128)(2,1)S(1)} %collective-permute-done.20.refs_3_, ...), custom_call_target="tpu_custom_call" | custom-call | flops 80000000 | tf_op jit(solution)/shard_map/in_weight_grad/pallas_call | solution.py:296
  60.6 0.8 collective-permute-done.17.refs_1_
  61.5 3.4 %out_weight_grad.6 = (bf16[6144,1536]{1,0:T(8,128)(2,1)}, f32[8,128]{1,0:T(8,128)S(1)}) custom-call(bf16[64,6144]{1,0:T(8,128)(2,1)S(1)} %stack.31.refs_3_.refs_0_, bf16[64,6144]{1,0:T(8,128)(2,1)S(1)} %collective-permute-done.15.refs_1_, bf16[128,1536]{1,0:T(8,128)(2,1)S(1)} %get-tuple-element.45.refs_2_, ...), custom_call_target="tpu_custom_call", output_to_operand_aliasing={{0}: (3, {})} | custom-call | flops 80000000 | tf_op jit(solution)/shard_map/out_weight_grad/pallas_call | solution.py:296
  64.9 1.4 %token_grad.2.refs_1_.refs_6_ = f32[128,1536]{1,0:T(8,128)S(1)} custom-call(bf16[32,3072]{1,0:T(8,128)(2,1)S(1)} %stack.32.refs_4_.refs_0_, bf16[32,3072]{1,0:T(8,128)(2,1)S(1)} %tie.2.refs_0_.refs_1_, bf16[32,3072]{1,0:T(8,128)(2,1)S(1)} %collective-permute-done.19.refs_2_, bf16[32,3072]{1,0:T(8,128)(2,1)S(1)} %collective-permute-done.20.refs_3_, ...), custom_call_target="tpu_custom_call" | custom-call | flops 8000000000 | tf_op jit(solution)/shard_map/token_grad/pallas_call | solution.py:353
  66.3 1.8 %collective-permute-done.21.refs_0_ = bf16[32,3072]{1,0:T(8,128)(2,1)S(1)} collective-permute-done((bf16[32,3072]{1,0:T(8,128)(2,1)S(1)}, bf16[32,3072]{1,0:T(8,128)(2,1)S(1)}, u32[]{:S(2)}, u32[]{:S(2)}) %collective-permute-start.21) | collective-permute-done | bytes 196640 | tf_op jit(solution)/shard_map/ppermute | solution.py:79
  68.1 1.8 %out_weight_grad.7 = (bf16[6144,1536]{1,0:T(8,128)(2,1)}, f32[8,128]{1,0:T(8,128)S(1)}) custom-call(bf16[64,6144]{1,0:T(8,128)(2,1)S(1)} %stack.31.refs_3_.refs_0_, bf16[64,6144]{1,0:T(8,128)(2,1)S(1)} %collective-permute-done.15.refs_1_, bf16[128,1536]{1,0:T(8,128)(2,1)S(1)} %get-tuple-element.45.refs_2_, ...), custom_call_target="tpu_custom_call", output_to_operand_aliasing={{0}: (3, {})} | custom-call | flops 8000000000 | tf_op jit(solution)/shard_map/out_weight_grad/pallas_call | solution.py:296
  69.9 2.0 %token_grad.3 = (f32[32,1536]{1,0:T(8,128)S(1)}, bf16[32,1536]{1,0:T(8,128)(2,1)S(1)}, bf16[32,1536]{1,0:T(8,128)(2,1)S(1)}, bf16[32,1536]{1,0:T(8,128)(2,1)S(1)}) custom-call(s32[5]{0:T(128)S(1)} %stack.28.refs_0_.place_ref, bf16[32,3072]{1,0:T(8,128)(2,1)S(1)} %stack.33.refs_4_.refs_1_.refs_0_, bf16[32,3072]{1,0:T(8,128)(2,1)S(1)} %tie.3.refs_4_.refs_2_.refs_1_, ...), custom_call_target="tpu_custom_call" | custom-call | flops 8000000000 | tf_op jit(solution)/shard_map/token_grad/pallas_call | solution.py:353
  72.9 2.5 %collective-permute-start.26 = (bf16[32,1536]{1,0:T(8,128)(2,1)S(1)}, bf16[32,1536]{1,0:T(8,128)(2,1)S(1)}, u32[]{:S(2)}, u32[]{:S(2)}) collective-permute-start(bf16[32,1536]{1,0:T(8,128)(2,1)S(1)} %get-tuple-element.57), channel_id=1, source_target_pairs={{0,24},{8,16},{16,8},{24,0},{1,25},{9,17},{17,9},{25,1},{2,26},{10... | collective-permute-start | bytes 294920 | tf_op jit(solution)/shard_map/ppermute | solution.py:75
  75.4 4.9 %in_weight_grad.3 = (bf16[6144,1536]{1,0:T(8,128)(2,1)}, f32[8,128]{1,0:T(8,128)}) custom-call(bf16[32,3072]{1,0:T(8,128)(2,1)S(1)} %stack.33.refs_4_.refs_1_.refs_0_, bf16[32,3072]{1,0:T(8,128)(2,1)S(1)} %tie.3.refs_4_.refs_2_.refs_1_, bf16[32,3072]{1,0:T(8,128)(2,1)S(1)} %collective-permute-done.22.refs_3_.refs_2_, ...), custom_call_target="tpu_custom_call", output_to_operand_aliasing={{0}: (5, {})} | custom-call | flops 8000000000 | tf_op jit(solution)/shard_map/in_weight_grad/pallas_call | solution.py:296
  80.3 0.7 add_convert_fusion
  (74 shorter events, 4.0 us)
Async XLA Ops:
  0.6 9.4 %collective-permute-start = (bf16[32,1536]{1,0:T(8,128)(2,1)}, bf16[32,1536]{1,0:T(8,128)(2,1)S(1)}, u32[]{:S(2)}, u32[]{:S(2)}) collective-permute-start(bf16[32,1536]{1,0:T(8,128)(2,1)} %refs_1_.3), channel_id=1, source_target_pairs={{0,8},{8,0},{16,24},{24,16},{1,9},{9,1},{17,25},{25,17},{2,10},{10... | collective-permute-start | bytes 294920 | tf_op jit(solution)/shard_map/ppermute | solution.py:75
  3.6 6.4 %collective-permute-start.1 = (bf16[32,1536]{1,0:T(8,128)(2,1)}, bf16[32,1536]{1,0:T(8,128)(2,1)S(1)}, u32[]{:S(2)}, u32[]{:S(2)}) collective-permute-start(bf16[32,1536]{1,0:T(8,128)(2,1)} %refs_1_.3), channel_id=1, source_target_pairs={{0,16},{8,24},{16,0},{24,8},{1,17},{9,25},{17,1},{25,9},{2,18},{10... | collective-permute-start | bytes 294920 | tf_op jit(solution)/shard_map/ppermute | solution.py:75
  5.2 5.7 %collective-permute-start.2 = (bf16[32,1536]{1,0:T(8,128)(2,1)}, bf16[32,1536]{1,0:T(8,128)(2,1)S(1)}, u32[]{:S(2)}, u32[]{:S(2)}) collective-permute-start(bf16[32,1536]{1,0:T(8,128)(2,1)} %refs_1_.3), channel_id=1, source_target_pairs={{0,24},{8,16},{16,8},{24,0},{1,25},{9,17},{17,9},{25,1},{2,26},{10... | collective-permute-start | bytes 294920 | tf_op jit(solution)/shard_map/ppermute | solution.py:75
  5.2 12.5 %collective-permute-start.4 = (bf16[16,6144]{1,0:T(8,128)(2,1)}, bf16[16,6144]{1,0:T(8,128)(2,1)S(1)}, u32[]{:S(2)}, u32[]{:S(2)}) collective-permute-start(bf16[16,6144]{1,0:T(8,128)(2,1)} %refs_2_.3), channel_id=1, source_target_pairs={{0,4},{1,5},{2,6},{3,7},{4,0},{5,1},{6,2},{7,3},{8,12},{9,13},{10,... | collective-permute-start | bytes 589832 | tf_op jit(solution)/shard_map/ppermute | solution.py:79
  8.2 11.1 %collective-permute-start.5 = (bf16[16,6144]{1,0:T(8,128)(2,1)}, bf16[16,6144]{1,0:T(8,128)(2,1)S(1)}, u32[]{:S(2)}, u32[]{:S(2)}) collective-permute-start(bf16[16,6144]{1,0:T(8,128)(2,1)} %refs_2_.3), channel_id=1, source_target_pairs={{0,2},{1,3},{2,0},{3,1},{4,6},{5,7},{6,4},{7,5},{8,10},{9,11},{10,... | collective-permute-start | bytes 589832 | tf_op jit(solution)/shard_map/ppermute | solution.py:79
  9.8 9.5 %copy-start = (bf16[16,6144]{1,0:T(8,128)(2,1)S(1)}, bf16[16,6144]{1,0:T(8,128)(2,1)}, u32[]{:S(2)}) copy-start(bf16[16,6144]{1,0:T(8,128)(2,1)} %refs_2_.3) | copy-start | bytes 589828
  17.6 1.8 %collective-permute-start.3 = (bf16[64,3072]{1,0:T(8,128)(2,1)S(1)}, bf16[64,3072]{1,0:T(8,128)(2,1)S(1)}, u32[]{:S(2)}, u32[]{:S(2)}) collective-permute-start(bf16[64,3072]{1,0:T(8,128)(2,1)S(1)} %get-tuple-element.33.refs_3_), channel_id=1, source_target_pairs={{0,1},{1,0},{2,3},{3,2},{4,5},{5,4},{6,7},{7,6},{8,9},{9,8},{10,11... | collective-permute-start | bytes 1179656 | tf_op jit(solution)/shard_map/ppermute | solution.py:83
  17.7 15.9 %collective-permute-start.10 = (bf16[16,6144]{1,0:T(8,128)(2,1)S(1)}, bf16[16,6144]{1,0:T(8,128)(2,1)S(1)}, u32[]{:S(2)}, u32[]{:S(2)}) collective-permute-start(bf16[16,6144]{1,0:T(8,128)(2,1)S(1)} %collective-permute-done.4.refs_1_), channel_id=1, source_target_pairs={{0,2},{1,3},{2,0},{3,1},{4,6},{5,7},{6,4},{7,5},{8,10},{9,11},{10,... | collective-permute-start | bytes 589832 | tf_op jit(solution)/shard_map/ppermute | solution.py:79
  19.5 9.7 %collective-permute-start.6 = (bf16[32,3072]{1,0:T(8,128)(2,1)S(1)}, bf16[32,3072]{1,0:T(8,128)(2,1)S(1)}, u32[]{:S(2)}, u32[]{:S(2)}) collective-permute-start(bf16[32,3072]{1,0:T(8,128)(2,1)S(1)} %get-tuple-element.35.refs_2_), channel_id=1, source_target_pairs={{0,2},{1,3},{2,0},{3,1},{4,6},{5,7},{6,4},{7,5},{8,10},{9,11},{10,... | collective-permute-start | bytes 589832 | tf_op jit(solution)/shard_map/ppermute | solution.py:79
  27.3 1.9 %collective-permute-start.7 = (bf16[64,3072]{1,0:T(8,128)(2,1)S(1)}, bf16[64,3072]{1,0:T(8,128)(2,1)S(1)}, u32[]{:S(2)}, u32[]{:S(2)}) collective-permute-start(bf16[64,3072]{1,0:T(8,128)(2,1)S(1)} %get-tuple-element.38.refs_1_), channel_id=1, source_target_pairs={{0,1},{1,0},{2,3},{3,2},{4,5},{5,4},{6,7},{7,6},{8,9},{9,8},{10,11... | collective-permute-start | bytes 1179656 | tf_op jit(solution)/shard_map/ppermute | solution.py:83
  29.3 7.8 %collective-permute-start.9 = (bf16[16,3072]{1,0:T(8,128)(2,1)S(1)}, bf16[16,3072]{1,0:T(8,128)(2,1)S(1)}, u32[]{:S(2)}, u32[]{:S(2)}) collective-permute-start(bf16[16,3072]{1,0:T(8,128)(2,1)S(1)} %get-tuple-element.42), channel_id=1, source_target_pairs={{0,4},{1,5},{2,6},{3,7},{4,0},{5,1},{6,2},{7,3},{8,12},{9,13},{10,... | collective-permute-start | bytes 294920 | tf_op jit(solution)/shard_map/ppermute | solution.py:79
  32.0 8.9 %collective-permute-start.8 = (bf16[32,3072]{1,0:T(8,128)(2,1)S(1)}, bf16[32,3072]{1,0:T(8,128)(2,1)S(1)}, u32[]{:S(2)}, u32[]{:S(2)}) collective-permute-start(bf16[32,3072]{1,0:T(8,128)(2,1)S(1)} %get-tuple-element.40.refs_4_), channel_id=1, source_target_pairs={{0,2},{1,3},{2,0},{3,1},{4,6},{5,7},{6,4},{7,5},{8,10},{9,11},{10,... | collective-permute-start | bytes 589832 | tf_op jit(solution)/shard_map/ppermute | solution.py:79
  33.6 8.7 %collective-permute-start.15 = (bf16[64,6144]{1,0:T(8,128)(2,1)S(1)}, bf16[64,6144]{1,0:T(8,128)(2,1)S(1)}, u32[]{:S(2)}, u32[]{:S(2)}) collective-permute-start(bf16[64,6144]{1,0:T(8,128)(2,1)S(1)} %stack.31.refs_3_.refs_0_), channel_id=1, source_target_pairs={{0,1},{1,0},{2,3},{3,2},{4,5},{5,4},{6,7},{7,6},{8,9},{9,8},{10,11... | collective-permute-start | bytes 2359304 | tf_op jit(solution)/shard_map/ppermute | solution.py:83
  37.2 8.9 %collective-permute-start.16 = (bf16[16,3072]{1,0:T(8,128)(2,1)S(1)}, bf16[16,3072]{1,0:T(8,128)(2,1)S(1)}, u32[]{:S(2)}, u32[]{:S(2)}) collective-permute-start(bf16[16,3072]{1,0:T(8,128)(2,1)S(1)} %far_slope.2.refs_2_.refs_0_), channel_id=1, source_target_pairs={{0,4},{1,5},{2,6},{3,7},{4,0},{5,1},{6,2},{7,3},{8,12},{9,13},{10,... | collective-permute-start | bytes 294920 | tf_op jit(solution)/shard_map/ppermute | solution.py:79
  38.8 13.1 %collective-permute-start.12 = (bf16[32,1536]{1,0:T(8,128)(2,1)S(1)}, bf16[32,1536]{1,0:T(8,128)(2,1)S(1)}, u32[]{:S(2)}, u32[]{:S(2)}) collective-permute-start(bf16[32,1536]{1,0:T(8,128)(2,1)S(1)} %stack.30.refs_4_.p0), channel_id=1, source_target_pairs={{0,8},{8,0},{16,24},{24,16},{1,9},{9,1},{17,25},{25,17},{2,10},{10... | collective-permute-start | bytes 294920 | tf_op jit(solution)/shard_map/ppermute | solution.py:75
  39.4 12.6 %collective-permute-start.13 = (bf16[32,1536]{1,0:T(8,128)(2,1)S(1)}, bf16[32,1536]{1,0:T(8,128)(2,1)S(1)}, u32[]{:S(2)}, u32[]{:S(2)}) collective-permute-start(bf16[32,1536]{1,0:T(8,128)(2,1)S(1)} %stack.30.refs_4_.p0), channel_id=1, source_target_pairs={{0,16},{8,24},{16,0},{24,8},{1,17},{9,25},{17,1},{25,9},{2,18},{10... | collective-permute-start | bytes 294920 | tf_op jit(solution)/shard_map/ppermute | solution.py:75
  40.9 11.1 %collective-permute-start.14 = (bf16[32,1536]{1,0:T(8,128)(2,1)S(1)}, bf16[32,1536]{1,0:T(8,128)(2,1)S(1)}, u32[]{:S(2)}, u32[]{:S(2)}) collective-permute-start(bf16[32,1536]{1,0:T(8,128)(2,1)S(1)} %stack.30.refs_4_.p0), channel_id=1, source_target_pairs={{0,24},{8,16},{16,8},{24,0},{1,25},{9,17},{17,9},{25,1},{2,26},{10... | collective-permute-start | bytes 294920 | tf_op jit(solution)/shard_map/ppermute | solution.py:75
  42.3 10.3 %collective-permute-start.11 = (bf16[16,3072]{1,0:T(8,128)(2,1)S(1)}, bf16[16,3072]{1,0:T(8,128)(2,1)S(1)}, u32[]{:S(2)}, u32[]{:S(2)}) collective-permute-start(bf16[16,3072]{1,0:T(8,128)(2,1)S(1)} %get-tuple-element.44.refs_3_), channel_id=1, source_target_pairs={{0,4},{1,5},{2,6},{3,7},{4,0},{5,1},{6,2},{7,3},{8,12},{9,13},{10,... | collective-permute-start | bytes 294920 | tf_op jit(solution)/shard_map/ppermute | solution.py:79
  46.2 10.1 %slice-start = ((s8[18874368]{0:T(1024)(128)(4,1)}), s8[4194304]{0:T(1024)(128)(4,1)S(1)}, s32[]{:S(2)}) async-start(s8[18874368]{0:T(1024)(128)(4,1)} %bitcast.5), calls=%async_computation | async-start | bytes 8388608
  46.2 10.1 %slice-start.1 = ((s8[18874368]{0:T(1024)(128)(4,1)}), s8[4194304]{0:T(1024)(128)(4,1)S(1)}, s32[]{:S(2)}) async-start(s8[18874368]{0:T(1024)(128)(4,1)} %bitcast.5), calls=%async_computation.1 | async-start | bytes 8388608
  46.2 10.0 %slice-start.2 = ((s8[18874368]{0:T(1024)(128)(4,1)}), s8[4194304]{0:T(1024)(128)(4,1)S(1)}, s32[]{:S(2)}) async-start(s8[18874368]{0:T(1024)(128)(4,1)} %bitcast.5), calls=%async_computation.2 | async-start | bytes 8388608
  46.2 6.6 %collective-permute-start.18 = (bf16[32,3072]{1,0:T(8,128)(2,1)S(1)}, bf16[32,3072]{1,0:T(8,128)(2,1)S(1)}, u32[]{:S(2)}, u32[]{:S(2)}) collective-permute-start(bf16[32,3072]{1,0:T(8,128)(2,1)S(1)} %stack.32.refs_4_.refs_0_), channel_id=1, source_target_pairs={{0,2},{1,3},{2,0},{3,1},{4,6},{5,7},{6,4},{7,5},{8,10},{9,11},{10,... | collective-permute-start | bytes 589832 | tf_op jit(solution)/shard_map/ppermute | solution.py:79
  47.4 8.9 %slice-start.4 = ((s8[18874368]{0:T(1024)(128)(4,1)}), s8[2097152]{0:T(1024)(128)(4,1)S(1)}, s32[]{:S(2)}) async-start(s8[18874368]{0:T(1024)(128)(4,1)} %bitcast.5), calls=%async_computation.4 | async-start | bytes 4194304
  51.9 4.3 %collective-permute-start.19 = (bf16[32,3072]{1,0:T(8,128)(2,1)S(1)}, bf16[32,3072]{1,0:T(8,128)(2,1)S(1)}, u32[]{:S(2)}, u32[]{:S(2)}) collective-permute-start(bf16[32,3072]{1,0:T(8,128)(2,1)S(1)} %stack.32.refs_4_.refs_0_), channel_id=1, source_target_pairs={{0,1},{1,0},{2,3},{3,2},{4,5},{5,4},{6,7},{7,6},{8,9},{9,8},{10,11... | collective-permute-start | bytes 589832 | tf_op jit(solution)/shard_map/ppermute | solution.py:83
  52.8 3.5 %collective-permute-start.20 = (bf16[32,3072]{1,0:T(8,128)(2,1)S(1)}, bf16[32,3072]{1,0:T(8,128)(2,1)S(1)}, u32[]{:S(2)}, u32[]{:S(2)}) collective-permute-start(bf16[32,3072]{1,0:T(8,128)(2,1)S(1)} %tie.2.refs_0_.refs_1_), channel_id=1, source_target_pairs={{0,1},{1,0},{2,3},{3,2},{4,5},{5,4},{6,7},{7,6},{8,9},{9,8},{10,11... | collective-permute-start | bytes 589832 | tf_op jit(solution)/shard_map/ppermute | solution.py:83
  53.4 8.0 %collective-permute-start.17 = (bf16[16,3072]{1,0:T(8,128)(2,1)S(1)}, bf16[16,3072]{1,0:T(8,128)(2,1)S(1)}, u32[]{:S(2)}, u32[]{:S(2)}) collective-permute-start(bf16[16,3072]{1,0:T(8,128)(2,1)S(1)} %far_slope.3.refs_1_.refs_0_), channel_id=1, source_target_pairs={{0,4},{1,5},{2,6},{3,7},{4,0},{5,1},{6,2},{7,3},{8,12},{9,13},{10,... | collective-permute-start | bytes 294920 | tf_op jit(solution)/shard_map/ppermute | solution.py:79
  61.4 6.7 %collective-permute-start.21 = (bf16[32,3072]{1,0:T(8,128)(2,1)S(1)}, bf16[32,3072]{1,0:T(8,128)(2,1)S(1)}, u32[]{:S(2)}, u32[]{:S(2)}) collective-permute-start(bf16[32,3072]{1,0:T(8,128)(2,1)S(1)} %stack.33.refs_4_.refs_1_.refs_0_), channel_id=1, source_target_pairs={{0,2},{1,3},{2,0},{3,1},{4,6},{5,7},{6,4},{7,5},{8,10},{9,11},{10,... | collective-permute-start | bytes 589832 | tf_op jit(solution)/shard_map/ppermute | solution.py:79
  61.5 8.4 %collective-permute-start.22 = (bf16[32,3072]{1,0:T(8,128)(2,1)S(1)}, bf16[32,3072]{1,0:T(8,128)(2,1)S(1)}, u32[]{:S(2)}, u32[]{:S(2)}) collective-permute-start(bf16[32,3072]{1,0:T(8,128)(2,1)S(1)} %stack.33.refs_4_.refs_1_.refs_0_), channel_id=1, source_target_pairs={{0,1},{1,0},{2,3},{3,2},{4,5},{5,4},{6,7},{7,6},{8,9},{9,8},{10,11... | collective-permute-start | bytes 589832 | tf_op jit(solution)/shard_map/ppermute | solution.py:83
  68.1 1.8 %collective-permute-start.23 = (bf16[32,3072]{1,0:T(8,128)(2,1)S(1)}, bf16[32,3072]{1,0:T(8,128)(2,1)S(1)}, u32[]{:S(2)}, u32[]{:S(2)}) collective-permute-start(bf16[32,3072]{1,0:T(8,128)(2,1)S(1)} %tie.3.refs_4_.refs_2_.refs_1_), channel_id=1, source_target_pairs={{0,1},{1,0},{2,3},{3,2},{4,5},{5,4},{6,7},{7,6},{8,9},{9,8},{10,11... | collective-permute-start | bytes 589832 | tf_op jit(solution)/shard_map/ppermute | solution.py:83
  71.9 8.4 %collective-permute-start.24 = (bf16[32,1536]{1,0:T(8,128)(2,1)S(1)}, bf16[32,1536]{1,0:T(8,128)(2,1)S(1)}, u32[]{:S(2)}, u32[]{:S(2)}) collective-permute-start(bf16[32,1536]{1,0:T(8,128)(2,1)S(1)} %get-tuple-element.55), channel_id=1, source_target_pairs={{0,8},{8,0},{16,24},{24,16},{1,9},{9,1},{17,25},{25,17},{2,10},{10... | collective-permute-start | bytes 294920 | tf_op jit(solution)/shard_map/ppermute | solution.py:75
  72.3 8.0 %collective-permute-start.25 = (bf16[32,1536]{1,0:T(8,128)(2,1)S(1)}, bf16[32,1536]{1,0:T(8,128)(2,1)S(1)}, u32[]{:S(2)}, u32[]{:S(2)}) collective-permute-start(bf16[32,1536]{1,0:T(8,128)(2,1)S(1)} %get-tuple-element.56), channel_id=1, source_target_pairs={{0,16},{8,24},{16,0},{24,8},{1,17},{9,25},{17,1},{25,9},{2,18},{10... | collective-permute-start | bytes 294920 | tf_op jit(solution)/shard_map/ppermute | solution.py:75
  72.9 7.4 %collective-permute-start.26 = (bf16[32,1536]{1,0:T(8,128)(2,1)S(1)}, bf16[32,1536]{1,0:T(8,128)(2,1)S(1)}, u32[]{:S(2)}, u32[]{:S(2)}) collective-permute-start(bf16[32,1536]{1,0:T(8,128)(2,1)S(1)} %get-tuple-element.57), channel_id=1, source_target_pairs={{0,24},{8,16},{16,8},{24,0},{1,25},{9,17},{17,9},{25,1},{2,26},{10... | collective-permute-start | bytes 294920 | tf_op jit(solution)/shard_map/ppermute | solution.py:75
  (3 other events, 17.8 us)

commit v4 on v3

--- a/solution.py
+++ b/solution.py
@@ -265,6 +265,8 @@
     count = len(pieces)
     extra = len(after) + (held is not None)
     parts = cuts(rows, 512)
+    low, high = parts[-1].start, parts[-1].stop
+    parts = parts[:-1] + [slice(low, high - 256), slice(high - 256, high)]
 
     def body(*refs):
         a_refs, x_ref = refs[:count], refs[count]
@@ -448,7 +450,7 @@
     pre = [pre_own, swap_cores(pre_own)]
     grad0 = far_slope(mine0, swap_chips(out0, 2), pre_act, 0, (pre_own,), COST)
     mine1, out1 = add_halves(held1, swap_chips(out1, 1), (grad0,), LIGHT)
-    ends = [units * n // 12 for n in (0, 2, 7, 11, 12)]
+    ends = [units * n // 12 for n in (0, 2, 7, 12)]
     parts = [b - a for a, b in zip(ends[:-1], ends[1:])]
     grad_w_out, token = weight_grad(pre, x, 0, 0, parts[0], units, None, True, (out1,), LIGHT)
     pair0 = stack([grad0, swap_chips(grad0, 2)], (token,))
@@ -470,10 +472,7 @@
     (total,) = token_grad(whole, w_in, 0, None, None, (token,))
     near1 = tie(swap_chips(pair1, 1), (total,))
     whole = [pair1, near1, swap_cores(pair1), swap_cores(near1)]
-    grad_w_out, token = weight_grad(
-        pre, x, 0, ends[3], parts[3], units, grad_w_out, True, (near1,)
-    )
-    part, *parts = token_grad(whole, w_in, per_chunk, total, place, (token,))
+    part, *parts = token_grad(whole, w_in, per_chunk, total, place)
     grad_w_in, _ = weight_grad(
         whole, tok, per_chunk, 0, per_chunk, units, grad_w_in, False, (part,)
     )

time: 81.2 us -> 81.5 us (level)
  waiting for transfers between devices: 9.21 us -> 10.8 us
  Pallas kernels: 38.6 us -> 37.3 us
    ppermute x7, waiting for transfers between devices: 0.02 us -> 1.45 us  [swap_cores(): return lax.ppermute(array, 'col', [(i, i ^ 1) for i in range(8)])]
    pallas_call x6 -> x5, Pallas kernels: 21.1 us -> 19.8 us  [weight_grad(): pl.pallas_call(body, in_specs=[VMEM] * (count + 1) + [ANY] * extra, out_s...]
  transfers between devices with their start and end apart: 27 -> 27, of which waited for: 6 -> 7; matrix products, arithmetic and copies ran while one was open for 0% -> 0% of each run, Pallas kernels for 45% -> 43%
where the time goes in v4:
time: 81.5 us; the launch traced here: 81.4 us
  Pallas kernels  37.3 us (46%)
  starting transfers between devices  31.3 us (38%)
  waiting for transfers between devices  10.8 us (13%)
  between operations  1.13 us (1%)
    pallas_call x5, Pallas kernels, weight_grad(): pl.pallas_call(body, in_specs=[VMEM] * (count + 1) + [ANY] * extra, out_s...  19.8 us
    ppermute x11, starting transfers between devices, swap_chips(): return lax.ppermute(array, 'col', [(i, i ^ 2 * d) for i in range(8)])  18.8 us
    pallas_call x2, Pallas kernels, hidden_grad(): pl.pallas_call(body, in_specs=[SMEM] * join + [VMEM] * pieces + [ANY] * (...  12.8 us
    ppermute x9, starting transfers between devices, swap_rows(): return lax.ppermute(array, 'row', [(r, r ^ d) for r in range(4)])  11.6 us
    ppermute x11, waiting for transfers between devices, swap_chips(): return lax.ppermute(array, 'col', [(i, i ^ 2 * d) for i in range(8)])  8.48 us
    pallas_call x2, Pallas kernels, token_grad(): pl.pallas_call(body, in_specs=[SMEM] * last + [VMEM] * (count + 1 + more)...  3.41 us
  transfers between devices with their start and end apart: 27, of which 7 were waited for; matrix products, arithmetic and copies ran while one was open for 0% of the time, Pallas kernels for 43%

profile of v4, /device:TPU:0, one launch (start us, length us, event | category | flops | bytes accessed | tf_op | source)
XLA Modules:
  0.0 81.4 jit_solution(18032951803817027746)
XLA Ops:
  0.6 3.0 %collective-permute-start.1 = (bf16[32,1536]{1,0:T(8,128)(2,1)}, bf16[32,1536]{1,0:T(8,128)(2,1)S(1)}, u32[]{:S(2)}, u32[]{:S(2)}) collective-permute-start(bf16[32,1536]{1,0:T(8,128)(2,1)} %refs_1_.3), channel_id=1, source_target_pairs={{0,16},{8,24},{16,0},{24,8},{1,17},{9,25},{17,1},{25,9},{2,18},{10... | collective-permute-start | bytes 294920 | tf_op jit(solution)/shard_map/ppermute | solution.py:75
  3.7 1.5 %collective-permute-start = (bf16[32,1536]{1,0:T(8,128)(2,1)}, bf16[32,1536]{1,0:T(8,128)(2,1)S(1)}, u32[]{:S(2)}, u32[]{:S(2)}) collective-permute-start(bf16[32,1536]{1,0:T(8,128)(2,1)} %refs_1_.3), channel_id=1, source_target_pairs={{0,8},{8,0},{16,24},{24,16},{1,9},{9,1},{17,25},{25,17},{2,10},{10... | collective-permute-start | bytes 294920 | tf_op jit(solution)/shard_map/ppermute | solution.py:75
  5.2 2.0 %collective-permute-start.5 = (bf16[16,6144]{1,0:T(8,128)(2,1)}, bf16[16,6144]{1,0:T(8,128)(2,1)S(1)}, u32[]{:S(2)}, u32[]{:S(2)}) collective-permute-start(bf16[16,6144]{1,0:T(8,128)(2,1)} %refs_2_.3), channel_id=1, source_target_pairs={{0,2},{1,3},{2,0},{3,1},{4,6},{5,7},{6,4},{7,5},{8,10},{9,11},{10,... | collective-permute-start | bytes 589832 | tf_op jit(solution)/shard_map/ppermute | solution.py:79
  7.2 2.6 %collective-permute-start.4 = (bf16[16,6144]{1,0:T(8,128)(2,1)}, bf16[16,6144]{1,0:T(8,128)(2,1)S(1)}, u32[]{:S(2)}, u32[]{:S(2)}) collective-permute-start(bf16[16,6144]{1,0:T(8,128)(2,1)} %refs_2_.3), channel_id=1, source_target_pairs={{0,4},{1,5},{2,6},{3,7},{4,0},{5,1},{6,2},{7,3},{8,12},{9,13},{10,... | collective-permute-start | bytes 589832 | tf_op jit(solution)/shard_map/ppermute | solution.py:79
  10.0 0.9 %collective-permute-done.2.refs_4_ = bf16[32,1536]{1,0:T(8,128)(2,1)S(1)} collective-permute-done((bf16[32,1536]{1,0:T(8,128)(2,1)}, bf16[32,1536]{1,0:T(8,128)(2,1)S(1)}, u32[]{:S(2)}, u32[]{:S(2)}) %collective-permute-start.2) | collective-permute-done | bytes 98336 | tf_op jit(solution)/shard_map/ppermute | solution.py:75
  10.9 6.7 %hidden_grad.2 = (f32[64,3072]{1,0:T(8,128)S(1)}, bf16[64,3072]{1,0:T(8,128)(2,1)S(1)}, bf16[128,1536]{1,0:T(8,128)(2,1)S(1)}, bf16[1536,128]{1,0:T(8,128)(2,1)S(1)}) custom-call(s32[5]{0:T(128)S(1)} %stack.28.refs_0_.place_ref, bf16[32,1536]{1,0:T(8,128)(2,1)S(1)} %copy-done.1, bf16[32,1536]{1,0:T(8,128)(2,1)S(1)} %collective-permute-done.refs_2_, ...), custom_call_target="tpu_custom_call" | custom-call | flops 80000000 | tf_op jit(solution)/shard_map/hidden_grad/pallas_call | solution.py:171
  18.1 1.2 %collective-permute-start.10 = (bf16[16,6144]{1,0:T(8,128)(2,1)S(1)}, bf16[16,6144]{1,0:T(8,128)(2,1)S(1)}, u32[]{:S(2)}, u32[]{:S(2)}) collective-permute-start(bf16[16,6144]{1,0:T(8,128)(2,1)S(1)} %collective-permute-done.4.refs_1_), channel_id=1, source_target_pairs={{0,2},{1,3},{2,0},{3,1},{4,6},{5,7},{6,4},{7,5},{8,10},{9,11},{10,... | collective-permute-start | bytes 589832 | tf_op jit(solution)/shard_map/ppermute | solution.py:79
  19.5 1.6 %collective-permute-start.6 = (bf16[32,3072]{1,0:T(8,128)(2,1)S(1)}, bf16[32,3072]{1,0:T(8,128)(2,1)S(1)}, u32[]{:S(2)}, u32[]{:S(2)}) collective-permute-start(bf16[32,3072]{1,0:T(8,128)(2,1)S(1)} %get-tuple-element.33.refs_2_), channel_id=1, source_target_pairs={{0,2},{1,3},{2,0},{3,1},{4,6},{5,7},{6,4},{7,5},{8,10},{9,11},{10,... | collective-permute-start | bytes 589832 | tf_op jit(solution)/shard_map/ppermute | solution.py:79
  21.1 6.1 %hidden_grad.3 = (f32[64,3072]{1,0:T(8,128)S(1)}, bf16[64,3072]{1,0:T(8,128)(2,1)S(1)}) custom-call(bf16[1536,128]{1,0:T(8,128)(2,1)S(1)} %get-tuple-element.34.refs_0_, bf16[6144,1536]{1,0:T(8,128)(2,1)} %refs_1_.4, bf16[32,3072]{1,0:T(8,128)(2,1)S(1)} %get-tuple-element.33.refs_2_), custom_call_target="tpu_custom_call" | custom-call | flops 8000000000 | tf_op jit(solution)/shard_map/hidden_grad/pallas_call | solution.py:171
  27.3 1.8 %collective-permute-done.6.refs_1_ = bf16[32,3072]{1,0:T(8,128)(2,1)S(1)} collective-permute-done((bf16[32,3072]{1,0:T(8,128)(2,1)S(1)}, bf16[32,3072]{1,0:T(8,128)(2,1)S(1)}, u32[]{:S(2)}, u32[]{:S(2)}) %collective-permute-start.6) | collective-permute-done | bytes 196640 | tf_op jit(solution)/shard_map/ppermute | solution.py:79
  29.3 2.7 %collective-permute-start.9 = (bf16[16,3072]{1,0:T(8,128)(2,1)S(1)}, bf16[16,3072]{1,0:T(8,128)(2,1)S(1)}, u32[]{:S(2)}, u32[]{:S(2)}) collective-permute-start(bf16[16,3072]{1,0:T(8,128)(2,1)S(1)} %get-tuple-element.40), channel_id=1, source_target_pairs={{0,4},{1,5},{2,6},{3,7},{4,0},{5,1},{6,2},{7,3},{8,12},{9,13},{10,... | collective-permute-start | bytes 294920 | tf_op jit(solution)/shard_map/ppermute | solution.py:79
  32.0 1.6 %collective-permute-start.8 = (bf16[32,3072]{1,0:T(8,128)(2,1)S(1)}, bf16[32,3072]{1,0:T(8,128)(2,1)S(1)}, u32[]{:S(2)}, u32[]{:S(2)}) collective-permute-start(bf16[32,3072]{1,0:T(8,128)(2,1)S(1)} %get-tuple-element.38.refs_4_), channel_id=1, source_target_pairs={{0,2},{1,3},{2,0},{3,1},{4,6},{5,7},{6,4},{7,5},{8,10},{9,11},{10,... | collective-permute-start | bytes 589832 | tf_op jit(solution)/shard_map/ppermute | solution.py:79
  33.7 3.4 %collective-permute-done.9.refs_1_ = bf16[16,3072]{1,0:T(8,128)(2,1)S(1)} collective-permute-done((bf16[16,3072]{1,0:T(8,128)(2,1)S(1)}, bf16[16,3072]{1,0:T(8,128)(2,1)S(1)}, u32[]{:S(2)}, u32[]{:S(2)}) %collective-permute-start.9) | collective-permute-done | bytes 98336 | tf_op jit(solution)/shard_map/ppermute | solution.py:79
  37.2 1.5 %collective-permute-start.16 = (bf16[16,3072]{1,0:T(8,128)(2,1)S(1)}, bf16[16,3072]{1,0:T(8,128)(2,1)S(1)}, u32[]{:S(2)}, u32[]{:S(2)}) collective-permute-start(bf16[16,3072]{1,0:T(8,128)(2,1)S(1)} %far_slope.2.refs_2_.refs_0_), channel_id=1, source_target_pairs={{0,4},{1,5},{2,6},{3,7},{4,0},{5,1},{6,2},{7,3},{8,12},{9,13},{10,... | collective-permute-start | bytes 294920 | tf_op jit(solution)/shard_map/ppermute | solution.py:79
  38.7 1.7 %collective-permute-start.14 = (bf16[32,1536]{1,0:T(8,128)(2,1)S(1)}, bf16[32,1536]{1,0:T(8,128)(2,1)S(1)}, u32[]{:S(2)}, u32[]{:S(2)}) collective-permute-start(bf16[32,1536]{1,0:T(8,128)(2,1)S(1)} %stack.30.refs_4_.p0), channel_id=1, source_target_pairs={{0,24},{8,16},{16,8},{24,0},{1,25},{9,17},{17,9},{25,1},{2,26},{10... | collective-permute-start | bytes 294920 | tf_op jit(solution)/shard_map/ppermute | solution.py:75
  41.2 1.1 %collective-permute-start.12 = (bf16[32,1536]{1,0:T(8,128)(2,1)S(1)}, bf16[32,1536]{1,0:T(8,128)(2,1)S(1)}, u32[]{:S(2)}, u32[]{:S(2)}) collective-permute-start(bf16[32,1536]{1,0:T(8,128)(2,1)S(1)} %stack.30.refs_4_.p0), channel_id=1, source_target_pairs={{0,8},{8,0},{16,24},{24,16},{1,9},{9,1},{17,25},{25,17},{2,10},{10... | collective-permute-start | bytes 294920 | tf_op jit(solution)/shard_map/ppermute | solution.py:75
  42.3 1.5 %collective-permute-start.11 = (bf16[16,3072]{1,0:T(8,128)(2,1)S(1)}, bf16[16,3072]{1,0:T(8,128)(2,1)S(1)}, u32[]{:S(2)}, u32[]{:S(2)}) collective-permute-start(bf16[16,3072]{1,0:T(8,128)(2,1)S(1)} %get-tuple-element.42.refs_3_), channel_id=1, source_target_pairs={{0,4},{1,5},{2,6},{3,7},{4,0},{5,1},{6,2},{7,3},{8,12},{9,13},{10,... | collective-permute-start | bytes 294920 | tf_op jit(solution)/shard_map/ppermute | solution.py:79
  43.8 2.3 %out_weight_grad.3 = (bf16[6144,1536]{1,0:T(8,128)(2,1)}, f32[8,128]{1,0:T(8,128)S(1)}) custom-call(bf16[64,6144]{1,0:T(8,128)(2,1)S(1)} %stack.31.refs_3_.refs_0_, bf16[64,6144]{1,0:T(8,128)(2,1)S(1)} %collective-permute-done.15.refs_1_, bf16[128,1536]{1,0:T(8,128)(2,1)S(1)} %get-tuple-element.43.refs_2_, bf16[16,3072]{1,0:T(8,128)(2,1)S(1)} %get-tuple-element.42.refs_3_), custom_call_target="tpu_custom_call" | custom-call | flops 80000000 | tf_op jit(solution)/shard_map/out_weight_grad/pallas_call | solution.py:298
  46.2 1.2 %collective-permute-start.18 = (bf16[32,3072]{1,0:T(8,128)(2,1)S(1)}, bf16[32,3072]{1,0:T(8,128)(2,1)S(1)}, u32[]{:S(2)}, u32[]{:S(2)}) collective-permute-start(bf16[32,3072]{1,0:T(8,128)(2,1)S(1)} %stack.32.refs_4_.refs_0_), channel_id=1, source_target_pairs={{0,2},{1,3},{2,0},{3,1},{4,6},{5,7},{6,4},{7,5},{8,10},{9,11},{10,... | collective-permute-start | bytes 589832 | tf_op jit(solution)/shard_map/ppermute | solution.py:79
  47.3 4.6 %out_weight_grad.4 = (bf16[6144,1536]{1,0:T(8,128)(2,1)}, f32[8,128]{1,0:T(8,128)S(1)}) custom-call(bf16[64,6144]{1,0:T(8,128)(2,1)S(1)} %stack.31.refs_3_.refs_0_, bf16[64,6144]{1,0:T(8,128)(2,1)S(1)} %collective-permute-done.15.refs_1_, bf16[128,1536]{1,0:T(8,128)(2,1)S(1)} %get-tuple-element.43.refs_2_, ...), custom_call_target="tpu_custom_call", output_to_operand_aliasing={{0}: (3, {})} | custom-call | flops 8000000000 | tf_op jit(solution)/shard_map/out_weight_grad/pallas_call | solution.py:298
  53.4 2.8 %collective-permute-start.17 = (bf16[16,3072]{1,0:T(8,128)(2,1)S(1)}, bf16[16,3072]{1,0:T(8,128)(2,1)S(1)}, u32[]{:S(2)}, u32[]{:S(2)}) collective-permute-start(bf16[16,3072]{1,0:T(8,128)(2,1)S(1)} %far_slope.3.refs_1_.refs_0_), channel_id=1, source_target_pairs={{0,4},{1,5},{2,6},{3,7},{4,0},{5,1},{6,2},{7,3},{8,12},{9,13},{10,... | collective-permute-start | bytes 294920 | tf_op jit(solution)/shard_map/ppermute | solution.py:79
  56.3 4.3 %in_weight_grad.2 = (bf16[6144,1536]{1,0:T(8,128)(2,1)}, f32[8,128]{1,0:T(8,128)S(1)}) custom-call(bf16[32,3072]{1,0:T(8,128)(2,1)S(1)} %stack.32.refs_4_.refs_0_, bf16[32,3072]{1,0:T(8,128)(2,1)S(1)} %tie.2.refs_0_.refs_1_, bf16[32,3072]{1,0:T(8,128)(2,1)S(1)} %collective-permute-done.19.refs_2_, bf16[32,3072]{1,0:T(8,128)(2,1)S(1)} %collective-permute-done.20.refs_3_, ...), custom_call_target="tpu_custom_call" | custom-call | flops 80000000 | tf_op jit(solution)/shard_map/in_weight_grad/pallas_call | solution.py:298
  60.6 0.8 collective-permute-done.17.refs_1_
  61.5 3.8 %out_weight_grad.5 = (bf16[6144,1536]{1,0:T(8,128)(2,1)}, f32[8,128]{1,0:T(8,128)S(1)}) custom-call(bf16[64,6144]{1,0:T(8,128)(2,1)S(1)} %stack.31.refs_3_.refs_0_, bf16[64,6144]{1,0:T(8,128)(2,1)S(1)} %collective-permute-done.15.refs_1_, bf16[128,1536]{1,0:T(8,128)(2,1)S(1)} %get-tuple-element.43.refs_2_, ...), custom_call_target="tpu_custom_call", output_to_operand_aliasing={{0}: (3, {})} | custom-call | flops 80000000 | tf_op jit(solution)/shard_map/out_weight_grad/pallas_call | solution.py:298
  65.4 1.4 %token_grad.2.refs_1_.refs_6_ = f32[128,1536]{1,0:T(8,128)S(1)} custom-call(bf16[32,3072]{1,0:T(8,128)(2,1)S(1)} %stack.32.refs_4_.refs_0_, bf16[32,3072]{1,0:T(8,128)(2,1)S(1)} %tie.2.refs_0_.refs_1_, bf16[32,3072]{1,0:T(8,128)(2,1)S(1)} %collective-permute-done.19.refs_2_, bf16[32,3072]{1,0:T(8,128)(2,1)S(1)} %collective-permute-done.20.refs_3_, ...), custom_call_target="tpu_custom_call" | custom-call | flops 8000000000 | tf_op jit(solution)/shard_map/token_grad/pallas_call | solution.py:355
  66.8 2.0 %collective-permute-done.21.refs_0_ = bf16[32,3072]{1,0:T(8,128)(2,1)S(1)} collective-permute-done((bf16[32,3072]{1,0:T(8,128)(2,1)S(1)}, bf16[32,3072]{1,0:T(8,128)(2,1)S(1)}, u32[]{:S(2)}, u32[]{:S(2)}) %collective-permute-start.21) | collective-permute-done | bytes 196640 | tf_op jit(solution)/shard_map/ppermute | solution.py:79
  68.8 1.4 %collective-permute-done.23.refs_4_.refs_3_ = bf16[32,3072]{1,0:T(8,128)(2,1)S(1)} collective-permute-done((bf16[32,3072]{1,0:T(8,128)(2,1)S(1)}, bf16[32,3072]{1,0:T(8,128)(2,1)S(1)}, u32[]{:S(2)}, u32[]{:S(2)}) %collective-permute-start.23) | collective-permute-done | bytes 196640 | tf_op jit(solution)/shard_map/ppermute | solution.py:83
  70.2 2.0 %token_grad.3 = (f32[32,1536]{1,0:T(8,128)S(1)}, bf16[32,1536]{1,0:T(8,128)(2,1)S(1)}, bf16[32,1536]{1,0:T(8,128)(2,1)S(1)}, bf16[32,1536]{1,0:T(8,128)(2,1)S(1)}) custom-call(s32[5]{0:T(128)S(1)} %stack.28.refs_0_.place_ref, bf16[32,3072]{1,0:T(8,128)(2,1)S(1)} %stack.33.refs_4_.refs_1_.refs_0_, bf16[32,3072]{1,0:T(8,128)(2,1)S(1)} %tie.3.refs_2_.refs_1_, ...), custom_call_target="tpu_custom_call" | custom-call | flops 8000000000 | tf_op jit(solution)/shard_map/token_grad/pallas_call | solution.py:355
  72.2 1.0 %collective-permute-start.24 = (bf16[32,1536]{1,0:T(8,128)(2,1)S(1)}, bf16[32,1536]{1,0:T(8,128)(2,1)S(1)}, u32[]{:S(2)}, u32[]{:S(2)}) collective-permute-start(bf16[32,1536]{1,0:T(8,128)(2,1)S(1)} %get-tuple-element.51), channel_id=1, source_target_pairs={{0,8},{8,0},{16,24},{24,16},{1,9},{9,1},{17,25},{25,17},{2,10},{10... | collective-permute-start | bytes 294920 | tf_op jit(solution)/shard_map/ppermute | solution.py:75
  73.3 1.4 %collective-permute-start.25 = (bf16[32,1536]{1,0:T(8,128)(2,1)S(1)}, bf16[32,1536]{1,0:T(8,128)(2,1)S(1)}, u32[]{:S(2)}, u32[]{:S(2)}) collective-permute-start(bf16[32,1536]{1,0:T(8,128)(2,1)S(1)} %get-tuple-element.52), channel_id=1, source_target_pairs={{0,16},{8,24},{16,0},{24,8},{1,17},{9,25},{17,1},{25,9},{2,18},{10... | collective-permute-start | bytes 294920 | tf_op jit(solution)/shard_map/ppermute | solution.py:75
  74.6 1.2 %collective-permute-start.26 = (bf16[32,1536]{1,0:T(8,128)(2,1)S(1)}, bf16[32,1536]{1,0:T(8,128)(2,1)S(1)}, u32[]{:S(2)}, u32[]{:S(2)}) collective-permute-start(bf16[32,1536]{1,0:T(8,128)(2,1)S(1)} %get-tuple-element.53), channel_id=1, source_target_pairs={{0,24},{8,16},{16,8},{24,0},{1,25},{9,17},{17,9},{25,1},{2,26},{10... | collective-permute-start | bytes 294920 | tf_op jit(solution)/shard_map/ppermute | solution.py:75
  75.8 4.9 %in_weight_grad.3 = (bf16[6144,1536]{1,0:T(8,128)(2,1)}, f32[8,128]{1,0:T(8,128)}) custom-call(bf16[32,3072]{1,0:T(8,128)(2,1)S(1)} %stack.33.refs_4_.refs_1_.refs_0_, bf16[32,3072]{1,0:T(8,128)(2,1)S(1)} %tie.3.refs_2_.refs_1_, bf16[32,3072]{1,0:T(8,128)(2,1)S(1)} %collective-permute-done.22.refs_3_.refs_2_, ...), custom_call_target="tpu_custom_call", output_to_operand_aliasing={{0}: (5, {})} | custom-call | flops 8000000000 | tf_op jit(solution)/shard_map/in_weight_grad/pallas_call | solution.py:298
  (73 shorter events, 4.3 us)
Async XLA Ops:
  0.6 9.4 %collective-permute-start.1 = (bf16[32,1536]{1,0:T(8,128)(2,1)}, bf16[32,1536]{1,0:T(8,128)(2,1)S(1)}, u32[]{:S(2)}, u32[]{:S(2)}) collective-permute-start(bf16[32,1536]{1,0:T(8,128)(2,1)} %refs_1_.3), channel_id=1, source_target_pairs={{0,16},{8,24},{16,0},{24,8},{1,17},{9,25},{17,1},{25,9},{2,18},{10... | collective-permute-start | bytes 294920 | tf_op jit(solution)/shard_map/ppermute | solution.py:75
  3.7 6.4 %collective-permute-start = (bf16[32,1536]{1,0:T(8,128)(2,1)}, bf16[32,1536]{1,0:T(8,128)(2,1)S(1)}, u32[]{:S(2)}, u32[]{:S(2)}) collective-permute-start(bf16[32,1536]{1,0:T(8,128)(2,1)} %refs_1_.3), channel_id=1, source_target_pairs={{0,8},{8,0},{16,24},{24,16},{1,9},{9,1},{17,25},{25,17},{2,10},{10... | collective-permute-start | bytes 294920 | tf_op jit(solution)/shard_map/ppermute | solution.py:75
  5.2 5.7 %collective-permute-start.2 = (bf16[32,1536]{1,0:T(8,128)(2,1)}, bf16[32,1536]{1,0:T(8,128)(2,1)S(1)}, u32[]{:S(2)}, u32[]{:S(2)}) collective-permute-start(bf16[32,1536]{1,0:T(8,128)(2,1)} %refs_1_.3), channel_id=1, source_target_pairs={{0,24},{8,16},{16,8},{24,0},{1,25},{9,17},{17,9},{25,1},{2,26},{10... | collective-permute-start | bytes 294920 | tf_op jit(solution)/shard_map/ppermute | solution.py:75
  5.2 14.1 %collective-permute-start.5 = (bf16[16,6144]{1,0:T(8,128)(2,1)}, bf16[16,6144]{1,0:T(8,128)(2,1)S(1)}, u32[]{:S(2)}, u32[]{:S(2)}) collective-permute-start(bf16[16,6144]{1,0:T(8,128)(2,1)} %refs_2_.3), channel_id=1, source_target_pairs={{0,2},{1,3},{2,0},{3,1},{4,6},{5,7},{6,4},{7,5},{8,10},{9,11},{10,... | collective-permute-start | bytes 589832 | tf_op jit(solution)/shard_map/ppermute | solution.py:79
  7.2 10.9 %collective-permute-start.4 = (bf16[16,6144]{1,0:T(8,128)(2,1)}, bf16[16,6144]{1,0:T(8,128)(2,1)S(1)}, u32[]{:S(2)}, u32[]{:S(2)}) collective-permute-start(bf16[16,6144]{1,0:T(8,128)(2,1)} %refs_2_.3), channel_id=1, source_target_pairs={{0,4},{1,5},{2,6},{3,7},{4,0},{5,1},{6,2},{7,3},{8,12},{9,13},{10,... | collective-permute-start | bytes 589832 | tf_op jit(solution)/shard_map/ppermute | solution.py:79
  9.8 9.5 %copy-start = (bf16[16,6144]{1,0:T(8,128)(2,1)S(1)}, bf16[16,6144]{1,0:T(8,128)(2,1)}, u32[]{:S(2)}) copy-start(bf16[16,6144]{1,0:T(8,128)(2,1)} %refs_2_.3) | copy-start | bytes 589828
  17.6 1.8 %collective-permute-start.3 = (bf16[64,3072]{1,0:T(8,128)(2,1)S(1)}, bf16[64,3072]{1,0:T(8,128)(2,1)S(1)}, u32[]{:S(2)}, u32[]{:S(2)}) collective-permute-start(bf16[64,3072]{1,0:T(8,128)(2,1)S(1)} %get-tuple-element.31.refs_3_), channel_id=1, source_target_pairs={{0,1},{1,0},{2,3},{3,2},{4,5},{5,4},{6,7},{7,6},{8,9},{9,8},{10,11... | collective-permute-start | bytes 1179656 | tf_op jit(solution)/shard_map/ppermute | solution.py:83
  18.1 15.4 %collective-permute-start.10 = (bf16[16,6144]{1,0:T(8,128)(2,1)S(1)}, bf16[16,6144]{1,0:T(8,128)(2,1)S(1)}, u32[]{:S(2)}, u32[]{:S(2)}) collective-permute-start(bf16[16,6144]{1,0:T(8,128)(2,1)S(1)} %collective-permute-done.4.refs_1_), channel_id=1, source_target_pairs={{0,2},{1,3},{2,0},{3,1},{4,6},{5,7},{6,4},{7,5},{8,10},{9,11},{10,... | collective-permute-start | bytes 589832 | tf_op jit(solution)/shard_map/ppermute | solution.py:79
  19.5 9.7 %collective-permute-start.6 = (bf16[32,3072]{1,0:T(8,128)(2,1)S(1)}, bf16[32,3072]{1,0:T(8,128)(2,1)S(1)}, u32[]{:S(2)}, u32[]{:S(2)}) collective-permute-start(bf16[32,3072]{1,0:T(8,128)(2,1)S(1)} %get-tuple-element.33.refs_2_), channel_id=1, source_target_pairs={{0,2},{1,3},{2,0},{3,1},{4,6},{5,7},{6,4},{7,5},{8,10},{9,11},{10,... | collective-permute-start | bytes 589832 | tf_op jit(solution)/shard_map/ppermute | solution.py:79
  27.2 1.9 %collective-permute-start.7 = (bf16[64,3072]{1,0:T(8,128)(2,1)S(1)}, bf16[64,3072]{1,0:T(8,128)(2,1)S(1)}, u32[]{:S(2)}, u32[]{:S(2)}) collective-permute-start(bf16[64,3072]{1,0:T(8,128)(2,1)S(1)} %get-tuple-element.36.refs_1_), channel_id=1, source_target_pairs={{0,1},{1,0},{2,3},{3,2},{4,5},{5,4},{6,7},{7,6},{8,9},{9,8},{10,11... | collective-permute-start | bytes 1179656 | tf_op jit(solution)/shard_map/ppermute | solution.py:83
  29.3 7.8 %collective-permute-start.9 = (bf16[16,3072]{1,0:T(8,128)(2,1)S(1)}, bf16[16,3072]{1,0:T(8,128)(2,1)S(1)}, u32[]{:S(2)}, u32[]{:S(2)}) collective-permute-start(bf16[16,3072]{1,0:T(8,128)(2,1)S(1)} %get-tuple-element.40), channel_id=1, source_target_pairs={{0,4},{1,5},{2,6},{3,7},{4,0},{5,1},{6,2},{7,3},{8,12},{9,13},{10,... | collective-permute-start | bytes 294920 | tf_op jit(solution)/shard_map/ppermute | solution.py:79
  32.0 9.2 %collective-permute-start.8 = (bf16[32,3072]{1,0:T(8,128)(2,1)S(1)}, bf16[32,3072]{1,0:T(8,128)(2,1)S(1)}, u32[]{:S(2)}, u32[]{:S(2)}) collective-permute-start(bf16[32,3072]{1,0:T(8,128)(2,1)S(1)} %get-tuple-element.38.refs_4_), channel_id=1, source_target_pairs={{0,2},{1,3},{2,0},{3,1},{4,6},{5,7},{6,4},{7,5},{8,10},{9,11},{10,... | collective-permute-start | bytes 589832 | tf_op jit(solution)/shard_map/ppermute | solution.py:79
  33.6 8.7 %collective-permute-start.15 = (bf16[64,6144]{1,0:T(8,128)(2,1)S(1)}, bf16[64,6144]{1,0:T(8,128)(2,1)S(1)}, u32[]{:S(2)}, u32[]{:S(2)}) collective-permute-start(bf16[64,6144]{1,0:T(8,128)(2,1)S(1)} %stack.31.refs_3_.refs_0_), channel_id=1, source_target_pairs={{0,1},{1,0},{2,3},{3,2},{4,5},{5,4},{6,7},{7,6},{8,9},{9,8},{10,11... | collective-permute-start | bytes 2359304 | tf_op jit(solution)/shard_map/ppermute | solution.py:83
  37.2 8.9 %collective-permute-start.16 = (bf16[16,3072]{1,0:T(8,128)(2,1)S(1)}, bf16[16,3072]{1,0:T(8,128)(2,1)S(1)}, u32[]{:S(2)}, u32[]{:S(2)}) collective-permute-start(bf16[16,3072]{1,0:T(8,128)(2,1)S(1)} %far_slope.2.refs_2_.refs_0_), channel_id=1, source_target_pairs={{0,4},{1,5},{2,6},{3,7},{4,0},{5,1},{6,2},{7,3},{8,12},{9,13},{10,... | collective-permute-start | bytes 294920 | tf_op jit(solution)/shard_map/ppermute | solution.py:79
  38.7 13.2 %collective-permute-start.14 = (bf16[32,1536]{1,0:T(8,128)(2,1)S(1)}, bf16[32,1536]{1,0:T(8,128)(2,1)S(1)}, u32[]{:S(2)}, u32[]{:S(2)}) collective-permute-start(bf16[32,1536]{1,0:T(8,128)(2,1)S(1)} %stack.30.refs_4_.p0), channel_id=1, source_target_pairs={{0,24},{8,16},{16,8},{24,0},{1,25},{9,17},{17,9},{25,1},{2,26},{10... | collective-permute-start | bytes 294920 | tf_op jit(solution)/shard_map/ppermute | solution.py:75
  40.5 11.5 %collective-permute-start.13 = (bf16[32,1536]{1,0:T(8,128)(2,1)S(1)}, bf16[32,1536]{1,0:T(8,128)(2,1)S(1)}, u32[]{:S(2)}, u32[]{:S(2)}) collective-permute-start(bf16[32,1536]{1,0:T(8,128)(2,1)S(1)} %stack.30.refs_4_.p0), channel_id=1, source_target_pairs={{0,16},{8,24},{16,0},{24,8},{1,17},{9,25},{17,1},{25,9},{2,18},{10... | collective-permute-start | bytes 294920 | tf_op jit(solution)/shard_map/ppermute | solution.py:75
  41.2 10.9 %collective-permute-start.12 = (bf16[32,1536]{1,0:T(8,128)(2,1)S(1)}, bf16[32,1536]{1,0:T(8,128)(2,1)S(1)}, u32[]{:S(2)}, u32[]{:S(2)}) collective-permute-start(bf16[32,1536]{1,0:T(8,128)(2,1)S(1)} %stack.30.refs_4_.p0), channel_id=1, source_target_pairs={{0,8},{8,0},{16,24},{24,16},{1,9},{9,1},{17,25},{25,17},{2,10},{10... | collective-permute-start | bytes 294920 | tf_op jit(solution)/shard_map/ppermute | solution.py:75
  42.3 10.3 %collective-permute-start.11 = (bf16[16,3072]{1,0:T(8,128)(2,1)S(1)}, bf16[16,3072]{1,0:T(8,128)(2,1)S(1)}, u32[]{:S(2)}, u32[]{:S(2)}) collective-permute-start(bf16[16,3072]{1,0:T(8,128)(2,1)S(1)} %get-tuple-element.42.refs_3_), channel_id=1, source_target_pairs={{0,4},{1,5},{2,6},{3,7},{4,0},{5,1},{6,2},{7,3},{8,12},{9,13},{10,... | collective-permute-start | bytes 294920 | tf_op jit(solution)/shard_map/ppermute | solution.py:79
  46.1 10.1 %slice-start = ((s8[18874368]{0:T(1024)(128)(4,1)}), s8[4194304]{0:T(1024)(128)(4,1)S(1)}, s32[]{:S(2)}) async-start(s8[18874368]{0:T(1024)(128)(4,1)} %bitcast.5), calls=%async_computation | async-start | bytes 8388608
  46.1 10.1 %slice-start.1 = ((s8[18874368]{0:T(1024)(128)(4,1)}), s8[4194304]{0:T(1024)(128)(4,1)S(1)}, s32[]{:S(2)}) async-start(s8[18874368]{0:T(1024)(128)(4,1)} %bitcast.5), calls=%async_computation.1 | async-start | bytes 8388608
  46.1 10.1 %slice-start.2 = ((s8[18874368]{0:T(1024)(128)(4,1)}), s8[4194304]{0:T(1024)(128)(4,1)S(1)}, s32[]{:S(2)}) async-start(s8[18874368]{0:T(1024)(128)(4,1)} %bitcast.5), calls=%async_computation.2 | async-start | bytes 8388608
  46.2 6.6 %collective-permute-start.18 = (bf16[32,3072]{1,0:T(8,128)(2,1)S(1)}, bf16[32,3072]{1,0:T(8,128)(2,1)S(1)}, u32[]{:S(2)}, u32[]{:S(2)}) collective-permute-start(bf16[32,3072]{1,0:T(8,128)(2,1)S(1)} %stack.32.refs_4_.refs_0_), channel_id=1, source_target_pairs={{0,2},{1,3},{2,0},{3,1},{4,6},{5,7},{6,4},{7,5},{8,10},{9,11},{10,... | collective-permute-start | bytes 589832 | tf_op jit(solution)/shard_map/ppermute | solution.py:79
  47.3 8.9 %slice-start.4 = ((s8[18874368]{0:T(1024)(128)(4,1)}), s8[2097152]{0:T(1024)(128)(4,1)S(1)}, s32[]{:S(2)}) async-start(s8[18874368]{0:T(1024)(128)(4,1)} %bitcast.5), calls=%async_computation.4 | async-start | bytes 4194304
  51.9 4.3 %collective-permute-start.19 = (bf16[32,3072]{1,0:T(8,128)(2,1)S(1)}, bf16[32,3072]{1,0:T(8,128)(2,1)S(1)}, u32[]{:S(2)}, u32[]{:S(2)}) collective-permute-start(bf16[32,3072]{1,0:T(8,128)(2,1)S(1)} %stack.32.refs_4_.refs_0_), channel_id=1, source_target_pairs={{0,1},{1,0},{2,3},{3,2},{4,5},{5,4},{6,7},{7,6},{8,9},{9,8},{10,11... | collective-permute-start | bytes 589832 | tf_op jit(solution)/shard_map/ppermute | solution.py:83
  52.8 3.4 %collective-permute-start.20 = (bf16[32,3072]{1,0:T(8,128)(2,1)S(1)}, bf16[32,3072]{1,0:T(8,128)(2,1)S(1)}, u32[]{:S(2)}, u32[]{:S(2)}) collective-permute-start(bf16[32,3072]{1,0:T(8,128)(2,1)S(1)} %tie.2.refs_0_.refs_1_), channel_id=1, source_target_pairs={{0,1},{1,0},{2,3},{3,2},{4,5},{5,4},{6,7},{7,6},{8,9},{9,8},{10,11... | collective-permute-start | bytes 589832 | tf_op jit(solution)/shard_map/ppermute | solution.py:83
  53.4 8.0 %collective-permute-start.17 = (bf16[16,3072]{1,0:T(8,128)(2,1)S(1)}, bf16[16,3072]{1,0:T(8,128)(2,1)S(1)}, u32[]{:S(2)}, u32[]{:S(2)}) collective-permute-start(bf16[16,3072]{1,0:T(8,128)(2,1)S(1)} %far_slope.3.refs_1_.refs_0_), channel_id=1, source_target_pairs={{0,4},{1,5},{2,6},{3,7},{4,0},{5,1},{6,2},{7,3},{8,12},{9,13},{10,... | collective-permute-start | bytes 294920 | tf_op jit(solution)/shard_map/ppermute | solution.py:79
  61.4 7.4 %collective-permute-start.22 = (bf16[32,3072]{1,0:T(8,128)(2,1)S(1)}, bf16[32,3072]{1,0:T(8,128)(2,1)S(1)}, u32[]{:S(2)}, u32[]{:S(2)}) collective-permute-start(bf16[32,3072]{1,0:T(8,128)(2,1)S(1)} %stack.33.refs_4_.refs_1_.refs_0_), channel_id=1, source_target_pairs={{0,1},{1,0},{2,3},{3,2},{4,5},{5,4},{6,7},{7,6},{8,9},{9,8},{10,11... | collective-permute-start | bytes 589832 | tf_op jit(solution)/shard_map/ppermute | solution.py:83
  61.5 7.3 %collective-permute-start.21 = (bf16[32,3072]{1,0:T(8,128)(2,1)S(1)}, bf16[32,3072]{1,0:T(8,128)(2,1)S(1)}, u32[]{:S(2)}, u32[]{:S(2)}) collective-permute-start(bf16[32,3072]{1,0:T(8,128)(2,1)S(1)} %stack.33.refs_4_.refs_1_.refs_0_), channel_id=1, source_target_pairs={{0,2},{1,3},{2,0},{3,1},{4,6},{5,7},{6,4},{7,5},{8,10},{9,11},{10,... | collective-permute-start | bytes 589832 | tf_op jit(solution)/shard_map/ppermute | solution.py:79
  68.8 1.4 %collective-permute-start.23 = (bf16[32,3072]{1,0:T(8,128)(2,1)S(1)}, bf16[32,3072]{1,0:T(8,128)(2,1)S(1)}, u32[]{:S(2)}, u32[]{:S(2)}) collective-permute-start(bf16[32,3072]{1,0:T(8,128)(2,1)S(1)} %tie.3.refs_2_.refs_1_), channel_id=1, source_target_pairs={{0,1},{1,0},{2,3},{3,2},{4,5},{5,4},{6,7},{7,6},{8,9},{9,8},{10,11... | collective-permute-start | bytes 589832 | tf_op jit(solution)/shard_map/ppermute | solution.py:83
  72.2 8.4 %collective-permute-start.24 = (bf16[32,1536]{1,0:T(8,128)(2,1)S(1)}, bf16[32,1536]{1,0:T(8,128)(2,1)S(1)}, u32[]{:S(2)}, u32[]{:S(2)}) collective-permute-start(bf16[32,1536]{1,0:T(8,128)(2,1)S(1)} %get-tuple-element.51), channel_id=1, source_target_pairs={{0,8},{8,0},{16,24},{24,16},{1,9},{9,1},{17,25},{25,17},{2,10},{10... | collective-permute-start | bytes 294920 | tf_op jit(solution)/shard_map/ppermute | solution.py:75
  73.3 7.4 %collective-permute-start.25 = (bf16[32,1536]{1,0:T(8,128)(2,1)S(1)}, bf16[32,1536]{1,0:T(8,128)(2,1)S(1)}, u32[]{:S(2)}, u32[]{:S(2)}) collective-permute-start(bf16[32,1536]{1,0:T(8,128)(2,1)S(1)} %get-tuple-element.52), channel_id=1, source_target_pairs={{0,16},{8,24},{16,0},{24,8},{1,17},{9,25},{17,1},{25,9},{2,18},{10... | collective-permute-start | bytes 294920 | tf_op jit(solution)/shard_map/ppermute | solution.py:75
  74.6 6.1 %collective-permute-start.26 = (bf16[32,1536]{1,0:T(8,128)(2,1)S(1)}, bf16[32,1536]{1,0:T(8,128)(2,1)S(1)}, u32[]{:S(2)}, u32[]{:S(2)}) collective-permute-start(bf16[32,1536]{1,0:T(8,128)(2,1)S(1)} %get-tuple-element.53), channel_id=1, source_target_pairs={{0,24},{8,16},{16,8},{24,0},{1,25},{9,17},{17,9},{25,1},{2,26},{10... | collective-permute-start | bytes 294920 | tf_op jit(solution)/shard_map/ppermute | solution.py:75
  (3 other events, 17.8 us)
